TPU v7x, 32 devices: a whole 2x2x4 slice. The times are simulated.
32 devices in a mesh: grp: 2 (over x), seq: 16 (over z, y, core).
Axes of the slice: x: 2, y: 2, z: 4, core: 2. Of those that a mesh axis runs over, the one named last changes fastest.
Arguments:
- inputs: bfloat16 [4096, 4096], P(('grp', 'seq')), parts along dimension 0, may hold values from -6 to 6
- in_weight: bfloat16 [4096, 768], replicated, may hold values from -0.09375 to 0.09375
- filter_taps: float32 [2048, 256], P('seq'), may hold values from -6 to 6
- grad_out: bfloat16 [4096, 256], P(('grp', 'seq')), parts along dimension 0, may hold values from -6 to 6
Outputs:
- grad_inputs: bfloat16 [4096, 4096], P(('grp', 'seq')), parts along dimension 0
- grad_weight: float32 [8192, 768], P(('grp', 'seq')), parts along dimension 0
- grad_taps: float32 [4096, 256], P(('grp', 'seq')), parts along dimension 0
There are 2 independent parts, one for each index of `grp`. A program takes and returns all parts, laid end to end along the dimension named above; an argument that names none is the same for every part. Nothing has to cross between parts.
All inputs are finite; a program needn't handle non-finite values.
Results may differ from a plain program's by a relative error of at most 0.0064.
Values sent between devices are 32-bit elements; how exact they have to be, the bound alone decides.
No kernel may reach another device: no remote copies, remote signals or barrier semaphores. Data moves between devices by JAX's collectives and lax.ppermute only.
A program may use at most 128 MiB of HBM per device.

v0:
```python
import functools
import math

import jax
import jax.numpy as jnp
import numpy as np
from jax import lax
from jax.experimental import pallas as pl
from jax.experimental.pallas import tpu as pltpu
from jax.sharding import PartitionSpec as P

VMEM_LIMIT = 48 * 1024 * 1024
VMEM_WIDE = 60 * 1024 * 1024
SIDE = 4


def split_pair(table):
    high = table.astype(np.float32).astype(jnp.bfloat16)
    low = (table - high.astype(np.float64)).astype(np.float32).astype(jnp.bfloat16)
    return high, low


def transform_tables(blocks, width, rows):
    length = 2 * blocks * rows
    kept = blocks + 1
    padded = -(-kept * width // 16) * 16
    k1 = np.arange(kept)
    block = np.arange(blocks)
    angle = 2.0 * np.pi * ((k1[:, None] * block[None, :]) % (2 * blocks)) / (2 * blocks)
    eye = np.eye(width)

    def spread(matrix):
        wide = np.kron(matrix, eye)
        return np.pad(wide, ((0, padded - wide.shape[0]), (0, 0)))

    mix = np.concatenate([spread(np.cos(angle)), spread(-np.sin(angle))], axis=0)
    weight = np.where((k1 == 0) | (k1 == blocks), 1.0, 2.0)[:, None] / length
    unmix = np.concatenate(
        [spread(weight * np.cos(angle)), spread(-weight * np.sin(angle))], axis=0
    ).T
    row = np.arange(rows)
    turn = 2.0 * np.pi * ((k1[:, None] * row[None, :]) % length) / length
    turn = np.pad(np.repeat(turn, width, axis=0), ((0, padded - kept * width), (0, 0)))
    inner = 2.0 * np.pi * ((row[:, None] * row[None, :]) % rows) / rows
    cos, sin = np.cos(inner), np.sin(inner)
    forward = np.block([[cos, -sin], [sin, cos]])
    inverse = np.block([[cos, sin], [-sin, cos]])
    turn = np.concatenate([np.cos(turn), np.sin(turn)], axis=1).astype(np.float32)
    return [split_pair(matrix) for matrix in (mix, forward, inverse, unmix)], turn


def packed(tables):
    width = max(min(high.shape) for high, _ in tables)
    slabs, places, first = [], [], 0
    for pair in tables:
        for table in pair:
            pieces = []
            for start in range(0, table.shape[1], width):
                slab = table[:, start : start + width]
                pieces.append((first, slab.shape))
                first += slab.shape[0]
                slabs.append(np.pad(slab, ((0, 0), (0, width - slab.shape[1]))))
            places.append(pieces)
    return np.concatenate(slabs, axis=0), places


def halves(value):
    high = value.astype(jnp.bfloat16)
    return high, (value - high.astype(jnp.float32)).astype(jnp.bfloat16)


def dot32(left, right):
    (lh, ll), (rh, rl) = left, right
    dot = functools.partial(jnp.dot, preferred_element_type=jnp.float32)
    return dot(lh, rh) + (dot(lh, rl) + dot(ll, rh))


def layout_kernel(x_ref, own_ref, y_ref, z_ref):
    _, far, _, part = own_ref.shape
    device = lax.axis_index("seq")
    places = {
        (0, 0): (own_ref, 0),
        (0, 1): (own_ref, 1),
        (1, 0): (y_ref, 0),
        (3, 0): (y_ref, 1),
        (1, 1): (y_ref, 2),
        (2, 1): (z_ref, 0),
        (3, 1): (z_ref, 1),
        (2, 0): (z_ref, 2),
    }
    for chip in range(far * SIDE):
        distance = (chip // SIDE) ^ (device // (2 * SIDE))
        near = (chip % SIDE) ^ ((device // 2) % SIDE)
        for core in range(2):
            first = (2 * chip + core) * part
            flip = (device % 2) ^ core
            for (side, cross), (out_ref, slot) in places.items():

                @pl.when((near == side) & (flip == cross))
                def _():
                    out_ref[slot, distance] = x_ref[:, first : first + part].astype(jnp.float32)


def project_kernel(scaling, x_ref, w_ref, taps_ref, go_ref, *refs):
    sig_ref, gates_ref, acc = refs[-3:]
    step = pl.program_id(0)
    product = jnp.dot(x_ref[...], w_ref[...], preferred_element_type=jnp.float32)

    @pl.when(step == 0)
    def _():
        acc[...] = product

    @pl.when(step > 0)
    def _():
        acc[...] += product

    @pl.when(step == pl.num_programs(0) - 1)
    def _():
        count, _, width, _ = sig_ref.shape
        channels = count * width
        projected = acc[...].astype(jnp.bfloat16).astype(jnp.float32).T
        query = projected[:channels]
        key = projected[channels : 2 * channels]
        value = projected[2 * channels :]
        go = go_ref[...].astype(jnp.float32).T
        signals = ((taps_ref[...] * scaling).T, key * value, go * query)
        for which, signal in enumerate(signals):
            for owner in range(count):
                sig_ref[owner, which] = signal[owner * width : (owner + 1) * width]
        for index, gate in enumerate((go, value, key)):
            gates_ref[index] = gate.astype(jnp.bfloat16)


def conv_kernel(places, x_ref, table_ref, turn_ref, *refs):
    y_ref, flat = refs[-2:]
    blocks, _, width, rows = x_ref.shape

    def table(which):
        slabs = [table_ref[at : at + shape[0], : shape[1]] for at, shape in places[which]]
        return slabs[0] if len(slabs) == 1 else jnp.concatenate(slabs, axis=1)

    m_h, m_l, f_h, f_l, i_h, i_l, u_h, u_l = [functools.partial(table, w) for w in range(8)]
    for p in range(blocks):
        for s in range(3):
            flat[p * width : (p + 1) * width, s * rows : (s + 1) * rows] = x_ref[p, s]
    turn_re, turn_im = turn_ref[:, :rows], turn_ref[:, rows:]
    count = turn_re.shape[0]
    mixed = dot32((m_h(), m_l()), halves(flat[...]))
    turned = []
    for s in range(3):
        re = mixed[:count, s * rows : (s + 1) * rows]
        im = mixed[count:, s * rows : (s + 1) * rows]
        turned.append(
            jnp.concatenate([re * turn_re + im * turn_im, im * turn_re - re * turn_im], axis=1)
        )
    spectrum = dot32(halves(jnp.concatenate(turned, axis=0)), (f_h(), f_l()))
    (k_re, k_im), (g_re, g_im), (b_re, b_im) = [
        (spectrum[s * count : (s + 1) * count, :rows], spectrum[s * count : (s + 1) * count, rows:])
        for s in range(3)
    ]
    products = jnp.concatenate(
        [
            jnp.concatenate([k_re * g_re - k_im * g_im, k_re * g_im + k_im * g_re], axis=1),
            jnp.concatenate([k_re * b_re + k_im * b_im, k_re * b_im - k_im * b_re], axis=1),
            jnp.concatenate([b_re * g_re + b_im * g_im, b_im * g_re - b_re * g_im], axis=1),
        ],
        axis=0,
    )
    back = dot32(halves(products), (i_h(), i_l()))
    parts_re, parts_im = [], []
    for s in range(3):
        re = back[s * count : (s + 1) * count, :rows]
        im = back[s * count : (s + 1) * count, rows:]
        parts_re.append(re * turn_re - im * turn_im)
        parts_im.append(im * turn_re + re * turn_im)
    stacked = jnp.concatenate(
        [jnp.concatenate(parts_re, axis=1), jnp.concatenate(parts_im, axis=1)], axis=0
    )
    result = dot32((u_h(), u_l()), halves(stacked))
    for p in range(blocks):
        for s in range(3):
            y_ref[p, s] = result[p * width : (p + 1) * width, s * rows : (s + 1) * rows]


def gate_kernel(scaling, y_ref, gates_ref, *refs):
    gp_ref, first_ref, rest_ref, taps_ref, flat = refs[-5:]
    count, _, width, _ = y_ref.shape
    channels = count * width
    for s in range(3):
        for owner in range(count):
            flat[s, owner * width : (owner + 1) * width] = y_ref[owner, s]
    for index in range(3):
        gate = gates_ref[index].astype(jnp.float32)
        rounded = (gate * flat[min(index, 1)]).T.astype(jnp.bfloat16)
        gp_ref[:, index * channels : (index + 1) * channels] = rounded
        if index == 0:
            first_ref[...] = rounded.astype(jnp.float32)
        else:
            span = slice((index - 1) * channels, index * channels)
            rest_ref[:, span] = rounded.astype(jnp.float32)
    taps_ref[...] = flat[2].T * scaling


def turn_blocks(sources, out_ref):
    for which, (x_ref, slot) in enumerate(sources):
        _, far, rows, part = x_ref.shape
        for f in range(far):
            out_ref[f * part : (f + 1) * part, which * rows : (which + 1) * rows] = x_ref[
                slot, f
            ].T.astype(jnp.bfloat16)


def turn_kernel(own_ref, y_ref, z_ref, out_own_ref, out_other_ref, relay_z_ref, relay_y_ref):
    relay_z_ref[0] = y_ref[1]
    relay_y_ref[0] = z_ref[1]
    turn_blocks(((own_ref, 0), (y_ref, 0), (z_ref, 2)), out_own_ref)
    turn_blocks(((own_ref, 1), (y_ref, 2), (z_ref, 0)), out_other_ref)


def corner_kernel(corner_own_ref, corner_other_ref, out_own_ref, out_other_ref):
    turn_blocks(((corner_own_ref, 0),), out_own_ref)
    turn_blocks(((corner_other_ref, 0),), out_other_ref)


def joined_columns(x_ref, corner_ref, span):
    return jnp.concatenate([x_ref[span], corner_ref[span]], axis=1)


def joined(gp_refs):
    return jnp.concatenate([gp_ref[...].astype(jnp.bfloat16) for gp_ref in gp_refs], axis=0)


def other_kernel(x_ref, corner_ref, *refs):
    gp_refs, out_ref = refs[:SIDE], refs[-1]
    columns = joined_columns(x_ref, corner_ref, slice(None))
    out_ref[...] = jnp.dot(columns, joined(gp_refs), preferred_element_type=jnp.float32)


def own_kernel(x_ref, corner_ref, *refs):
    gp_refs, add_ref, out_refs = refs[:SIDE], refs[SIDE], refs[SIDE + 1 :]
    gp = joined(gp_refs)
    part = out_refs[0].shape[0]
    for which, out_ref in enumerate(out_refs):
        span = slice(which * part, (which + 1) * part)
        columns = joined_columns(x_ref, corner_ref, span)
        product = jnp.dot(columns, gp, preferred_element_type=jnp.float32)
        out_ref[...] = product + add_ref[span]


def sum_kernel(scaling, groups, *refs):
    *in_refs, out_ref = refs
    terms = len(in_refs) // groups
    first = 0
    for group in range(groups):
        total = in_refs[group * terms][...]
        for in_ref in in_refs[group * terms + 1 : (group + 1) * terms]:
            total = total + in_ref[...]
        out_ref[:, first : first + total.shape[1]] = total * scaling
        first += total.shape[1]


def per_device(inputs, in_weight, filter_taps, grad_out):
    rows, depth = inputs.shape
    channels = filter_taps.shape[1]
    columns = in_weight.shape[1]
    blocks = lax.axis_size("seq")
    width = channels // blocks
    part = depth // blocks
    far = blocks // (2 * SIDE)
    chunk = min(1024, depth)
    steps = depth // chunk
    scaling = 1.0 / math.sqrt(rows * blocks)
    f32, bf16 = jnp.float32, jnp.bfloat16
    params = pltpu.CompilerParams(vmem_limit_bytes=VMEM_LIMIT)
    wide = pltpu.CompilerParams(vmem_limit_bytes=VMEM_WIDE)

    def shaped(*shape, dtype=f32):
        return jax.ShapeDtypeStruct(shape, dtype)

    def exchange(value, flip):
        return lax.ppermute(value, "seq", [(i, i ^ flip) for i in range(blocks)])

    anywhere = pl.BlockSpec(memory_space=pl.ANY)
    inside = pl.BlockSpec(memory_space=pltpu.VMEM)
    own, to_y, to_z = pl.pallas_call(
        layout_kernel,
        out_shape=[shaped(2, far, rows, part)] + [shaped(3, far, rows, part)] * 2,
        compiler_params=wide,
    )(inputs)
    from_y, from_z = exchange(to_y, 2), exchange(to_z, 4)
    *turned, relay_z, relay_y = pl.pallas_call(
        turn_kernel,
        out_shape=[shaped(far * part, (SIDE - 1) * rows, dtype=bf16)] * 2
        + [shaped(1, far, rows, part)] * 2,
        compiler_params=params,
        cost_estimate=pl.CostEstimate(
            flops=0, bytes_accessed=200 * SIDE * far * rows * part, transcendentals=0
        ),
    )(own, from_y, from_z)
    corners = exchange(relay_z, 4), exchange(relay_y, 2)
    signals, gates = pl.pallas_call(
        functools.partial(project_kernel, scaling),
        grid=(steps,),
        in_specs=[
            pl.BlockSpec((rows, chunk), lambda i: (0, i)),
            pl.BlockSpec((chunk, columns), lambda i: (i, 0)),
            pl.BlockSpec((rows, channels), lambda i: (0, 0)),
            pl.BlockSpec((rows, channels), lambda i: (0, 0)),
        ],
        out_specs=[
            pl.BlockSpec((blocks, 3, width, rows), lambda i: (0, 0, 0, 0)),
            ]
        + [pl.BlockSpec((3, channels, rows), lambda i: (0, 0, 0))],
        out_shape=[shaped(blocks, 3, width, rows), shaped(3, channels, rows, dtype=bf16)],
        scratch_shapes=[pltpu.VMEM((rows, columns), f32)],
        compiler_params=wide,
        cost_estimate=pl.CostEstimate(
            flops=2 * rows * depth * columns,
            bytes_accessed=2 * depth * (rows + columns),
            transcendentals=0,
        ),
    )(inputs, in_weight, filter_taps, grad_out)

    signals = lax.all_to_all(signals, "seq", split_axis=0, concat_axis=0, tiled=True)
    pairs, turn = transform_tables(blocks, width, rows)
    table, places = packed(pairs)
    results = pl.pallas_call(
        functools.partial(conv_kernel, places),
        in_specs=[inside] * 3 + [anywhere] * 2,
        out_shape=shaped(blocks, 3, width, rows),
        scratch_shapes=[pltpu.VMEM((blocks * width, 3 * rows), f32)],
        compiler_params=params,
    )(signals, jnp.asarray(table), jnp.asarray(turn), *turned)
    results = lax.all_to_all(results, "seq", split_axis=0, concat_axis=0, tiled=True)
    turned_corners = pl.pallas_call(
        corner_kernel,
        out_shape=[shaped(far * part, rows, dtype=bf16)] * 2,
        compiler_params=params,
        cost_estimate=pl.CostEstimate(
            flops=0, bytes_accessed=200 * SIDE * far * rows * part, transcendentals=0
        ),
    )(*corners)
    grad_proj, sent_first, sent_rest, grad_taps = pl.pallas_call(
        functools.partial(gate_kernel, scaling),
        in_specs=[inside] * 2 + [anywhere] * 2,
        out_shape=[
            shaped(rows, columns, dtype=bf16),
            shaped(rows, channels),
            shaped(rows, columns - channels),
            shaped(rows, channels),
        ],
        scratch_shapes=[pltpu.VMEM((3, channels, rows), f32)],
        compiler_params=params,
    )(results, gates, *turned_corners)
    grad_inputs = lax.dot_general(
        grad_proj, in_weight, (((1,), (1,)), ((), ())), preferred_element_type=f32
    ).astype(bf16)
    terms = []
    for block in (sent_first, sent_rest):
        cols = block.shape[1]
        gathered = [block] + [exchange(block, 2 * k) for k in range(1, SIDE)]
        cost = pl.CostEstimate(
            flops=2 * far * part * SIDE * rows * cols,
            bytes_accessed=4 * far * part * cols,
            transcendentals=0,
        )
        other = pl.pallas_call(
            other_kernel,
            in_specs=[inside] * (2 + SIDE) + [anywhere] * len(terms[1:]),
            out_shape=shaped(far * part, cols),
            compiler_params=params,
            cost_estimate=cost,
        )(turned[1], turned_corners[1], *gathered, *terms[1:])
        kept, *leaving = pl.pallas_call(
            own_kernel,
            out_shape=[shaped(part, cols)] * far,
            compiler_params=params,
            cost_estimate=cost,
        )(turned[0], turned_corners[0], *gathered, exchange(other, 1))
        terms += [kept] + [exchange(v, 2 * SIDE * (k + 1)) for k, v in enumerate(leaving)]
    grad_weight = pl.pallas_call(
        functools.partial(sum_kernel, scaling, 2),
        out_shape=shaped(part, columns),
        compiler_params=params,
    )(*terms)
    return grad_inputs, grad_weight, grad_taps


def solution(mesh):
    in_specs = (P(("grp", "seq"), None), P(), P("seq", None), P(("grp", "seq"), None))
    out_specs = (P(("grp", "seq"), None), P(("grp", "seq"), None), P(("grp", "seq"), None))
    return jax.shard_map(
        per_device, mesh=mesh, in_specs=in_specs, out_specs=out_specs, check_vma=False
    )
```

profile of v0, /device:TPU:0, one launch (start us, length us, event | category | flops | bytes accessed | tf_op | source)
XLA Modules:
  0.0 121.7 jit_solution(13776340107778705408)
XLA Ops:
  0.6 0.0 copy-start
  0.6 0.0 copy-start.4
  0.7 3.6 %shard_map.86 = (f32[2,2,128,256]{3,2,1,0:T(8,128)}, f32[3,2,128,256]{3,2,1,0:T(8,128)}, f32[3,2,128,256]{3,2,1,0:T(8,128)}) custom-call(bf16[128,4096]{1,0:T(8,128)(2,1)} %x_ref.3), custom_call_target="tpu_custom_call" | custom-call | tf_op jit(solution)/shard_map/pallas_call | solution.py:285
  4.3 3.0 %collective-permute-start = (f32[3,2,128,256]{3,2,1,0:T(8,128)}, f32[3,2,128,256]{3,2,1,0:T(8,128)S(1)}, u32[]{:S(2)}, u32[]{:S(2)}) collective-permute-start(f32[3,2,128,256]{3,2,1,0:T(8,128)} %get-tuple-element.24), channel_id=1, source_target_pairs={{0,2},{1,3},{2,0},{3,1},{4,6},{5,7},{6,4},{7,5},{8,10},{9,11},{10,... | collective-permute-start | bytes 2359304 | tf_op jit(solution)/shard_map/ppermute | solution.py:281
  7.2 1.6 %collective-permute-start.1 = (f32[3,2,128,256]{3,2,1,0:T(8,128)}, f32[3,2,128,256]{3,2,1,0:T(8,128)}, u32[]{:S(2)}, u32[]{:S(2)}) collective-permute-start(f32[3,2,128,256]{3,2,1,0:T(8,128)} %get-tuple-element.25), channel_id=1, source_target_pairs={{0,4},{1,5},{2,6},{3,7},{4,0},{5,1},{6,2},{7,3},{8,12},{9,13},{10,... | collective-permute-start | bytes 2359304 | tf_op jit(solution)/shard_map/ppermute | solution.py:281
  8.8 5.6 %shard_map.85 = (f32[16,3,16,128]{3,2,1,0:T(8,128)}, bf16[3,256,128]{2,1,0:T(8,128)(2,1)}) custom-call(bf16[128,4096]{1,0:T(8,128)(2,1)} %x_ref.3, bf16[4096,768]{1,0:T(8,128)(2,1)} %w_ref.1, f32[128,256]{1,0:T(8,128)} %taps_ref.1, bf16[128,256]{1,0:T(8,128)(2,1)} %go_ref.1), custom_call_target="tpu_custom_call" | custom-call | flops 805306368 | bytes 7340032 | tf_op jit(solution)/shard_map/pallas_call | solution.py:301
  14.4 4.1 %all-to-all-start = ((f32[16,3,16,128]{3,2,1,0:T(8,128)}), f32[16,3,16,128]{3,2,1,0:T(8,128)S(1)}, u32[]{:S(2)}, u32[]{:S(2)}) async-start(f32[16,3,16,128]{3,2,1,0:T(8,128)} %get-tuple-element.22), calls=%async_computation | async-start | bytes 786432 | tf_op jit(solution)/shard_map/all_to_all | solution.py:324
  18.5 8.0 %collective-permute-done.y_ref = f32[3,2,128,256]{3,2,1,0:T(8,128)S(1)} collective-permute-done((f32[3,2,128,256]{3,2,1,0:T(8,128)}, f32[3,2,128,256]{3,2,1,0:T(8,128)S(1)}, u32[]{:S(2)}, u32[]{:S(2)}) %collective-permute-start) | collective-permute-done | bytes 786464 | tf_op jit(solution)/shard_map/ppermute | solution.py:281
  26.5 0.9 copy-done.1
  27.4 2.9 %collective-permute-done.1.z_ref = f32[3,2,128,256]{3,2,1,0:T(8,128)} collective-permute-done((f32[3,2,128,256]{3,2,1,0:T(8,128)}, f32[3,2,128,256]{3,2,1,0:T(8,128)}, u32[]{:S(2)}, u32[]{:S(2)}) %collective-permute-start.1) | collective-permute-done | bytes 786464 | tf_op jit(solution)/shard_map/ppermute | solution.py:281
  30.3 1.1 copy-done.2
  31.5 1.0 copy-done.3
  32.5 1.4 %shard_map.87 = (bf16[512,384]{1,0:T(8,128)(2,1)S(1)}, bf16[512,384]{1,0:T(8,128)(2,1)S(1)}, f32[1,2,128,256]{3,2,1,0:T(8,128)S(1)}, f32[1,2,128,256]{3,2,1,0:T(8,128)S(1)}) custom-call(f32[2,2,128,256]{3,2,1,0:T(8,128)S(1)} %copy-done.3, f32[3,2,128,256]{3,2,1,0:T(8,128)S(1)} %copy-done.2, f32[3,2,128,256]{3,2,1,0:T(8,128)} %collective-permute-done.1.z_ref), custom_call_target="tpu_custom_call" | custom-call | bytes 52428800 | tf_op jit(solution)/shard_map/pallas_call | solution.py:291
  34.0 0.7 copy-done.6
  34.6 0.7 copy-done.7
  35.4 3.3 %shard_map.88 = f32[16,3,16,128]{3,2,1,0:T(8,128)} custom-call(f32[16,3,16,128]{3,2,1,0:T(8,128)S(1)} %all-to-all-done.x_ref, bf16[3648,256]{1,0:T(8,128)(2,1)S(1)} %copy-done, f32[272,256]{1,0:T(8,128)S(1)} %copy-done.4, bf16[512,384]{1,0:T(8,128)(2,1)S(1)} %get-tuple-element.26.refs_0_.x_ref, bf16[512,384]{1,0:T(8,128)(2,1)S(1)} %get-tuple-element.27.refs_1_.x_ref), custom_call_target="tpu_custom_call" | custom-call | tf_op jit(solution)/shard_map/pallas_call | solution.py:327
  38.7 5.9 %all-to-all-start.1 = ((f32[16,3,16,128]{3,2,1,0:T(8,128)}), f32[16,3,16,128]{3,2,1,0:T(8,128)S(1)}, u32[]{:S(2)}, u32[]{:S(2)}) async-start(f32[16,3,16,128]{3,2,1,0:T(8,128)} %shard_map.88), calls=%async_computation.1 | async-start | bytes 786432 | tf_op jit(solution)/shard_map/all_to_all | solution.py:334
  44.6 1.9 %collective-permute-start.2 = (f32[1,2,128,256]{3,2,1,0:T(8,128)}, f32[1,2,128,256]{3,2,1,0:T(8,128)S(1)}, u32[]{:S(2)}, u32[]{:S(2)}) collective-permute-start(f32[1,2,128,256]{3,2,1,0:T(8,128)} %copy-done.7), channel_id=1, source_target_pairs={{0,4},{1,5},{2,6},{3,7},{4,0},{5,1},{6,2},{7,3},{8,12},{9,13},{10,... | collective-permute-start | bytes 786440 | tf_op jit(solution)/shard_map/ppermute | solution.py:281
  46.5 1.5 %collective-permute-start.3 = (f32[1,2,128,256]{3,2,1,0:T(8,128)}, f32[1,2,128,256]{3,2,1,0:T(8,128)S(1)}, u32[]{:S(2)}, u32[]{:S(2)}) collective-permute-start(f32[1,2,128,256]{3,2,1,0:T(8,128)} %copy-done.6), channel_id=1, source_target_pairs={{0,2},{1,3},{2,0},{3,1},{4,6},{5,7},{6,4},{7,5},{8,10},{9,11},{10,... | collective-permute-start | bytes 786440 | tf_op jit(solution)/shard_map/ppermute | solution.py:281
  48.0 11.7 %collective-permute-done.2.corner_own_ref = f32[1,2,128,256]{3,2,1,0:T(8,128)S(1)} collective-permute-done((f32[1,2,128,256]{3,2,1,0:T(8,128)}, f32[1,2,128,256]{3,2,1,0:T(8,128)S(1)}, u32[]{:S(2)}, u32[]{:S(2)}) %collective-permute-start.2) | collective-permute-done | bytes 262176 | tf_op jit(solution)/shard_map/ppermute | solution.py:281
  59.7 0.0 collective-permute-done.3.corner_other_ref
  59.7 0.1 shard_map.89
  59.8 0.0 all-to-all-done.1.y_ref
  59.8 0.8 shard_map.90
  60.7 1.5 %collective-permute-start.4 = (f32[128,256]{1,0:T(8,128)S(1)}, f32[128,256]{1,0:T(8,128)S(1)}, u32[]{:S(2)}, u32[]{:S(2)}) collective-permute-start(f32[128,256]{1,0:T(8,128)S(1)} %get-tuple-element.34.refs_0_), channel_id=1, source_target_pairs={{0,2},{1,3},{2,0},{3,1},{4,6},{5,7},{6,4},{7,5},{8,10},{9,11},{10,... | collective-permute-start | bytes 393224 | tf_op jit(solution)/shard_map/ppermute | solution.py:281
  62.1 0.6 collective-permute-start.5
  62.7 1.5 %collective-permute-start.6 = (f32[128,256]{1,0:T(8,128)S(1)}, f32[128,256]{1,0:T(8,128)S(1)}, u32[]{:S(2)}, u32[]{:S(2)}) collective-permute-start(f32[128,256]{1,0:T(8,128)S(1)} %get-tuple-element.34.refs_0_), channel_id=1, source_target_pairs={{0,6},{1,7},{2,4},{3,5},{4,2},{5,3},{6,0},{7,1},{8,14},{9,15},{10,... | collective-permute-start | bytes 393224 | tf_op jit(solution)/shard_map/ppermute | solution.py:281
  64.2 2.0 %collective-permute-done.4.refs_1_ = f32[128,256]{1,0:T(8,128)S(1)} collective-permute-done((f32[128,256]{1,0:T(8,128)S(1)}, f32[128,256]{1,0:T(8,128)S(1)}, u32[]{:S(2)}, u32[]{:S(2)}) %collective-permute-start.4) | collective-permute-done | bytes 131104 | tf_op jit(solution)/shard_map/ppermute | solution.py:281
  66.2 2.1 %collective-permute-done.5.refs_2_ = f32[128,256]{1,0:T(8,128)S(1)} collective-permute-done((f32[128,256]{1,0:T(8,128)S(1)}, f32[128,256]{1,0:T(8,128)S(1)}, u32[]{:S(2)}, u32[]{:S(2)}) %collective-permute-start.5) | collective-permute-done | bytes 131104 | tf_op jit(solution)/shard_map/ppermute | solution.py:281
  68.3 1.4 %collective-permute-done.6.refs_3_ = f32[128,256]{1,0:T(8,128)S(1)} collective-permute-done((f32[128,256]{1,0:T(8,128)S(1)}, f32[128,256]{1,0:T(8,128)S(1)}, u32[]{:S(2)}, u32[]{:S(2)}) %collective-permute-start.6) | collective-permute-done | bytes 131104 | tf_op jit(solution)/shard_map/ppermute | solution.py:281
  69.7 0.3 shard_map.91
  70.0 0.1 collective-permute-start.7
  70.1 0.8 collective-permute-start.10
  70.9 2.2 %collective-permute-start.11 = (f32[128,512]{1,0:T(8,128)S(1)}, f32[128,512]{1,0:T(8,128)S(1)}, u32[]{:S(2)}, u32[]{:S(2)}) collective-permute-start(f32[128,512]{1,0:T(8,128)S(1)} %get-tuple-element.37.refs_0_), channel_id=1, source_target_pairs={{0,6},{1,7},{2,4},{3,5},{4,2},{5,3},{6,0},{7,1},{8,14},{9,15},{10,... | collective-permute-start | bytes 786440 | tf_op jit(solution)/shard_map/ppermute | solution.py:281
  73.1 0.6 collective-permute-start.9
  73.6 0.0 collective-permute-done.7.refs_4_
  73.6 0.3 shard_map.92
  74.0 2.5 %collective-permute-start.8 = (f32[256,256]{1,0:T(8,128)S(1)}, f32[256,256]{1,0:T(8,128)S(1)}, u32[]{:S(2)}, u32[]{:S(2)}) collective-permute-start(f32[256,256]{1,0:T(8,128)S(1)} %get-tuple-element.36), channel_id=1, source_target_pairs={{0,8},{1,9},{2,10},{3,11},{4,12},{5,13},{6,14},{7,15},{8,0},{9,1},... | collective-permute-start | bytes 786440 | tf_op jit(solution)/shard_map/ppermute | solution.py:281
  76.4 8.4 %collective-permute-done.10.refs_2_ = f32[128,512]{1,0:T(8,128)S(1)} collective-permute-done((f32[128,512]{1,0:T(8,128)S(1)}, f32[128,512]{1,0:T(8,128)S(1)}, u32[]{:S(2)}, u32[]{:S(2)}) %collective-permute-start.10) | collective-permute-done | bytes 262176 | tf_op jit(solution)/shard_map/ppermute | solution.py:281
  84.9 6.1 %collective-permute-done.11.refs_3_ = f32[128,512]{1,0:T(8,128)S(1)} collective-permute-done((f32[128,512]{1,0:T(8,128)S(1)}, f32[128,512]{1,0:T(8,128)S(1)}, u32[]{:S(2)}, u32[]{:S(2)}) %collective-permute-start.11) | collective-permute-done | bytes 262176 | tf_op jit(solution)/shard_map/ppermute | solution.py:281
  91.0 0.4 shard_map.93
  91.4 0.1 collective-permute-start.12
  91.5 2.6 %collective-permute-done.12.refs_4_ = f32[512,512]{1,0:T(8,128)S(1)} collective-permute-done((f32[512,512]{1,0:T(8,128)S(1)}, f32[512,512]{1,0:T(8,128)S(1)}, u32[]{:S(2)}, u32[]{:S(2)}) %collective-permute-start.12) | collective-permute-done | bytes 1048608 | tf_op jit(solution)/shard_map/ppermute | solution.py:281
  94.1 0.4 shard_map.94
  94.6 0.8 collective-permute-start.13
  95.4 5.9 %convolution_convert_fusion = bf16[128,4096]{1,0:T(8,128)(2,1)} fusion(bf16[128,768]{1,0:T(8,128)(2,1)S(1)} %get-tuple-element.33, bf16[4096,768]{1,0:T(8,128)(2,1)} %w_ref.1), kind=kOutput, calls=%fused_computation | convolution fusion | flops 805830656 | bytes 7536640 | tf_op jit(solution)/shard_map/dot_general | solution.py:355
  101.3 19.4 %collective-permute-done.13.refs_3_ = f32[256,512]{1,0:T(8,128)S(1)} collective-permute-done((f32[256,512]{1,0:T(8,128)S(1)}, f32[256,512]{1,0:T(8,128)S(1)}, u32[]{:S(2)}, u32[]{:S(2)}) %collective-permute-start.13) | collective-permute-done | bytes 524320 | tf_op jit(solution)/shard_map/ppermute | solution.py:281
  120.7 1.0 shard_map.95
  (12 shorter events, 0.0 us)
Async XLA Ops:
  0.6 34.7 %copy-start = (bf16[3648,256]{1,0:T(8,128)(2,1)S(1)}, bf16[3648,256]{1,0:T(8,128)(2,1)}, u32[]{:S(2)}) copy-start(bf16[3648,256]{1,0:T(8,128)(2,1)} %constant.4.clone.table_ref) | copy-start | bytes 5603332
  0.6 34.7 %copy-start.4 = (f32[272,256]{1,0:T(8,128)S(1)}, f32[272,256]{1,0:T(8,128)}, u32[]{:S(2)}) copy-start(f32[272,256]{1,0:T(8,128)} %constant.5.clone.turn_ref) | copy-start | bytes 835588
  4.3 22.3 %collective-permute-start = (f32[3,2,128,256]{3,2,1,0:T(8,128)}, f32[3,2,128,256]{3,2,1,0:T(8,128)S(1)}, u32[]{:S(2)}, u32[]{:S(2)}) collective-permute-start(f32[3,2,128,256]{3,2,1,0:T(8,128)} %get-tuple-element.24), channel_id=1, source_target_pairs={{0,2},{1,3},{2,0},{3,1},{4,6},{5,7},{6,4},{7,5},{8,10},{9,11},{10,... | collective-permute-start | bytes 2359304 | tf_op jit(solution)/shard_map/ppermute | solution.py:281
  7.2 23.1 %collective-permute-start.1 = (f32[3,2,128,256]{3,2,1,0:T(8,128)}, f32[3,2,128,256]{3,2,1,0:T(8,128)}, u32[]{:S(2)}, u32[]{:S(2)}) collective-permute-start(f32[3,2,128,256]{3,2,1,0:T(8,128)} %get-tuple-element.25), channel_id=1, source_target_pairs={{0,4},{1,5},{2,6},{3,7},{4,0},{5,1},{6,2},{7,3},{8,12},{9,13},{10,... | collective-permute-start | bytes 2359304 | tf_op jit(solution)/shard_map/ppermute | solution.py:281
  14.4 45.4 %copy-start.5 = (bf16[3,256,128]{2,1,0:T(8,128)(2,1)S(1)}, bf16[3,256,128]{2,1,0:T(8,128)(2,1)}, u32[]{:S(2)}) copy-start(bf16[3,256,128]{2,1,0:T(8,128)(2,1)} %get-tuple-element.28.gates_ref) | copy-start | bytes 589828
  14.4 21.0 %all-to-all-start = ((f32[16,3,16,128]{3,2,1,0:T(8,128)}), f32[16,3,16,128]{3,2,1,0:T(8,128)S(1)}, u32[]{:S(2)}, u32[]{:S(2)}) async-start(f32[16,3,16,128]{3,2,1,0:T(8,128)} %get-tuple-element.22), calls=%async_computation | async-start | bytes 786432 | tf_op jit(solution)/shard_map/all_to_all | solution.py:324
  26.5 0.9 copy-start.1
  30.3 1.1 copy-start.2
  31.5 1.0 copy-start.3
  33.9 0.7 copy-start.6
  34.6 0.7 copy-start.7
  38.7 21.1 %all-to-all-start.1 = ((f32[16,3,16,128]{3,2,1,0:T(8,128)}), f32[16,3,16,128]{3,2,1,0:T(8,128)S(1)}, u32[]{:S(2)}, u32[]{:S(2)}) async-start(f32[16,3,16,128]{3,2,1,0:T(8,128)} %shard_map.88), calls=%async_computation.1 | async-start | bytes 786432 | tf_op jit(solution)/shard_map/all_to_all | solution.py:334
  44.6 15.1 %collective-permute-start.2 = (f32[1,2,128,256]{3,2,1,0:T(8,128)}, f32[1,2,128,256]{3,2,1,0:T(8,128)S(1)}, u32[]{:S(2)}, u32[]{:S(2)}) collective-permute-start(f32[1,2,128,256]{3,2,1,0:T(8,128)} %copy-done.7), channel_id=1, source_target_pairs={{0,4},{1,5},{2,6},{3,7},{4,0},{5,1},{6,2},{7,3},{8,12},{9,13},{10,... | collective-permute-start | bytes 786440 | tf_op jit(solution)/shard_map/ppermute | solution.py:281
  46.5 13.1 %collective-permute-start.3 = (f32[1,2,128,256]{3,2,1,0:T(8,128)}, f32[1,2,128,256]{3,2,1,0:T(8,128)S(1)}, u32[]{:S(2)}, u32[]{:S(2)}) collective-permute-start(f32[1,2,128,256]{3,2,1,0:T(8,128)} %copy-done.6), channel_id=1, source_target_pairs={{0,2},{1,3},{2,0},{3,1},{4,6},{5,7},{6,4},{7,5},{8,10},{9,11},{10,... | collective-permute-start | bytes 786440 | tf_op jit(solution)/shard_map/ppermute | solution.py:281
  60.7 5.5 %collective-permute-start.4 = (f32[128,256]{1,0:T(8,128)S(1)}, f32[128,256]{1,0:T(8,128)S(1)}, u32[]{:S(2)}, u32[]{:S(2)}) collective-permute-start(f32[128,256]{1,0:T(8,128)S(1)} %get-tuple-element.34.refs_0_), channel_id=1, source_target_pairs={{0,2},{1,3},{2,0},{3,1},{4,6},{5,7},{6,4},{7,5},{8,10},{9,11},{10,... | collective-permute-start | bytes 393224 | tf_op jit(solution)/shard_map/ppermute | solution.py:281
  62.1 6.2 %collective-permute-start.5 = (f32[128,256]{1,0:T(8,128)S(1)}, f32[128,256]{1,0:T(8,128)S(1)}, u32[]{:S(2)}, u32[]{:S(2)}) collective-permute-start(f32[128,256]{1,0:T(8,128)S(1)} %get-tuple-element.34.refs_0_), channel_id=1, source_target_pairs={{0,4},{1,5},{2,6},{3,7},{4,0},{5,1},{6,2},{7,3},{8,12},{9,13},{10,... | collective-permute-start | bytes 393224 | tf_op jit(solution)/shard_map/ppermute | solution.py:281
  62.7 7.0 %collective-permute-start.6 = (f32[128,256]{1,0:T(8,128)S(1)}, f32[128,256]{1,0:T(8,128)S(1)}, u32[]{:S(2)}, u32[]{:S(2)}) collective-permute-start(f32[128,256]{1,0:T(8,128)S(1)} %get-tuple-element.34.refs_0_), channel_id=1, source_target_pairs={{0,6},{1,7},{2,4},{3,5},{4,2},{5,3},{6,0},{7,1},{8,14},{9,15},{10,... | collective-permute-start | bytes 393224 | tf_op jit(solution)/shard_map/ppermute | solution.py:281
  70.0 3.6 %collective-permute-start.7 = (f32[512,256]{1,0:T(8,128)S(1)}, f32[512,256]{1,0:T(8,128)S(1)}, u32[]{:S(2)}, u32[]{:S(2)}) collective-permute-start(f32[512,256]{1,0:T(8,128)S(1)} %shard_map.91), channel_id=1, source_target_pairs={{0,1},{1,0},{2,3},{3,2},{4,5},{5,4},{6,7},{7,6},{8,9},{9,8},{10,11... | collective-permute-start | bytes 1572872 | tf_op jit(solution)/shard_map/ppermute | solution.py:281
  70.1 14.8 %collective-permute-start.10 = (f32[128,512]{1,0:T(8,128)S(1)}, f32[128,512]{1,0:T(8,128)S(1)}, u32[]{:S(2)}, u32[]{:S(2)}) collective-permute-start(f32[128,512]{1,0:T(8,128)S(1)} %get-tuple-element.37.refs_0_), channel_id=1, source_target_pairs={{0,4},{1,5},{2,6},{3,7},{4,0},{5,1},{6,2},{7,3},{8,12},{9,13},{10,... | collective-permute-start | bytes 786440 | tf_op jit(solution)/shard_map/ppermute | solution.py:281
  70.9 20.1 %collective-permute-start.11 = (f32[128,512]{1,0:T(8,128)S(1)}, f32[128,512]{1,0:T(8,128)S(1)}, u32[]{:S(2)}, u32[]{:S(2)}) collective-permute-start(f32[128,512]{1,0:T(8,128)S(1)} %get-tuple-element.37.refs_0_), channel_id=1, source_target_pairs={{0,6},{1,7},{2,4},{3,5},{4,2},{5,3},{6,0},{7,1},{8,14},{9,15},{10,... | collective-permute-start | bytes 786440 | tf_op jit(solution)/shard_map/ppermute | solution.py:281
  73.1 17.9 %collective-permute-start.9 = (f32[128,512]{1,0:T(8,128)S(1)}, f32[128,512]{1,0:T(8,128)S(1)}, u32[]{:S(2)}, u32[]{:S(2)}) collective-permute-start(f32[128,512]{1,0:T(8,128)S(1)} %get-tuple-element.37.refs_0_), channel_id=1, source_target_pairs={{0,2},{1,3},{2,0},{3,1},{4,6},{5,7},{6,4},{7,5},{8,10},{9,11},{10,... | collective-permute-start | bytes 786440 | tf_op jit(solution)/shard_map/ppermute | solution.py:281
  74.0 17.0 %collective-permute-start.8 = (f32[256,256]{1,0:T(8,128)S(1)}, f32[256,256]{1,0:T(8,128)S(1)}, u32[]{:S(2)}, u32[]{:S(2)}) collective-permute-start(f32[256,256]{1,0:T(8,128)S(1)} %get-tuple-element.36), channel_id=1, source_target_pairs={{0,8},{1,9},{2,10},{3,11},{4,12},{5,13},{6,14},{7,15},{8,0},{9,1},... | collective-permute-start | bytes 786440 | tf_op jit(solution)/shard_map/ppermute | solution.py:281
  91.4 2.7 %collective-permute-start.12 = (f32[512,512]{1,0:T(8,128)S(1)}, f32[512,512]{1,0:T(8,128)S(1)}, u32[]{:S(2)}, u32[]{:S(2)}) collective-permute-start(f32[512,512]{1,0:T(8,128)S(1)} %shard_map.93), channel_id=1, source_target_pairs={{0,1},{1,0},{2,3},{3,2},{4,5},{5,4},{6,7},{7,6},{8,9},{9,8},{10,11... | collective-permute-start | bytes 3145736 | tf_op jit(solution)/shard_map/ppermute | solution.py:281
  94.6 26.2 %collective-permute-start.13 = (f32[256,512]{1,0:T(8,128)S(1)}, f32[256,512]{1,0:T(8,128)S(1)}, u32[]{:S(2)}, u32[]{:S(2)}) collective-permute-start(f32[256,512]{1,0:T(8,128)S(1)} %get-tuple-element.39), channel_id=1, source_target_pairs={{0,8},{1,9},{2,10},{3,11},{4,12},{5,13},{6,14},{7,15},{8,0},{9,1},... | collective-permute-start | bytes 1572872 | tf_op jit(solution)/shard_map/ppermute | solution.py:281
where the time goes:
time: 122 us
  waiting for transfers between devices  64.8 us (53%)
  starting transfers between devices  28.4 us (23%)
  Pallas kernels  17.4 us (14%)
  matrix products  5.89 us (5%)
  local copies, waits for them, and re-layouts  4.46 us (4%)
    ppermute x14, waiting for transfers between devices, exchange(): return lax.ppermute(value, 'seq', [(i, i ^ flip) for i in range(blocks)])  64.8 us
    ppermute x14, starting transfers between devices, exchange(): return lax.ppermute(value, 'seq', [(i, i ^ flip) for i in range(blocks)])  18.4 us
    all_to_all x1, starting transfers between devices, per_device(): lax.all_to_all(results, 'seq', split_axis=0, concat_axis=0, tiled=True)  5.91 us
    dot_general x1, matrix products, per_device(): lax.dot_general(grad_proj, in_weight, (((1,), (1,)), ((), ())), preferred...  5.89 us
    pallas_call x1, Pallas kernels, per_device(): pl.pallas_call(functools.partial(project_kernel, scaling), grid=(steps,),...  5.6 us
    unnamed x16, local copies, waits for them, and re-layouts  4.46 us
    all_to_all x1, starting transfers between devices, per_device(): lax.all_to_all(signals, 'seq', split_axis=0, concat_axis=0, tiled=True)  4.1 us
    pallas_call x1, Pallas kernels, per_device(): pl.pallas_call(layout_kernel, out_shape=[shaped(2, far, rows, part)] + [s...  3.61 us
  transfers between devices with their start and end apart: 16, of which 10 were waited for; matrix products, arithmetic and copies ran while one was open for 5% of the time, Pallas kernels for 6%

commit v1 on v0

--- a/solution.py
+++ b/solution.py
@@ -9,8 +9,7 @@
 from jax.experimental.pallas import tpu as pltpu
 from jax.sharding import PartitionSpec as P
 
-VMEM_LIMIT = 48 * 1024 * 1024
-VMEM_WIDE = 60 * 1024 * 1024
+VMEM_LIMIT = 28 * 1024 * 1024
 SIDE = 4
 
 
@@ -272,7 +271,6 @@
     scaling = 1.0 / math.sqrt(rows * blocks)
     f32, bf16 = jnp.float32, jnp.bfloat16
     params = pltpu.CompilerParams(vmem_limit_bytes=VMEM_LIMIT)
-    wide = pltpu.CompilerParams(vmem_limit_bytes=VMEM_WIDE)
 
     def shaped(*shape, dtype=f32):
         return jax.ShapeDtypeStruct(shape, dtype)
@@ -285,7 +283,7 @@
     own, to_y, to_z = pl.pallas_call(
         layout_kernel,
         out_shape=[shaped(2, far, rows, part)] + [shaped(3, far, rows, part)] * 2,
-        compiler_params=wide,
+        compiler_params=params,
     )(inputs)
     from_y, from_z = exchange(to_y, 2), exchange(to_z, 4)
     *turned, relay_z, relay_y = pl.pallas_call(
@@ -313,7 +311,7 @@
         + [pl.BlockSpec((3, channels, rows), lambda i: (0, 0, 0))],
         out_shape=[shaped(blocks, 3, width, rows), shaped(3, channels, rows, dtype=bf16)],
         scratch_shapes=[pltpu.VMEM((rows, columns), f32)],
-        compiler_params=wide,
+        compiler_params=params,
         cost_estimate=pl.CostEstimate(
             flops=2 * rows * depth * columns,
             bytes_accessed=2 * depth * (rows + columns),
@@ -337,7 +335,7 @@
         out_shape=[shaped(far * part, rows, dtype=bf16)] * 2,
         compiler_params=params,
         cost_estimate=pl.CostEstimate(
-            flops=0, bytes_accessed=200 * SIDE * far * rows * part, transcendentals=0
+            flops=0, bytes_accessed=800 * SIDE * far * rows * part, transcendentals=0
         ),
     )(*corners)
     grad_proj, sent_first, sent_rest, grad_taps = pl.pallas_call(

time: 122 us -> 121 us (level)
  Pallas kernels: 17.4 us -> 11.8 us
  local copies, waits for them, and re-layouts: 4.46 us -> 9.61 us
  waiting for transfers between devices: 64.8 us -> 69.7 us
  matrix products: 5.89 us -> 3.1 us
  starting transfers between devices: 28.4 us -> 25.8 us
    unnamed x16 -> x24, local copies, waits for them, and re-layouts: 4.46 us -> 9.61 us
    pallas_call x1, Pallas kernels: 5.6 us -> 2.7 us  [per_device(): pl.pallas_call(functools.partial(project_kernel, scaling), grid=(steps,),...]
    all_to_all x1, waiting for transfers between devices: 0.01 us -> 2.85 us  [per_device(): lax.all_to_all(signals, 'seq', split_axis=0, concat_axis=0, tiled=True)]
    dot_general x1, matrix products: 5.89 us -> 3.1 us  [per_device(): lax.dot_general(grad_proj, in_weight, (((1,), (1,)), ((), ())), preferred...]
    all_to_all x1, starting transfers between devices: 5.91 us -> 3.55 us  [per_device(): lax.all_to_all(results, 'seq', split_axis=0, concat_axis=0, tiled=True)]
    ppermute x14, waiting for transfers between devices: 64.8 us -> 66.9 us  [exchange(): return lax.ppermute(value, 'seq', [(i, i ^ flip) for i in range(blocks)])]
    pallas_call x1, Pallas kernels: 3.61 us -> 2.09 us  [per_device(): pl.pallas_call(layout_kernel, out_shape=[shaped(2, far, rows, part)] + [s...]
  transfers between devices with their start and end apart: 16 -> 16, of which waited for: 10 -> 11; matrix products, arithmetic and copies ran while one was open for 5% -> 3% of each run, Pallas kernels for 6% -> 3%
where the time goes in v1:
time: 121 us
  waiting for transfers between devices  69.7 us (58%)
  starting transfers between devices  25.8 us (21%)
  Pallas kernels  11.8 us (10%)
  local copies, waits for them, and re-layouts  9.61 us (8%)
  matrix products  3.1 us (3%)
    ppermute x14, waiting for transfers between devices, exchange(): return lax.ppermute(value, 'seq', [(i, i ^ flip) for i in range(blocks)])  66.9 us
    ppermute x14, starting transfers between devices, exchange(): return lax.ppermute(value, 'seq', [(i, i ^ flip) for i in range(blocks)])  18.3 us
    unnamed x24, local copies, waits for them, and re-layouts  9.61 us
    all_to_all x1, starting transfers between devices, per_device(): lax.all_to_all(signals, 'seq', split_axis=0, concat_axis=0, tiled=True)  3.97 us
    all_to_all x1, starting transfers between devices, per_device(): lax.all_to_all(results, 'seq', split_axis=0, concat_axis=0, tiled=True)  3.55 us
    pallas_call x1, Pallas kernels, per_device(): pl.pallas_call(functools.partial(conv_kernel, places), in_specs=[inside]...  3.33 us
    dot_general x1, matrix products, per_device(): lax.dot_general(grad_proj, in_weight, (((1,), (1,)), ((), ())), preferred...  3.1 us
    all_to_all x1, waiting for transfers between devices, per_device(): lax.all_to_all(signals, 'seq', split_axis=0, concat_axis=0, tiled=True)  2.85 us
  transfers between devices with their start and end apart: 16, of which 11 were waited for; matrix products, arithmetic and copies ran while one was open for 3% of the time, Pallas kernels for 3%

profile of v1, /device:TPU:0, one launch (start us, length us, event | category | flops | bytes accessed | tf_op | source)
XLA Modules:
  0.0 120.8 jit_solution(1930699478382196630)
XLA Ops:
  0.6 1.2 %copy-done.1 = bf16[128,4096]{1,0:T(8,128)(2,1)S(1)} copy-done((bf16[128,4096]{1,0:T(8,128)(2,1)S(1)}, bf16[128,4096]{1,0:T(8,128)(2,1)}, u32[]{:S(2)}) %copy-start.1) | copy-done | bytes 1048600
  1.9 2.1 %shard_map.86 = (f32[2,2,128,256]{3,2,1,0:T(8,128)S(1)}, f32[3,2,128,256]{3,2,1,0:T(8,128)}, f32[3,2,128,256]{3,2,1,0:T(8,128)}) custom-call(bf16[128,4096]{1,0:T(8,128)(2,1)S(1)} %copy-done.1), custom_call_target="tpu_custom_call" | custom-call | tf_op jit(solution)/shard_map/pallas_call | solution.py:283
  4.0 3.0 %collective-permute-start = (f32[3,2,128,256]{3,2,1,0:T(8,128)}, f32[3,2,128,256]{3,2,1,0:T(8,128)S(1)}, u32[]{:S(2)}, u32[]{:S(2)}) collective-permute-start(f32[3,2,128,256]{3,2,1,0:T(8,128)} %get-tuple-element.24), channel_id=1, source_target_pairs={{0,2},{1,3},{2,0},{3,1},{4,6},{5,7},{6,4},{7,5},{8,10},{9,11},{10,... | collective-permute-start | bytes 2359304 | tf_op jit(solution)/shard_map/ppermute | solution.py:279
  6.9 1.6 %collective-permute-start.1 = (f32[3,2,128,256]{3,2,1,0:T(8,128)}, f32[3,2,128,256]{3,2,1,0:T(8,128)S(1)}, u32[]{:S(2)}, u32[]{:S(2)}) collective-permute-start(f32[3,2,128,256]{3,2,1,0:T(8,128)} %get-tuple-element.25), channel_id=1, source_target_pairs={{0,4},{1,5},{2,6},{3,7},{4,0},{5,1},{6,2},{7,3},{8,12},{9,13},{10,... | collective-permute-start | bytes 2359304 | tf_op jit(solution)/shard_map/ppermute | solution.py:279
  8.5 2.8 %copy-done = bf16[4096,768]{1,0:T(8,128)(2,1)S(1)} copy-done((bf16[4096,768]{1,0:T(8,128)(2,1)S(1)}, bf16[4096,768]{1,0:T(8,128)(2,1)}, u32[]{:S(2)}) %copy-start) | copy-done | bytes 6291480
  11.3 0.9 copy-done.6
  12.2 0.8 copy-done.7
  13.0 2.7 %shard_map.85 = (f32[16,3,16,128]{3,2,1,0:T(8,128)}, bf16[3,256,128]{2,1,0:T(8,128)(2,1)S(1)}) custom-call(bf16[128,4096]{1,0:T(8,128)(2,1)S(1)} %copy-done.1, bf16[4096,768]{1,0:T(8,128)(2,1)S(1)} %copy-done, f32[128,256]{1,0:T(8,128)S(1)} %copy-done.6, bf16[128,256]{1,0:T(8,128)(2,1)S(1)} %copy-done.7), custom_call_target="tpu_custom_call" | custom-call | flops 805306368 | bytes 7340032 | tf_op jit(solution)/shard_map/pallas_call | solution.py:299
  15.7 4.0 %all-to-all-start = ((f32[16,3,16,128]{3,2,1,0:T(8,128)}), f32[16,3,16,128]{3,2,1,0:T(8,128)S(1)}, u32[]{:S(2)}, u32[]{:S(2)}) async-start(f32[16,3,16,128]{3,2,1,0:T(8,128)} %get-tuple-element.22), calls=%async_computation | async-start | bytes 786432 | tf_op jit(solution)/shard_map/all_to_all | solution.py:322
  19.7 6.1 %collective-permute-done.y_ref = f32[3,2,128,256]{3,2,1,0:T(8,128)S(1)} collective-permute-done((f32[3,2,128,256]{3,2,1,0:T(8,128)}, f32[3,2,128,256]{3,2,1,0:T(8,128)S(1)}, u32[]{:S(2)}, u32[]{:S(2)}) %collective-permute-start) | collective-permute-done | bytes 786464 | tf_op jit(solution)/shard_map/ppermute | solution.py:279
  25.8 4.1 %collective-permute-done.1.z_ref = f32[3,2,128,256]{3,2,1,0:T(8,128)S(1)} collective-permute-done((f32[3,2,128,256]{3,2,1,0:T(8,128)}, f32[3,2,128,256]{3,2,1,0:T(8,128)S(1)}, u32[]{:S(2)}, u32[]{:S(2)}) %collective-permute-start.1) | collective-permute-done | bytes 786464 | tf_op jit(solution)/shard_map/ppermute | solution.py:279
  29.9 0.3 shard_map.87
  30.2 0.7 copy-done.8
  30.9 0.7 copy-done.9
  31.6 2.8 %all-to-all-done.x_ref = f32[16,3,16,128]{3,2,1,0:T(8,128)S(1)} async-done(((f32[16,3,16,128]{3,2,1,0:T(8,128)}), f32[16,3,16,128]{3,2,1,0:T(8,128)S(1)}, u32[]{:S(2)}, u32[]{:S(2)}) %all-to-all-start) | async-done | bytes 393248 | tf_op jit(solution)/shard_map/all_to_all | solution.py:322
  34.5 1.5 %copy-done.2 = bf16[3648,256]{1,0:T(8,128)(2,1)S(1)} copy-done((bf16[3648,256]{1,0:T(8,128)(2,1)S(1)}, bf16[3648,256]{1,0:T(8,128)(2,1)}, u32[]{:S(2)}) %copy-start.2) | copy-done | bytes 1867800
  36.0 3.3 %shard_map.88 = f32[16,3,16,128]{3,2,1,0:T(8,128)} custom-call(f32[16,3,16,128]{3,2,1,0:T(8,128)S(1)} %all-to-all-done.x_ref, bf16[3648,256]{1,0:T(8,128)(2,1)S(1)} %copy-done.2, f32[272,256]{1,0:T(8,128)S(1)} %copy-done.3, bf16[512,384]{1,0:T(8,128)(2,1)S(1)} %get-tuple-element.26.refs_0_.x_ref, bf16[512,384]{1,0:T(8,128)(2,1)S(1)} %get-tuple-element.27.refs_1_.x_ref), custom_call_target="tpu_custom_call" | custom-call | tf_op jit(solution)/shard_map/pallas_call | solution.py:325
  39.3 3.6 %all-to-all-start.1 = ((f32[16,3,16,128]{3,2,1,0:T(8,128)}), f32[16,3,16,128]{3,2,1,0:T(8,128)S(1)}, u32[]{:S(2)}, u32[]{:S(2)}) async-start(f32[16,3,16,128]{3,2,1,0:T(8,128)} %shard_map.88), calls=%async_computation.1 | async-start | bytes 786432 | tf_op jit(solution)/shard_map/all_to_all | solution.py:332
  42.9 1.8 %collective-permute-start.2 = (f32[1,2,128,256]{3,2,1,0:T(8,128)}, f32[1,2,128,256]{3,2,1,0:T(8,128)S(1)}, u32[]{:S(2)}, u32[]{:S(2)}) collective-permute-start(f32[1,2,128,256]{3,2,1,0:T(8,128)} %copy-done.9), channel_id=1, source_target_pairs={{0,4},{1,5},{2,6},{3,7},{4,0},{5,1},{6,2},{7,3},{8,12},{9,13},{10,... | collective-permute-start | bytes 786440 | tf_op jit(solution)/shard_map/ppermute | solution.py:279
  44.7 1.5 %collective-permute-start.3 = (f32[1,2,128,256]{3,2,1,0:T(8,128)}, f32[1,2,128,256]{3,2,1,0:T(8,128)S(1)}, u32[]{:S(2)}, u32[]{:S(2)}) collective-permute-start(f32[1,2,128,256]{3,2,1,0:T(8,128)} %copy-done.8), channel_id=1, source_target_pairs={{0,2},{1,3},{2,0},{3,1},{4,6},{5,7},{6,4},{7,5},{8,10},{9,11},{10,... | collective-permute-start | bytes 786440 | tf_op jit(solution)/shard_map/ppermute | solution.py:279
  46.2 11.7 %collective-permute-done.2.corner_own_ref = f32[1,2,128,256]{3,2,1,0:T(8,128)S(1)} collective-permute-done((f32[1,2,128,256]{3,2,1,0:T(8,128)}, f32[1,2,128,256]{3,2,1,0:T(8,128)S(1)}, u32[]{:S(2)}, u32[]{:S(2)}) %collective-permute-start.2) | collective-permute-done | bytes 262176 | tf_op jit(solution)/shard_map/ppermute | solution.py:279
  57.8 0.0 collective-permute-done.3.corner_other_ref
  57.8 0.1 shard_map.89
  58.0 0.9 copy-done.5
  58.9 0.8 shard_map.90
  59.7 1.5 %collective-permute-start.4 = (f32[128,256]{1,0:T(8,128)S(1)}, f32[128,256]{1,0:T(8,128)S(1)}, u32[]{:S(2)}, u32[]{:S(2)}) collective-permute-start(f32[128,256]{1,0:T(8,128)S(1)} %get-tuple-element.34.refs_0_), channel_id=1, source_target_pairs={{0,2},{1,3},{2,0},{3,1},{4,6},{5,7},{6,4},{7,5},{8,10},{9,11},{10,... | collective-permute-start | bytes 393224 | tf_op jit(solution)/shard_map/ppermute | solution.py:279
  61.2 0.5 collective-permute-start.5
  61.8 1.5 %collective-permute-start.6 = (f32[128,256]{1,0:T(8,128)S(1)}, f32[128,256]{1,0:T(8,128)S(1)}, u32[]{:S(2)}, u32[]{:S(2)}) collective-permute-start(f32[128,256]{1,0:T(8,128)S(1)} %get-tuple-element.34.refs_0_), channel_id=1, source_target_pairs={{0,6},{1,7},{2,4},{3,5},{4,2},{5,3},{6,0},{7,1},{8,14},{9,15},{10,... | collective-permute-start | bytes 393224 | tf_op jit(solution)/shard_map/ppermute | solution.py:279
  63.2 2.0 %collective-permute-done.4.refs_1_ = f32[128,256]{1,0:T(8,128)S(1)} collective-permute-done((f32[128,256]{1,0:T(8,128)S(1)}, f32[128,256]{1,0:T(8,128)S(1)}, u32[]{:S(2)}, u32[]{:S(2)}) %collective-permute-start.4) | collective-permute-done | bytes 131104 | tf_op jit(solution)/shard_map/ppermute | solution.py:279
  65.3 2.1 %collective-permute-done.5.refs_2_ = f32[128,256]{1,0:T(8,128)S(1)} collective-permute-done((f32[128,256]{1,0:T(8,128)S(1)}, f32[128,256]{1,0:T(8,128)S(1)}, u32[]{:S(2)}, u32[]{:S(2)}) %collective-permute-start.5) | collective-permute-done | bytes 131104 | tf_op jit(solution)/shard_map/ppermute | solution.py:279
  67.4 1.4 %collective-permute-done.6.refs_3_ = f32[128,256]{1,0:T(8,128)S(1)} collective-permute-done((f32[128,256]{1,0:T(8,128)S(1)}, f32[128,256]{1,0:T(8,128)S(1)}, u32[]{:S(2)}, u32[]{:S(2)}) %collective-permute-start.6) | collective-permute-done | bytes 131104 | tf_op jit(solution)/shard_map/ppermute | solution.py:279
  68.8 0.3 shard_map.91
  69.1 0.1 collective-permute-start.7
  69.2 0.7 collective-permute-start.10
  69.9 2.3 %collective-permute-start.11 = (f32[128,512]{1,0:T(8,128)S(1)}, f32[128,512]{1,0:T(8,128)S(1)}, u32[]{:S(2)}, u32[]{:S(2)}) collective-permute-start(f32[128,512]{1,0:T(8,128)S(1)} %get-tuple-element.37.refs_0_), channel_id=1, source_target_pairs={{0,6},{1,7},{2,4},{3,5},{4,2},{5,3},{6,0},{7,1},{8,14},{9,15},{10,... | collective-permute-start | bytes 786440 | tf_op jit(solution)/shard_map/ppermute | solution.py:279
  72.2 0.6 collective-permute-start.9
  72.7 0.3 shard_map.92
  73.0 2.5 %collective-permute-start.8 = (f32[256,256]{1,0:T(8,128)S(1)}, f32[256,256]{1,0:T(8,128)S(1)}, u32[]{:S(2)}, u32[]{:S(2)}) collective-permute-start(f32[256,256]{1,0:T(8,128)S(1)} %get-tuple-element.36), channel_id=1, source_target_pairs={{0,8},{1,9},{2,10},{3,11},{4,12},{5,13},{6,14},{7,15},{8,0},{9,1},... | collective-permute-start | bytes 786440 | tf_op jit(solution)/shard_map/ppermute | solution.py:279
  75.6 8.4 %collective-permute-done.10.refs_2_ = f32[128,512]{1,0:T(8,128)S(1)} collective-permute-done((f32[128,512]{1,0:T(8,128)S(1)}, f32[128,512]{1,0:T(8,128)S(1)}, u32[]{:S(2)}, u32[]{:S(2)}) %collective-permute-start.10) | collective-permute-done | bytes 262176 | tf_op jit(solution)/shard_map/ppermute | solution.py:279
  84.0 6.1 %collective-permute-done.11.refs_3_ = f32[128,512]{1,0:T(8,128)S(1)} collective-permute-done((f32[128,512]{1,0:T(8,128)S(1)}, f32[128,512]{1,0:T(8,128)S(1)}, u32[]{:S(2)}, u32[]{:S(2)}) %collective-permute-start.11) | collective-permute-done | bytes 262176 | tf_op jit(solution)/shard_map/ppermute | solution.py:279
  90.0 0.4 shard_map.93
  90.5 0.1 collective-permute-start.12
  90.6 2.6 %collective-permute-done.12.refs_4_ = f32[512,512]{1,0:T(8,128)S(1)} collective-permute-done((f32[512,512]{1,0:T(8,128)S(1)}, f32[512,512]{1,0:T(8,128)S(1)}, u32[]{:S(2)}, u32[]{:S(2)}) %collective-permute-start.12) | collective-permute-done | bytes 1048608 | tf_op jit(solution)/shard_map/ppermute | solution.py:279
  93.2 0.4 shard_map.94
  93.7 0.7 collective-permute-start.13
  94.4 3.1 %convolution_convert_fusion = bf16[128,4096]{1,0:T(8,128)(2,1)} fusion(bf16[128,768]{1,0:T(8,128)(2,1)S(1)} %get-tuple-element.33, bf16[4096,768]{1,0:T(8,128)(2,1)S(1)} %bitcast.3), kind=kOutput, calls=%fused_computation | convolution fusion | flops 805830656 | bytes 7536640 | tf_op jit(solution)/shard_map/dot_general | solution.py:353
  97.5 22.3 %collective-permute-done.13.refs_3_ = f32[256,512]{1,0:T(8,128)S(1)} collective-permute-done((f32[256,512]{1,0:T(8,128)S(1)}, f32[256,512]{1,0:T(8,128)S(1)}, u32[]{:S(2)}, u32[]{:S(2)}) %collective-permute-start.13) | collective-permute-done | bytes 524320 | tf_op jit(solution)/shard_map/ppermute | solution.py:279
  119.8 1.0 shard_map.95
  (21 shorter events, 0.0 us)
Async XLA Ops:
  0.6 1.2 %copy-start.1 = (bf16[128,4096]{1,0:T(8,128)(2,1)S(1)}, bf16[128,4096]{1,0:T(8,128)(2,1)}, u32[]{:S(2)}) copy-start(bf16[128,4096]{1,0:T(8,128)(2,1)} %x_ref.3) | copy-start | bytes 3145732
  1.9 32.6 %copy-start.3 = (f32[272,256]{1,0:T(8,128)S(1)}, f32[272,256]{1,0:T(8,128)}, u32[]{:S(2)}) copy-start(f32[272,256]{1,0:T(8,128)} %constant.5.clone.turn_ref) | copy-start | bytes 835588
  4.0 21.8 %collective-permute-start = (f32[3,2,128,256]{3,2,1,0:T(8,128)}, f32[3,2,128,256]{3,2,1,0:T(8,128)S(1)}, u32[]{:S(2)}, u32[]{:S(2)}) collective-permute-start(f32[3,2,128,256]{3,2,1,0:T(8,128)} %get-tuple-element.24), channel_id=1, source_target_pairs={{0,2},{1,3},{2,0},{3,1},{4,6},{5,7},{6,4},{7,5},{8,10},{9,11},{10,... | collective-permute-start | bytes 2359304 | tf_op jit(solution)/shard_map/ppermute | solution.py:279
  6.9 23.0 %collective-permute-start.1 = (f32[3,2,128,256]{3,2,1,0:T(8,128)}, f32[3,2,128,256]{3,2,1,0:T(8,128)S(1)}, u32[]{:S(2)}, u32[]{:S(2)}) collective-permute-start(f32[3,2,128,256]{3,2,1,0:T(8,128)} %get-tuple-element.25), channel_id=1, source_target_pairs={{0,4},{1,5},{2,6},{3,7},{4,0},{5,1},{6,2},{7,3},{8,12},{9,13},{10,... | collective-permute-start | bytes 2359304 | tf_op jit(solution)/shard_map/ppermute | solution.py:279
  8.5 2.8 %copy-start = (bf16[4096,768]{1,0:T(8,128)(2,1)S(1)}, bf16[4096,768]{1,0:T(8,128)(2,1)}, u32[]{:S(2)}) copy-start(bf16[4096,768]{1,0:T(8,128)(2,1)} %w_ref.1) | copy-start | bytes 18874372
  11.3 0.9 copy-start.6
  12.2 0.8 copy-start.7
  15.7 14.2 %copy-start.4 = (bf16[3,256,128]{2,1,0:T(8,128)(2,1)}, bf16[3,256,128]{2,1,0:T(8,128)(2,1)S(1)}, u32[]{:S(2)}) copy-start(bf16[3,256,128]{2,1,0:T(8,128)(2,1)S(1)} %get-tuple-element.28.gates_ref) | copy-start | bytes 589828
  15.7 18.7 %all-to-all-start = ((f32[16,3,16,128]{3,2,1,0:T(8,128)}), f32[16,3,16,128]{3,2,1,0:T(8,128)S(1)}, u32[]{:S(2)}, u32[]{:S(2)}) async-start(f32[16,3,16,128]{3,2,1,0:T(8,128)} %get-tuple-element.22), calls=%async_computation | async-start | bytes 786432 | tf_op jit(solution)/shard_map/all_to_all | solution.py:322
  30.2 0.7 copy-start.8
  30.9 0.7 copy-start.9
  34.5 1.5 %copy-start.2 = (bf16[3648,256]{1,0:T(8,128)(2,1)S(1)}, bf16[3648,256]{1,0:T(8,128)(2,1)}, u32[]{:S(2)}) copy-start(bf16[3648,256]{1,0:T(8,128)(2,1)} %constant.4.clone.table_ref) | copy-start | bytes 5603332
  36.0 58.4 %slice-start = ((s8[6291456]{0:T(1024)(128)(4,1)}), s8[2097152]{0:T(1024)(128)(4,1)S(1)}, s32[]{:S(2)}) async-start(s8[6291456]{0:T(1024)(128)(4,1)} %bitcast.2), calls=%async_computation.2 | async-start | bytes 4194304
  39.3 18.7 %all-to-all-start.1 = ((f32[16,3,16,128]{3,2,1,0:T(8,128)}), f32[16,3,16,128]{3,2,1,0:T(8,128)S(1)}, u32[]{:S(2)}, u32[]{:S(2)}) async-start(f32[16,3,16,128]{3,2,1,0:T(8,128)} %shard_map.88), calls=%async_computation.1 | async-start | bytes 786432 | tf_op jit(solution)/shard_map/all_to_all | solution.py:332
  42.9 15.0 %collective-permute-start.2 = (f32[1,2,128,256]{3,2,1,0:T(8,128)}, f32[1,2,128,256]{3,2,1,0:T(8,128)S(1)}, u32[]{:S(2)}, u32[]{:S(2)}) collective-permute-start(f32[1,2,128,256]{3,2,1,0:T(8,128)} %copy-done.9), channel_id=1, source_target_pairs={{0,4},{1,5},{2,6},{3,7},{4,0},{5,1},{6,2},{7,3},{8,12},{9,13},{10,... | collective-permute-start | bytes 786440 | tf_op jit(solution)/shard_map/ppermute | solution.py:279
  44.7 13.1 %collective-permute-start.3 = (f32[1,2,128,256]{3,2,1,0:T(8,128)}, f32[1,2,128,256]{3,2,1,0:T(8,128)S(1)}, u32[]{:S(2)}, u32[]{:S(2)}) collective-permute-start(f32[1,2,128,256]{3,2,1,0:T(8,128)} %copy-done.8), channel_id=1, source_target_pairs={{0,2},{1,3},{2,0},{3,1},{4,6},{5,7},{6,4},{7,5},{8,10},{9,11},{10,... | collective-permute-start | bytes 786440 | tf_op jit(solution)/shard_map/ppermute | solution.py:279
  58.0 0.9 copy-start.5
  59.7 34.6 %slice-start.1 = ((s8[6291456]{0:T(1024)(128)(4,1)}), s8[4194304]{0:T(1024)(128)(4,1)S(1)}, s32[]{:S(2)}) async-start(s8[6291456]{0:T(1024)(128)(4,1)} %bitcast.2), calls=%async_computation.3 | async-start | bytes 8388608
  59.7 5.5 %collective-permute-start.4 = (f32[128,256]{1,0:T(8,128)S(1)}, f32[128,256]{1,0:T(8,128)S(1)}, u32[]{:S(2)}, u32[]{:S(2)}) collective-permute-start(f32[128,256]{1,0:T(8,128)S(1)} %get-tuple-element.34.refs_0_), channel_id=1, source_target_pairs={{0,2},{1,3},{2,0},{3,1},{4,6},{5,7},{6,4},{7,5},{8,10},{9,11},{10,... | collective-permute-start | bytes 393224 | tf_op jit(solution)/shard_map/ppermute | solution.py:279
  61.2 6.2 %collective-permute-start.5 = (f32[128,256]{1,0:T(8,128)S(1)}, f32[128,256]{1,0:T(8,128)S(1)}, u32[]{:S(2)}, u32[]{:S(2)}) collective-permute-start(f32[128,256]{1,0:T(8,128)S(1)} %get-tuple-element.34.refs_0_), channel_id=1, source_target_pairs={{0,4},{1,5},{2,6},{3,7},{4,0},{5,1},{6,2},{7,3},{8,12},{9,13},{10,... | collective-permute-start | bytes 393224 | tf_op jit(solution)/shard_map/ppermute | solution.py:279
  61.8 7.0 %collective-permute-start.6 = (f32[128,256]{1,0:T(8,128)S(1)}, f32[128,256]{1,0:T(8,128)S(1)}, u32[]{:S(2)}, u32[]{:S(2)}) collective-permute-start(f32[128,256]{1,0:T(8,128)S(1)} %get-tuple-element.34.refs_0_), channel_id=1, source_target_pairs={{0,6},{1,7},{2,4},{3,5},{4,2},{5,3},{6,0},{7,1},{8,14},{9,15},{10,... | collective-permute-start | bytes 393224 | tf_op jit(solution)/shard_map/ppermute | solution.py:279
  69.1 3.6 %collective-permute-start.7 = (f32[512,256]{1,0:T(8,128)S(1)}, f32[512,256]{1,0:T(8,128)S(1)}, u32[]{:S(2)}, u32[]{:S(2)}) collective-permute-start(f32[512,256]{1,0:T(8,128)S(1)} %shard_map.91), channel_id=1, source_target_pairs={{0,1},{1,0},{2,3},{3,2},{4,5},{5,4},{6,7},{7,6},{8,9},{9,8},{10,11... | collective-permute-start | bytes 1572872 | tf_op jit(solution)/shard_map/ppermute | solution.py:279
  69.2 14.8 %collective-permute-start.10 = (f32[128,512]{1,0:T(8,128)S(1)}, f32[128,512]{1,0:T(8,128)S(1)}, u32[]{:S(2)}, u32[]{:S(2)}) collective-permute-start(f32[128,512]{1,0:T(8,128)S(1)} %get-tuple-element.37.refs_0_), channel_id=1, source_target_pairs={{0,4},{1,5},{2,6},{3,7},{4,0},{5,1},{6,2},{7,3},{8,12},{9,13},{10,... | collective-permute-start | bytes 786440 | tf_op jit(solution)/shard_map/ppermute | solution.py:279
  69.9 20.2 %collective-permute-start.11 = (f32[128,512]{1,0:T(8,128)S(1)}, f32[128,512]{1,0:T(8,128)S(1)}, u32[]{:S(2)}, u32[]{:S(2)}) collective-permute-start(f32[128,512]{1,0:T(8,128)S(1)} %get-tuple-element.37.refs_0_), channel_id=1, source_target_pairs={{0,6},{1,7},{2,4},{3,5},{4,2},{5,3},{6,0},{7,1},{8,14},{9,15},{10,... | collective-permute-start | bytes 786440 | tf_op jit(solution)/shard_map/ppermute | solution.py:279
  72.2 17.9 %collective-permute-start.9 = (f32[128,512]{1,0:T(8,128)S(1)}, f32[128,512]{1,0:T(8,128)S(1)}, u32[]{:S(2)}, u32[]{:S(2)}) collective-permute-start(f32[128,512]{1,0:T(8,128)S(1)} %get-tuple-element.37.refs_0_), channel_id=1, source_target_pairs={{0,2},{1,3},{2,0},{3,1},{4,6},{5,7},{6,4},{7,5},{8,10},{9,11},{10,... | collective-permute-start | bytes 786440 | tf_op jit(solution)/shard_map/ppermute | solution.py:279
  73.0 17.0 %collective-permute-start.8 = (f32[256,256]{1,0:T(8,128)S(1)}, f32[256,256]{1,0:T(8,128)S(1)}, u32[]{:S(2)}, u32[]{:S(2)}) collective-permute-start(f32[256,256]{1,0:T(8,128)S(1)} %get-tuple-element.36), channel_id=1, source_target_pairs={{0,8},{1,9},{2,10},{3,11},{4,12},{5,13},{6,14},{7,15},{8,0},{9,1},... | collective-permute-start | bytes 786440 | tf_op jit(solution)/shard_map/ppermute | solution.py:279
  90.5 2.7 %collective-permute-start.12 = (f32[512,512]{1,0:T(8,128)S(1)}, f32[512,512]{1,0:T(8,128)S(1)}, u32[]{:S(2)}, u32[]{:S(2)}) collective-permute-start(f32[512,512]{1,0:T(8,128)S(1)} %shard_map.93), channel_id=1, source_target_pairs={{0,1},{1,0},{2,3},{3,2},{4,5},{5,4},{6,7},{7,6},{8,9},{9,8},{10,11... | collective-permute-start | bytes 3145736 | tf_op jit(solution)/shard_map/ppermute | solution.py:279
  93.7 26.2 %collective-permute-start.13 = (f32[256,512]{1,0:T(8,128)S(1)}, f32[256,512]{1,0:T(8,128)S(1)}, u32[]{:S(2)}, u32[]{:S(2)}) collective-permute-start(f32[256,512]{1,0:T(8,128)S(1)} %get-tuple-element.39), channel_id=1, source_target_pairs={{0,8},{1,9},{2,10},{3,11},{4,12},{5,13},{6,14},{7,15},{8,0},{9,1},... | collective-permute-start | bytes 1572872 | tf_op jit(solution)/shard_map/ppermute | solution.py:279

commit v2 on v1

--- a/solution.py
+++ b/solution.py
@@ -10,6 +10,7 @@
 from jax.sharding import PartitionSpec as P
 
 VMEM_LIMIT = 28 * 1024 * 1024
+VMEM_STREAM = 57 * 1024 * 1024
 SIDE = 4
 
 
@@ -131,7 +132,7 @@
 
 
 def conv_kernel(places, x_ref, table_ref, turn_ref, *refs):
-    y_ref, flat = refs[-2:]
+    y_ref, taps_ref, flat = refs[-3:]
     blocks, _, width, rows = x_ref.shape
 
     def table(which):
@@ -177,15 +178,24 @@
     )
     result = dot32((u_h(), u_l()), halves(stacked))
     for p in range(blocks):
-        for s in range(3):
-            y_ref[p, s] = result[p * width : (p + 1) * width, s * rows : (s + 1) * rows]
-
-
-def gate_kernel(scaling, y_ref, gates_ref, *refs):
-    gp_ref, first_ref, rest_ref, taps_ref, flat = refs[-5:]
+        piece = result[p * width : (p + 1) * width]
+        for s in range(2):
+            y_ref[p, s] = piece[:, s * rows : (s + 1) * rows]
+        taps_ref[p] = piece[:, 2 * rows :]
+
+
+def taps_kernel(scaling, y_ref, taps_ref, flat):
+    count, width, _ = y_ref.shape
+    for owner in range(count):
+        flat[owner * width : (owner + 1) * width] = y_ref[owner]
+    taps_ref[...] = flat[...].T * scaling
+
+
+def gate_kernel(y_ref, gates_ref, *refs):
+    gp_ref, first_ref, rest_ref, flat = refs[-4:]
     count, _, width, _ = y_ref.shape
     channels = count * width
-    for s in range(3):
+    for s in range(2):
         for owner in range(count):
             flat[s, owner * width : (owner + 1) * width] = y_ref[owner, s]
     for index in range(3):
@@ -197,7 +207,6 @@
         else:
             span = slice((index - 1) * channels, index * channels)
             rest_ref[:, span] = rounded.astype(jnp.float32)
-    taps_ref[...] = flat[2].T * scaling
 
 
 def turn_blocks(sources, out_ref):
@@ -311,7 +320,7 @@
         + [pl.BlockSpec((3, channels, rows), lambda i: (0, 0, 0))],
         out_shape=[shaped(blocks, 3, width, rows), shaped(3, channels, rows, dtype=bf16)],
         scratch_shapes=[pltpu.VMEM((rows, columns), f32)],
-        compiler_params=params,
+        compiler_params=pltpu.CompilerParams(vmem_limit_bytes=VMEM_STREAM),
         cost_estimate=pl.CostEstimate(
             flops=2 * rows * depth * columns,
             bytes_accessed=2 * depth * (rows + columns),
@@ -322,14 +331,21 @@
     signals = lax.all_to_all(signals, "seq", split_axis=0, concat_axis=0, tiled=True)
     pairs, turn = transform_tables(blocks, width, rows)
     table, places = packed(pairs)
-    results = pl.pallas_call(
+    results, taps = pl.pallas_call(
         functools.partial(conv_kernel, places),
         in_specs=[inside] * 3 + [anywhere] * 2,
-        out_shape=shaped(blocks, 3, width, rows),
+        out_shape=[shaped(blocks, 2, width, rows), shaped(blocks, width, rows)],
         scratch_shapes=[pltpu.VMEM((blocks * width, 3 * rows), f32)],
         compiler_params=params,
     )(signals, jnp.asarray(table), jnp.asarray(turn), *turned)
     results = lax.all_to_all(results, "seq", split_axis=0, concat_axis=0, tiled=True)
+    taps = lax.all_to_all(taps, "seq", split_axis=0, concat_axis=0, tiled=True)
+    grad_taps = pl.pallas_call(
+        functools.partial(taps_kernel, scaling),
+        out_shape=shaped(rows, channels),
+        scratch_shapes=[pltpu.VMEM((channels, rows), f32)],
+        compiler_params=params,
+    )(taps)
     turned_corners = pl.pallas_call(
         corner_kernel,
         out_shape=[shaped(far * part, rows, dtype=bf16)] * 2,
@@ -338,16 +354,15 @@
             flops=0, bytes_accessed=800 * SIDE * far * rows * part, transcendentals=0
         ),
     )(*corners)
-    grad_proj, sent_first, sent_rest, grad_taps = pl.pallas_call(
-        functools.partial(gate_kernel, scaling),
+    grad_proj, sent_first, sent_rest = pl.pallas_call(
+        gate_kernel,
         in_specs=[inside] * 2 + [anywhere] * 2,
         out_shape=[
             shaped(rows, columns, dtype=bf16),
             shaped(rows, channels),
             shaped(rows, columns - channels),
-            shaped(rows, channels),
         ],
-        scratch_shapes=[pltpu.VMEM((3, channels, rows), f32)],
+        scratch_shapes=[pltpu.VMEM((2, channels, rows), f32)],
         compiler_params=params,
     )(results, gates, *turned_corners)
     grad_inputs = lax.dot_general(
@@ -356,6 +371,7 @@
     terms = []
     for block in (sent_first, sent_rest):
         cols = block.shape[1]
+        before = terms[1:] + [taps] if terms else []
         gathered = [block] + [exchange(block, 2 * k) for k in range(1, SIDE)]
         cost = pl.CostEstimate(
             flops=2 * far * part * SIDE * rows * cols,
@@ -364,11 +380,11 @@
         )
         other = pl.pallas_call(
             other_kernel,
-            in_specs=[inside] * (2 + SIDE) + [anywhere] * len(terms[1:]),
+            in_specs=[inside] * (2 + SIDE) + [anywhere] * len(before),
             out_shape=shaped(far * part, cols),
             compiler_params=params,
             cost_estimate=cost,
-        )(turned[1], turned_corners[1], *gathered, *terms[1:])
+        )(turned[1], turned_corners[1], *gathered, *before)
         kept, *leaving = pl.pallas_call(
             own_kernel,
             out_shape=[shaped(part, cols)] * far,

time: 121 us -> 124 us (1.025)
  waiting for transfers between devices: 69.7 us -> 47.5 us
  blocking collectives: 0 us -> 18.8 us
  Pallas kernels: 11.8 us -> 15.2 us
  matrix products: 3.1 us -> 5.89 us
  starting transfers between devices: 25.8 us -> 27.7 us
  local copies, waits for them, and re-layouts: 9.61 us -> 7.82 us
    ppermute x14, waiting for transfers between devices: 66.9 us -> 47.5 us  [exchange(): return lax.ppermute(value, 'seq', [(i, i ^ flip) for i in range(blocks)])]
    all_to_all x0 -> x1, blocking collectives: none -> 18.8 us  [per_device(): taps = lax.all_to_all(taps, 'seq', split_axis=0, concat_axis=0, tiled=True)]
    pallas_call x1, Pallas kernels: 2.7 us -> 5.57 us  [per_device(): pl.pallas_call(functools.partial(project_kernel, scaling), grid=(steps,),...]
    all_to_all x1, waiting for transfers between devices: 2.85 us -> 0.01 us  [per_device(): lax.all_to_all(signals, 'seq', split_axis=0, concat_axis=0, tiled=True)]
    dot_general x1, matrix products: 3.1 us -> 5.89 us  [per_device(): lax.dot_general(grad_proj, in_weight, (((1,), (1,)), ((), ())), preferred...]
    all_to_all x1, starting transfers between devices: 3.55 us -> 5.92 us  [per_device(): lax.all_to_all(results, 'seq', split_axis=0, concat_axis=0, tiled=True)]
    unnamed x24, local copies, waits for them, and re-layouts: 9.61 us -> 7.82 us
  transfers between devices with their start and end apart: 16 -> 16, of which waited for: 11 -> 8; matrix products, arithmetic and copies ran while one was open for 3% -> 5% of each run, Pallas kernels for 3% -> 7%
where the time goes in v2:
time: 124 us
  waiting for transfers between devices  47.5 us (38%)
  starting transfers between devices  27.7 us (22%)
  blocking collectives  18.8 us (15%)
  Pallas kernels  15.2 us (12%)
  local copies, waits for them, and re-layouts  7.82 us (6%)
  matrix products  5.89 us (5%)
    ppermute x14, waiting for transfers between devices, exchange(): return lax.ppermute(value, 'seq', [(i, i ^ flip) for i in range(blocks)])  47.5 us
    all_to_all x1, blocking collectives, per_device(): taps = lax.all_to_all(taps, 'seq', split_axis=0, concat_axis=0, tiled=True)  18.8 us
    ppermute x14, starting transfers between devices, exchange(): return lax.ppermute(value, 'seq', [(i, i ^ flip) for i in range(blocks)])  17.7 us
    unnamed x24, local copies, waits for them, and re-layouts  7.82 us
    all_to_all x1, starting transfers between devices, per_device(): lax.all_to_all(results, 'seq', split_axis=0, concat_axis=0, tiled=True)  5.92 us
    dot_general x1, matrix products, per_device(): lax.dot_general(grad_proj, in_weight, (((1,), (1,)), ((), ())), preferred...  5.89 us
    pallas_call x1, Pallas kernels, per_device(): pl.pallas_call(functools.partial(project_kernel, scaling), grid=(steps,),...  5.57 us
    all_to_all x1, starting transfers between devices, per_device(): lax.all_to_all(signals, 'seq', split_axis=0, concat_axis=0, tiled=True)  4.1 us
  transfers between devices with their start and end apart: 16, of which 8 were waited for; matrix products, arithmetic and copies ran while one was open for 5% of the time, Pallas kernels for 7%

profile of v2, /device:TPU:0, one launch (start us, length us, event | category | flops | bytes accessed | tf_op | source)
XLA Modules:
  0.0 123.6 jit_solution(8538761441171249247)
XLA Ops:
  0.6 1.2 copy-done
  1.9 2.1 %shard_map.86 = (f32[2,2,128,256]{3,2,1,0:T(8,128)S(1)}, f32[3,2,128,256]{3,2,1,0:T(8,128)}, f32[3,2,128,256]{3,2,1,0:T(8,128)}) custom-call(bf16[128,4096]{1,0:T(8,128)(2,1)S(1)} %copy-done), custom_call_target="tpu_custom_call" | custom-call | tf_op jit(solution)/shard_map/pallas_call | solution.py:292
  4.0 0.8 copy-done.4
  4.8 3.0 %collective-permute-start = (f32[3,2,128,256]{3,2,1,0:T(8,128)}, f32[3,2,128,256]{3,2,1,0:T(8,128)S(1)}, u32[]{:S(2)}, u32[]{:S(2)}) collective-permute-start(f32[3,2,128,256]{3,2,1,0:T(8,128)} %get-tuple-element.25), channel_id=1, source_target_pairs={{0,2},{1,3},{2,0},{3,1},{4,6},{5,7},{6,4},{7,5},{8,10},{9,11},{10,... | collective-permute-start | bytes 2359304 | tf_op jit(solution)/shard_map/ppermute | solution.py:288
  7.7 1.6 %collective-permute-start.1 = (f32[3,2,128,256]{3,2,1,0:T(8,128)}, f32[3,2,128,256]{3,2,1,0:T(8,128)}, u32[]{:S(2)}, u32[]{:S(2)}) collective-permute-start(f32[3,2,128,256]{3,2,1,0:T(8,128)} %get-tuple-element.26), channel_id=1, source_target_pairs={{0,4},{1,5},{2,6},{3,7},{4,0},{5,1},{6,2},{7,3},{8,12},{9,13},{10,... | collective-permute-start | bytes 2359304 | tf_op jit(solution)/shard_map/ppermute | solution.py:288
  9.3 5.6 %shard_map.85 = (f32[16,3,16,128]{3,2,1,0:T(8,128)}, bf16[3,256,128]{2,1,0:T(8,128)(2,1)}) custom-call(bf16[128,4096]{1,0:T(8,128)(2,1)} %x_ref.3, bf16[4096,768]{1,0:T(8,128)(2,1)} %w_ref.1, f32[128,256]{1,0:T(8,128)} %taps_ref.1, bf16[128,256]{1,0:T(8,128)(2,1)} %go_ref.1), custom_call_target="tpu_custom_call" | custom-call | flops 805306368 | bytes 7340032 | tf_op jit(solution)/shard_map/pallas_call | solution.py:308
  14.9 4.1 %all-to-all-start = ((f32[16,3,16,128]{3,2,1,0:T(8,128)}), f32[16,3,16,128]{3,2,1,0:T(8,128)S(1)}, u32[]{:S(2)}, u32[]{:S(2)}) async-start(f32[16,3,16,128]{3,2,1,0:T(8,128)} %get-tuple-element.23), calls=%async_computation | async-start | bytes 786432 | tf_op jit(solution)/shard_map/all_to_all | solution.py:331
  19.0 8.1 %collective-permute-done.y_ref = f32[3,2,128,256]{3,2,1,0:T(8,128)S(1)} collective-permute-done((f32[3,2,128,256]{3,2,1,0:T(8,128)}, f32[3,2,128,256]{3,2,1,0:T(8,128)S(1)}, u32[]{:S(2)}, u32[]{:S(2)}) %collective-permute-start) | collective-permute-done | bytes 786464 | tf_op jit(solution)/shard_map/ppermute | solution.py:288
  27.0 0.9 copy-done.2
  27.9 2.9 %collective-permute-done.1.z_ref = f32[3,2,128,256]{3,2,1,0:T(8,128)} collective-permute-done((f32[3,2,128,256]{3,2,1,0:T(8,128)}, f32[3,2,128,256]{3,2,1,0:T(8,128)}, u32[]{:S(2)}, u32[]{:S(2)}) %collective-permute-start.1) | collective-permute-done | bytes 786464 | tf_op jit(solution)/shard_map/ppermute | solution.py:288
  30.8 1.1 copy-done.3
  31.9 1.0 copy-done.5
  33.0 1.4 %shard_map.87 = (bf16[512,384]{1,0:T(8,128)(2,1)S(1)}, bf16[512,384]{1,0:T(8,128)(2,1)S(1)}, f32[1,2,128,256]{3,2,1,0:T(8,128)S(1)}, f32[1,2,128,256]{3,2,1,0:T(8,128)S(1)}) custom-call(f32[2,2,128,256]{3,2,1,0:T(8,128)S(1)} %copy-done.5, f32[3,2,128,256]{3,2,1,0:T(8,128)S(1)} %copy-done.3, f32[3,2,128,256]{3,2,1,0:T(8,128)} %collective-permute-done.1.z_ref), custom_call_target="tpu_custom_call" | custom-call | bytes 52428800 | tf_op jit(solution)/shard_map/pallas_call | solution.py:298
  34.4 0.7 copy-done.10
  35.1 0.7 copy-done.11
  35.8 2.6 %shard_map.88 = (f32[16,2,16,128]{3,2,1,0:T(8,128)S(1)}, f32[16,16,128]{2,1,0:T(8,128)S(1)}) custom-call(f32[16,3,16,128]{3,2,1,0:T(8,128)S(1)} %all-to-all-done.x_ref, bf16[3648,256]{1,0:T(8,128)(2,1)S(1)} %copy-done.1, f32[272,256]{1,0:T(8,128)S(1)} %copy-done.6, bf16[512,384]{1,0:T(8,128)(2,1)S(1)} %get-tuple-element.27.refs_0_.x_ref, ...), custom_call_target="tpu_custom_call" | custom-call | tf_op jit(solution)/shard_map/pallas_call | solution.py:334
  38.4 0.0 copy-start.7
  38.4 0.7 copy-done.7
  39.1 0.7 copy-done.9
  39.8 5.9 %all-to-all-start.1 = ((f32[16,2,16,128]{3,2,1,0:T(8,128)}), f32[16,2,16,128]{3,2,1,0:T(8,128)S(1)}, u32[]{:S(2)}, u32[]{:S(2)}) async-start(f32[16,2,16,128]{3,2,1,0:T(8,128)} %copy-done.7), calls=%async_computation.1 | async-start | bytes 524288 | tf_op jit(solution)/shard_map/all_to_all | solution.py:341
  45.7 1.9 %collective-permute-start.2 = (f32[1,2,128,256]{3,2,1,0:T(8,128)}, f32[1,2,128,256]{3,2,1,0:T(8,128)S(1)}, u32[]{:S(2)}, u32[]{:S(2)}) collective-permute-start(f32[1,2,128,256]{3,2,1,0:T(8,128)} %copy-done.11), channel_id=1, source_target_pairs={{0,4},{1,5},{2,6},{3,7},{4,0},{5,1},{6,2},{7,3},{8,12},{9,13},{10,... | collective-permute-start | bytes 786440 | tf_op jit(solution)/shard_map/ppermute | solution.py:288
  47.6 1.5 %collective-permute-start.3 = (f32[1,2,128,256]{3,2,1,0:T(8,128)}, f32[1,2,128,256]{3,2,1,0:T(8,128)S(1)}, u32[]{:S(2)}, u32[]{:S(2)}) collective-permute-start(f32[1,2,128,256]{3,2,1,0:T(8,128)} %copy-done.10), channel_id=1, source_target_pairs={{0,2},{1,3},{2,0},{3,1},{4,6},{5,7},{6,4},{7,5},{8,10},{9,11},{10,... | collective-permute-start | bytes 786440 | tf_op jit(solution)/shard_map/ppermute | solution.py:288
  49.1 9.6 %collective-permute-done.2.corner_own_ref = f32[1,2,128,256]{3,2,1,0:T(8,128)S(1)} collective-permute-done((f32[1,2,128,256]{3,2,1,0:T(8,128)}, f32[1,2,128,256]{3,2,1,0:T(8,128)S(1)}, u32[]{:S(2)}, u32[]{:S(2)}) %collective-permute-start.2) | collective-permute-done | bytes 262176 | tf_op jit(solution)/shard_map/ppermute | solution.py:288
  58.7 0.1 shard_map.89
  58.8 0.1 shard_map.90
  59.0 1.5 %collective-permute-start.4 = (f32[128,256]{1,0:T(8,128)S(1)}, f32[128,256]{1,0:T(8,128)S(1)}, u32[]{:S(2)}, u32[]{:S(2)}) collective-permute-start(f32[128,256]{1,0:T(8,128)S(1)} %get-tuple-element.36.refs_0_), channel_id=1, source_target_pairs={{0,2},{1,3},{2,0},{3,1},{4,6},{5,7},{6,4},{7,5},{8,10},{9,11},{10,... | collective-permute-start | bytes 393224 | tf_op jit(solution)/shard_map/ppermute | solution.py:288
  60.5 0.6 collective-permute-start.5
  61.1 1.5 %collective-permute-start.6 = (f32[128,256]{1,0:T(8,128)S(1)}, f32[128,256]{1,0:T(8,128)S(1)}, u32[]{:S(2)}, u32[]{:S(2)}) collective-permute-start(f32[128,256]{1,0:T(8,128)S(1)} %get-tuple-element.36.refs_0_), channel_id=1, source_target_pairs={{0,6},{1,7},{2,4},{3,5},{4,2},{5,3},{6,0},{7,1},{8,14},{9,15},{10,... | collective-permute-start | bytes 393224 | tf_op jit(solution)/shard_map/ppermute | solution.py:288
  62.5 2.0 %collective-permute-done.4.refs_1_ = f32[128,256]{1,0:T(8,128)S(1)} collective-permute-done((f32[128,256]{1,0:T(8,128)S(1)}, f32[128,256]{1,0:T(8,128)S(1)}, u32[]{:S(2)}, u32[]{:S(2)}) %collective-permute-start.4) | collective-permute-done | bytes 131104 | tf_op jit(solution)/shard_map/ppermute | solution.py:288
  64.6 2.1 %collective-permute-done.5.refs_2_ = f32[128,256]{1,0:T(8,128)S(1)} collective-permute-done((f32[128,256]{1,0:T(8,128)S(1)}, f32[128,256]{1,0:T(8,128)S(1)}, u32[]{:S(2)}, u32[]{:S(2)}) %collective-permute-start.5) | collective-permute-done | bytes 131104 | tf_op jit(solution)/shard_map/ppermute | solution.py:288
  66.7 1.4 %collective-permute-done.6.refs_3_ = f32[128,256]{1,0:T(8,128)S(1)} collective-permute-done((f32[128,256]{1,0:T(8,128)S(1)}, f32[128,256]{1,0:T(8,128)S(1)}, u32[]{:S(2)}, u32[]{:S(2)}) %collective-permute-start.6) | collective-permute-done | bytes 131104 | tf_op jit(solution)/shard_map/ppermute | solution.py:288
  68.1 0.3 shard_map.91
  68.4 0.1 collective-permute-start.7
  68.5 0.8 collective-permute-start.10
  69.2 2.2 %collective-permute-start.11 = (f32[128,512]{1,0:T(8,128)S(1)}, f32[128,512]{1,0:T(8,128)S(1)}, u32[]{:S(2)}, u32[]{:S(2)}) collective-permute-start(f32[128,512]{1,0:T(8,128)S(1)} %get-tuple-element.39.refs_0_), channel_id=1, source_target_pairs={{0,6},{1,7},{2,4},{3,5},{4,2},{5,3},{6,0},{7,1},{8,14},{9,15},{10,... | collective-permute-start | bytes 786440 | tf_op jit(solution)/shard_map/ppermute | solution.py:288
  71.5 0.6 collective-permute-start.9
  72.0 0.3 shard_map.92
  72.3 2.4 %collective-permute-start.8 = (f32[256,256]{1,0:T(8,128)S(1)}, f32[256,256]{1,0:T(8,128)S(1)}, u32[]{:S(2)}, u32[]{:S(2)}) collective-permute-start(f32[256,256]{1,0:T(8,128)S(1)} %get-tuple-element.38), channel_id=1, source_target_pairs={{0,8},{1,9},{2,10},{3,11},{4,12},{5,13},{6,14},{7,15},{8,0},{9,1},... | collective-permute-start | bytes 786440 | tf_op jit(solution)/shard_map/ppermute | solution.py:288
  74.8 18.8 %all_to_all.15.refs_5_.y_ref = f32[16,16,128]{2,1,0:T(8,128)S(1)} all-to-all(f32[16,16,128]{2,1,0:T(8,128)} %copy-done.9), channel_id=1, replica_groups=mesh['grp'=2,'seq'=16] {'seq'}, dimensions={0} | all-to-all | bytes 262144 | tf_op jit(solution)/shard_map/all_to_all | solution.py:342
  93.5 0.4 shard_map.93
  94.0 0.1 collective-permute-start.12
  94.1 2.6 %collective-permute-done.12.refs_4_ = f32[512,512]{1,0:T(8,128)S(1)} collective-permute-done((f32[512,512]{1,0:T(8,128)S(1)}, f32[512,512]{1,0:T(8,128)S(1)}, u32[]{:S(2)}, u32[]{:S(2)}) %collective-permute-start.12) | collective-permute-done | bytes 1048608 | tf_op jit(solution)/shard_map/ppermute | solution.py:288
  96.7 0.4 shard_map.94
  97.2 0.1 collective-permute-start.13
  97.2 0.8 shard_map.96
  98.0 5.9 %convolution_convert_fusion = bf16[128,4096]{1,0:T(8,128)(2,1)} fusion(bf16[128,768]{1,0:T(8,128)(2,1)S(1)} %get-tuple-element.35, bf16[4096,768]{1,0:T(8,128)(2,1)} %w_ref.1), kind=kOutput, calls=%fused_computation | convolution fusion | flops 805830656 | bytes 7536640 | tf_op jit(solution)/shard_map/dot_general | solution.py:368
  103.9 18.8 %collective-permute-done.13.refs_3_ = f32[256,512]{1,0:T(8,128)S(1)} collective-permute-done((f32[256,512]{1,0:T(8,128)S(1)}, f32[256,512]{1,0:T(8,128)S(1)}, u32[]{:S(2)}, u32[]{:S(2)}) %collective-permute-start.13) | collective-permute-done | bytes 524320 | tf_op jit(solution)/shard_map/ppermute | solution.py:288
  122.7 1.0 shard_map.95
  (22 shorter events, 0.0 us)
Async XLA Ops:
  0.6 1.2 copy-start
  1.9 34.0 %copy-start.1 = (bf16[3648,256]{1,0:T(8,128)(2,1)S(1)}, bf16[3648,256]{1,0:T(8,128)(2,1)}, u32[]{:S(2)}) copy-start(bf16[3648,256]{1,0:T(8,128)(2,1)} %constant.4.clone.table_ref) | copy-start | bytes 5603332
  1.9 34.0 %copy-start.6 = (f32[272,256]{1,0:T(8,128)S(1)}, f32[272,256]{1,0:T(8,128)}, u32[]{:S(2)}) copy-start(f32[272,256]{1,0:T(8,128)} %constant.5.clone.turn_ref) | copy-start | bytes 835588
  4.0 0.8 copy-start.4
  4.8 22.3 %collective-permute-start = (f32[3,2,128,256]{3,2,1,0:T(8,128)}, f32[3,2,128,256]{3,2,1,0:T(8,128)S(1)}, u32[]{:S(2)}, u32[]{:S(2)}) collective-permute-start(f32[3,2,128,256]{3,2,1,0:T(8,128)} %get-tuple-element.25), channel_id=1, source_target_pairs={{0,2},{1,3},{2,0},{3,1},{4,6},{5,7},{6,4},{7,5},{8,10},{9,11},{10,... | collective-permute-start | bytes 2359304 | tf_op jit(solution)/shard_map/ppermute | solution.py:288
  7.7 23.1 %collective-permute-start.1 = (f32[3,2,128,256]{3,2,1,0:T(8,128)}, f32[3,2,128,256]{3,2,1,0:T(8,128)}, u32[]{:S(2)}, u32[]{:S(2)}) collective-permute-start(f32[3,2,128,256]{3,2,1,0:T(8,128)} %get-tuple-element.26), channel_id=1, source_target_pairs={{0,4},{1,5},{2,6},{3,7},{4,0},{5,1},{6,2},{7,3},{8,12},{9,13},{10,... | collective-permute-start | bytes 2359304 | tf_op jit(solution)/shard_map/ppermute | solution.py:288
  14.9 44.0 %copy-start.8 = (bf16[3,256,128]{2,1,0:T(8,128)(2,1)S(1)}, bf16[3,256,128]{2,1,0:T(8,128)(2,1)}, u32[]{:S(2)}) copy-start(bf16[3,256,128]{2,1,0:T(8,128)(2,1)} %get-tuple-element.30.gates_ref) | copy-start | bytes 589828
  14.9 21.0 %all-to-all-start = ((f32[16,3,16,128]{3,2,1,0:T(8,128)}), f32[16,3,16,128]{3,2,1,0:T(8,128)S(1)}, u32[]{:S(2)}, u32[]{:S(2)}) async-start(f32[16,3,16,128]{3,2,1,0:T(8,128)} %get-tuple-element.23), calls=%async_computation | async-start | bytes 786432 | tf_op jit(solution)/shard_map/all_to_all | solution.py:331
  27.0 0.9 copy-start.2
  30.8 1.1 copy-start.3
  31.9 1.0 copy-start.5
  34.4 0.7 copy-start.10
  35.1 0.7 copy-start.11
  38.4 0.7 copy-start.7
  39.1 0.7 copy-start.9
  39.8 19.0 %all-to-all-start.1 = ((f32[16,2,16,128]{3,2,1,0:T(8,128)}), f32[16,2,16,128]{3,2,1,0:T(8,128)S(1)}, u32[]{:S(2)}, u32[]{:S(2)}) async-start(f32[16,2,16,128]{3,2,1,0:T(8,128)} %copy-done.7), calls=%async_computation.1 | async-start | bytes 524288 | tf_op jit(solution)/shard_map/all_to_all | solution.py:341
  45.7 13.0 %collective-permute-start.2 = (f32[1,2,128,256]{3,2,1,0:T(8,128)}, f32[1,2,128,256]{3,2,1,0:T(8,128)S(1)}, u32[]{:S(2)}, u32[]{:S(2)}) collective-permute-start(f32[1,2,128,256]{3,2,1,0:T(8,128)} %copy-done.11), channel_id=1, source_target_pairs={{0,4},{1,5},{2,6},{3,7},{4,0},{5,1},{6,2},{7,3},{8,12},{9,13},{10,... | collective-permute-start | bytes 786440 | tf_op jit(solution)/shard_map/ppermute | solution.py:288
  47.6 11.0 %collective-permute-start.3 = (f32[1,2,128,256]{3,2,1,0:T(8,128)}, f32[1,2,128,256]{3,2,1,0:T(8,128)S(1)}, u32[]{:S(2)}, u32[]{:S(2)}) collective-permute-start(f32[1,2,128,256]{3,2,1,0:T(8,128)} %copy-done.10), channel_id=1, source_target_pairs={{0,2},{1,3},{2,0},{3,1},{4,6},{5,7},{6,4},{7,5},{8,10},{9,11},{10,... | collective-permute-start | bytes 786440 | tf_op jit(solution)/shard_map/ppermute | solution.py:288
  59.0 5.6 %collective-permute-start.4 = (f32[128,256]{1,0:T(8,128)S(1)}, f32[128,256]{1,0:T(8,128)S(1)}, u32[]{:S(2)}, u32[]{:S(2)}) collective-permute-start(f32[128,256]{1,0:T(8,128)S(1)} %get-tuple-element.36.refs_0_), channel_id=1, source_target_pairs={{0,2},{1,3},{2,0},{3,1},{4,6},{5,7},{6,4},{7,5},{8,10},{9,11},{10,... | collective-permute-start | bytes 393224 | tf_op jit(solution)/shard_map/ppermute | solution.py:288
  60.5 6.2 %collective-permute-start.5 = (f32[128,256]{1,0:T(8,128)S(1)}, f32[128,256]{1,0:T(8,128)S(1)}, u32[]{:S(2)}, u32[]{:S(2)}) collective-permute-start(f32[128,256]{1,0:T(8,128)S(1)} %get-tuple-element.36.refs_0_), channel_id=1, source_target_pairs={{0,4},{1,5},{2,6},{3,7},{4,0},{5,1},{6,2},{7,3},{8,12},{9,13},{10,... | collective-permute-start | bytes 393224 | tf_op jit(solution)/shard_map/ppermute | solution.py:288
  61.1 7.0 %collective-permute-start.6 = (f32[128,256]{1,0:T(8,128)S(1)}, f32[128,256]{1,0:T(8,128)S(1)}, u32[]{:S(2)}, u32[]{:S(2)}) collective-permute-start(f32[128,256]{1,0:T(8,128)S(1)} %get-tuple-element.36.refs_0_), channel_id=1, source_target_pairs={{0,6},{1,7},{2,4},{3,5},{4,2},{5,3},{6,0},{7,1},{8,14},{9,15},{10,... | collective-permute-start | bytes 393224 | tf_op jit(solution)/shard_map/ppermute | solution.py:288
  68.4 3.6 %collective-permute-start.7 = (f32[512,256]{1,0:T(8,128)S(1)}, f32[512,256]{1,0:T(8,128)S(1)}, u32[]{:S(2)}, u32[]{:S(2)}) collective-permute-start(f32[512,256]{1,0:T(8,128)S(1)} %shard_map.91), channel_id=1, source_target_pairs={{0,1},{1,0},{2,3},{3,2},{4,5},{5,4},{6,7},{7,6},{8,9},{9,8},{10,11... | collective-permute-start | bytes 1572872 | tf_op jit(solution)/shard_map/ppermute | solution.py:288
  68.5 25.1 %collective-permute-start.10 = (f32[128,512]{1,0:T(8,128)S(1)}, f32[128,512]{1,0:T(8,128)S(1)}, u32[]{:S(2)}, u32[]{:S(2)}) collective-permute-start(f32[128,512]{1,0:T(8,128)S(1)} %get-tuple-element.39.refs_0_), channel_id=1, source_target_pairs={{0,4},{1,5},{2,6},{3,7},{4,0},{5,1},{6,2},{7,3},{8,12},{9,13},{10,... | collective-permute-start | bytes 786440 | tf_op jit(solution)/shard_map/ppermute | solution.py:288
  69.2 24.3 %collective-permute-start.11 = (f32[128,512]{1,0:T(8,128)S(1)}, f32[128,512]{1,0:T(8,128)S(1)}, u32[]{:S(2)}, u32[]{:S(2)}) collective-permute-start(f32[128,512]{1,0:T(8,128)S(1)} %get-tuple-element.39.refs_0_), channel_id=1, source_target_pairs={{0,6},{1,7},{2,4},{3,5},{4,2},{5,3},{6,0},{7,1},{8,14},{9,15},{10,... | collective-permute-start | bytes 786440 | tf_op jit(solution)/shard_map/ppermute | solution.py:288
  71.5 22.1 %collective-permute-start.9 = (f32[128,512]{1,0:T(8,128)S(1)}, f32[128,512]{1,0:T(8,128)S(1)}, u32[]{:S(2)}, u32[]{:S(2)}) collective-permute-start(f32[128,512]{1,0:T(8,128)S(1)} %get-tuple-element.39.refs_0_), channel_id=1, source_target_pairs={{0,2},{1,3},{2,0},{3,1},{4,6},{5,7},{6,4},{7,5},{8,10},{9,11},{10,... | collective-permute-start | bytes 786440 | tf_op jit(solution)/shard_map/ppermute | solution.py:288
  72.3 21.2 %collective-permute-start.8 = (f32[256,256]{1,0:T(8,128)S(1)}, f32[256,256]{1,0:T(8,128)S(1)}, u32[]{:S(2)}, u32[]{:S(2)}) collective-permute-start(f32[256,256]{1,0:T(8,128)S(1)} %get-tuple-element.38), channel_id=1, source_target_pairs={{0,8},{1,9},{2,10},{3,11},{4,12},{5,13},{6,14},{7,15},{8,0},{9,1},... | collective-permute-start | bytes 786440 | tf_op jit(solution)/shard_map/ppermute | solution.py:288
  94.0 2.7 %collective-permute-start.12 = (f32[512,512]{1,0:T(8,128)S(1)}, f32[512,512]{1,0:T(8,128)S(1)}, u32[]{:S(2)}, u32[]{:S(2)}) collective-permute-start(f32[512,512]{1,0:T(8,128)S(1)} %shard_map.93), channel_id=1, source_target_pairs={{0,1},{1,0},{2,3},{3,2},{4,5},{5,4},{6,7},{7,6},{8,9},{9,8},{10,11... | collective-permute-start | bytes 3145736 | tf_op jit(solution)/shard_map/ppermute | solution.py:288
  97.2 25.5 %collective-permute-start.13 = (f32[256,512]{1,0:T(8,128)S(1)}, f32[256,512]{1,0:T(8,128)S(1)}, u32[]{:S(2)}, u32[]{:S(2)}) collective-permute-start(f32[256,512]{1,0:T(8,128)S(1)} %get-tuple-element.42), channel_id=1, source_target_pairs={{0,8},{1,9},{2,10},{3,11},{4,12},{5,13},{6,14},{7,15},{8,0},{9,1},... | collective-permute-start | bytes 1572872 | tf_op jit(solution)/shard_map/ppermute | solution.py:288

commit v3 on v1

--- a/solution.py
+++ b/solution.py
@@ -9,7 +9,7 @@
 from jax.experimental.pallas import tpu as pltpu
 from jax.sharding import PartitionSpec as P
 
-VMEM_LIMIT = 28 * 1024 * 1024
+VMEM_LIMIT = 12 * 1024 * 1024
 SIDE = 4
 
 

time: 121 us -> 121 us (level)
  no operation moved by 1% of the time
where the time goes in v3:
time: 121 us
  waiting for transfers between devices  69.7 us (58%)
  starting transfers between devices  25.8 us (21%)
  Pallas kernels  11.8 us (10%)
  local copies, waits for them, and re-layouts  9.61 us (8%)
  matrix products  3.11 us (3%)
    ppermute x14, waiting for transfers between devices, exchange(): return lax.ppermute(value, 'seq', [(i, i ^ flip) for i in range(blocks)])  66.9 us
    ppermute x14, starting transfers between devices, exchange(): return lax.ppermute(value, 'seq', [(i, i ^ flip) for i in range(blocks)])  18.3 us
    unnamed x24, local copies, waits for them, and re-layouts  9.61 us
    all_to_all x1, starting transfers between devices, per_device(): lax.all_to_all(signals, 'seq', split_axis=0, concat_axis=0, tiled=True)  3.97 us
    all_to_all x1, starting transfers between devices, per_device(): lax.all_to_all(results, 'seq', split_axis=0, concat_axis=0, tiled=True)  3.55 us
    pallas_call x1, Pallas kernels, per_device(): pl.pallas_call(functools.partial(conv_kernel, places), in_specs=[inside]...  3.33 us
    dot_general x1, matrix products, per_device(): lax.dot_general(grad_proj, in_weight, (((1,), (1,)), ((), ())), preferred...  3.11 us
    all_to_all x1, waiting for transfers between devices, per_device(): lax.all_to_all(signals, 'seq', split_axis=0, concat_axis=0, tiled=True)  2.85 us
  transfers between devices with their start and end apart: 16, of which 11 were waited for; matrix products, arithmetic and copies ran while one was open for 3% of the time, Pallas kernels for 3%

profile of v3, /device:TPU:0, one launch (start us, length us, event | category | flops | bytes accessed | tf_op | source)
XLA Modules:
  0.0 120.8 jit_solution(15733269418959200782)
XLA Ops:
  0.6 1.2 %copy-done.1 = bf16[128,4096]{1,0:T(8,128)(2,1)S(1)} copy-done((bf16[128,4096]{1,0:T(8,128)(2,1)S(1)}, bf16[128,4096]{1,0:T(8,128)(2,1)}, u32[]{:S(2)}) %copy-start.1) | copy-done | bytes 1048600
  1.9 2.1 %shard_map.86 = (f32[2,2,128,256]{3,2,1,0:T(8,128)S(1)}, f32[3,2,128,256]{3,2,1,0:T(8,128)}, f32[3,2,128,256]{3,2,1,0:T(8,128)}) custom-call(bf16[128,4096]{1,0:T(8,128)(2,1)S(1)} %copy-done.1), custom_call_target="tpu_custom_call" | custom-call | tf_op jit(solution)/shard_map/pallas_call | solution.py:283
  4.0 3.0 %collective-permute-start = (f32[3,2,128,256]{3,2,1,0:T(8,128)}, f32[3,2,128,256]{3,2,1,0:T(8,128)S(1)}, u32[]{:S(2)}, u32[]{:S(2)}) collective-permute-start(f32[3,2,128,256]{3,2,1,0:T(8,128)} %get-tuple-element.24), channel_id=1, source_target_pairs={{0,2},{1,3},{2,0},{3,1},{4,6},{5,7},{6,4},{7,5},{8,10},{9,11},{10,... | collective-permute-start | bytes 2359304 | tf_op jit(solution)/shard_map/ppermute | solution.py:279
  6.9 1.6 %collective-permute-start.1 = (f32[3,2,128,256]{3,2,1,0:T(8,128)}, f32[3,2,128,256]{3,2,1,0:T(8,128)S(1)}, u32[]{:S(2)}, u32[]{:S(2)}) collective-permute-start(f32[3,2,128,256]{3,2,1,0:T(8,128)} %get-tuple-element.25), channel_id=1, source_target_pairs={{0,4},{1,5},{2,6},{3,7},{4,0},{5,1},{6,2},{7,3},{8,12},{9,13},{10,... | collective-permute-start | bytes 2359304 | tf_op jit(solution)/shard_map/ppermute | solution.py:279
  8.5 2.8 %copy-done = bf16[4096,768]{1,0:T(8,128)(2,1)S(1)} copy-done((bf16[4096,768]{1,0:T(8,128)(2,1)S(1)}, bf16[4096,768]{1,0:T(8,128)(2,1)}, u32[]{:S(2)}) %copy-start) | copy-done | bytes 6291480
  11.3 0.9 copy-done.6
  12.2 0.8 copy-done.7
  13.0 2.7 %shard_map.85 = (f32[16,3,16,128]{3,2,1,0:T(8,128)}, bf16[3,256,128]{2,1,0:T(8,128)(2,1)S(1)}) custom-call(bf16[128,4096]{1,0:T(8,128)(2,1)S(1)} %copy-done.1, bf16[4096,768]{1,0:T(8,128)(2,1)S(1)} %copy-done, f32[128,256]{1,0:T(8,128)S(1)} %copy-done.6, bf16[128,256]{1,0:T(8,128)(2,1)S(1)} %copy-done.7), custom_call_target="tpu_custom_call" | custom-call | flops 805306368 | bytes 7340032 | tf_op jit(solution)/shard_map/pallas_call | solution.py:299
  15.7 4.0 %all-to-all-start = ((f32[16,3,16,128]{3,2,1,0:T(8,128)}), f32[16,3,16,128]{3,2,1,0:T(8,128)S(1)}, u32[]{:S(2)}, u32[]{:S(2)}) async-start(f32[16,3,16,128]{3,2,1,0:T(8,128)} %get-tuple-element.22), calls=%async_computation | async-start | bytes 786432 | tf_op jit(solution)/shard_map/all_to_all | solution.py:322
  19.7 6.1 %collective-permute-done.y_ref = f32[3,2,128,256]{3,2,1,0:T(8,128)S(1)} collective-permute-done((f32[3,2,128,256]{3,2,1,0:T(8,128)}, f32[3,2,128,256]{3,2,1,0:T(8,128)S(1)}, u32[]{:S(2)}, u32[]{:S(2)}) %collective-permute-start) | collective-permute-done | bytes 786464 | tf_op jit(solution)/shard_map/ppermute | solution.py:279
  25.8 4.1 %collective-permute-done.1.z_ref = f32[3,2,128,256]{3,2,1,0:T(8,128)S(1)} collective-permute-done((f32[3,2,128,256]{3,2,1,0:T(8,128)}, f32[3,2,128,256]{3,2,1,0:T(8,128)S(1)}, u32[]{:S(2)}, u32[]{:S(2)}) %collective-permute-start.1) | collective-permute-done | bytes 786464 | tf_op jit(solution)/shard_map/ppermute | solution.py:279
  29.9 0.3 shard_map.87
  30.2 0.7 copy-done.8
  30.9 0.7 copy-done.9
  31.6 2.8 %all-to-all-done.x_ref = f32[16,3,16,128]{3,2,1,0:T(8,128)S(1)} async-done(((f32[16,3,16,128]{3,2,1,0:T(8,128)}), f32[16,3,16,128]{3,2,1,0:T(8,128)S(1)}, u32[]{:S(2)}, u32[]{:S(2)}) %all-to-all-start) | async-done | bytes 393248 | tf_op jit(solution)/shard_map/all_to_all | solution.py:322
  34.5 1.5 %copy-done.2 = bf16[3648,256]{1,0:T(8,128)(2,1)S(1)} copy-done((bf16[3648,256]{1,0:T(8,128)(2,1)S(1)}, bf16[3648,256]{1,0:T(8,128)(2,1)}, u32[]{:S(2)}) %copy-start.2) | copy-done | bytes 1867800
  36.0 3.3 %shard_map.88 = f32[16,3,16,128]{3,2,1,0:T(8,128)} custom-call(f32[16,3,16,128]{3,2,1,0:T(8,128)S(1)} %all-to-all-done.x_ref, bf16[3648,256]{1,0:T(8,128)(2,1)S(1)} %copy-done.2, f32[272,256]{1,0:T(8,128)S(1)} %copy-done.3, bf16[512,384]{1,0:T(8,128)(2,1)S(1)} %get-tuple-element.26.refs_0_.x_ref, bf16[512,384]{1,0:T(8,128)(2,1)S(1)} %get-tuple-element.27.refs_1_.x_ref), custom_call_target="tpu_custom_call" | custom-call | tf_op jit(solution)/shard_map/pallas_call | solution.py:325
  39.3 3.6 %all-to-all-start.1 = ((f32[16,3,16,128]{3,2,1,0:T(8,128)}), f32[16,3,16,128]{3,2,1,0:T(8,128)S(1)}, u32[]{:S(2)}, u32[]{:S(2)}) async-start(f32[16,3,16,128]{3,2,1,0:T(8,128)} %shard_map.88), calls=%async_computation.1 | async-start | bytes 786432 | tf_op jit(solution)/shard_map/all_to_all | solution.py:332
  42.9 1.8 %collective-permute-start.2 = (f32[1,2,128,256]{3,2,1,0:T(8,128)}, f32[1,2,128,256]{3,2,1,0:T(8,128)S(1)}, u32[]{:S(2)}, u32[]{:S(2)}) collective-permute-start(f32[1,2,128,256]{3,2,1,0:T(8,128)} %copy-done.9), channel_id=1, source_target_pairs={{0,4},{1,5},{2,6},{3,7},{4,0},{5,1},{6,2},{7,3},{8,12},{9,13},{10,... | collective-permute-start | bytes 786440 | tf_op jit(solution)/shard_map/ppermute | solution.py:279
  44.7 1.5 %collective-permute-start.3 = (f32[1,2,128,256]{3,2,1,0:T(8,128)}, f32[1,2,128,256]{3,2,1,0:T(8,128)S(1)}, u32[]{:S(2)}, u32[]{:S(2)}) collective-permute-start(f32[1,2,128,256]{3,2,1,0:T(8,128)} %copy-done.8), channel_id=1, source_target_pairs={{0,2},{1,3},{2,0},{3,1},{4,6},{5,7},{6,4},{7,5},{8,10},{9,11},{10,... | collective-permute-start | bytes 786440 | tf_op jit(solution)/shard_map/ppermute | solution.py:279
  46.2 11.7 %collective-permute-done.2.corner_own_ref = f32[1,2,128,256]{3,2,1,0:T(8,128)S(1)} collective-permute-done((f32[1,2,128,256]{3,2,1,0:T(8,128)}, f32[1,2,128,256]{3,2,1,0:T(8,128)S(1)}, u32[]{:S(2)}, u32[]{:S(2)}) %collective-permute-start.2) | collective-permute-done | bytes 262176 | tf_op jit(solution)/shard_map/ppermute | solution.py:279
  57.8 0.0 collective-permute-done.3.corner_other_ref
  57.8 0.1 shard_map.89
  58.0 0.9 copy-done.5
  58.9 0.8 shard_map.90
  59.7 1.5 %collective-permute-start.4 = (f32[128,256]{1,0:T(8,128)S(1)}, f32[128,256]{1,0:T(8,128)S(1)}, u32[]{:S(2)}, u32[]{:S(2)}) collective-permute-start(f32[128,256]{1,0:T(8,128)S(1)} %get-tuple-element.34.refs_0_), channel_id=1, source_target_pairs={{0,2},{1,3},{2,0},{3,1},{4,6},{5,7},{6,4},{7,5},{8,10},{9,11},{10,... | collective-permute-start | bytes 393224 | tf_op jit(solution)/shard_map/ppermute | solution.py:279
  61.2 0.5 collective-permute-start.5
  61.8 1.5 %collective-permute-start.6 = (f32[128,256]{1,0:T(8,128)S(1)}, f32[128,256]{1,0:T(8,128)S(1)}, u32[]{:S(2)}, u32[]{:S(2)}) collective-permute-start(f32[128,256]{1,0:T(8,128)S(1)} %get-tuple-element.34.refs_0_), channel_id=1, source_target_pairs={{0,6},{1,7},{2,4},{3,5},{4,2},{5,3},{6,0},{7,1},{8,14},{9,15},{10,... | collective-permute-start | bytes 393224 | tf_op jit(solution)/shard_map/ppermute | solution.py:279
  63.2 2.0 %collective-permute-done.4.refs_1_ = f32[128,256]{1,0:T(8,128)S(1)} collective-permute-done((f32[128,256]{1,0:T(8,128)S(1)}, f32[128,256]{1,0:T(8,128)S(1)}, u32[]{:S(2)}, u32[]{:S(2)}) %collective-permute-start.4) | collective-permute-done | bytes 131104 | tf_op jit(solution)/shard_map/ppermute | solution.py:279
  65.3 2.1 %collective-permute-done.5.refs_2_ = f32[128,256]{1,0:T(8,128)S(1)} collective-permute-done((f32[128,256]{1,0:T(8,128)S(1)}, f32[128,256]{1,0:T(8,128)S(1)}, u32[]{:S(2)}, u32[]{:S(2)}) %collective-permute-start.5) | collective-permute-done | bytes 131104 | tf_op jit(solution)/shard_map/ppermute | solution.py:279
  67.4 1.4 %collective-permute-done.6.refs_3_ = f32[128,256]{1,0:T(8,128)S(1)} collective-permute-done((f32[128,256]{1,0:T(8,128)S(1)}, f32[128,256]{1,0:T(8,128)S(1)}, u32[]{:S(2)}, u32[]{:S(2)}) %collective-permute-start.6) | collective-permute-done | bytes 131104 | tf_op jit(solution)/shard_map/ppermute | solution.py:279
  68.8 0.3 shard_map.91
  69.1 0.1 collective-permute-start.7
  69.2 0.7 collective-permute-start.10
  69.9 2.3 %collective-permute-start.11 = (f32[128,512]{1,0:T(8,128)S(1)}, f32[128,512]{1,0:T(8,128)S(1)}, u32[]{:S(2)}, u32[]{:S(2)}) collective-permute-start(f32[128,512]{1,0:T(8,128)S(1)} %get-tuple-element.37.refs_0_), channel_id=1, source_target_pairs={{0,6},{1,7},{2,4},{3,5},{4,2},{5,3},{6,0},{7,1},{8,14},{9,15},{10,... | collective-permute-start | bytes 786440 | tf_op jit(solution)/shard_map/ppermute | solution.py:279
  72.2 0.6 collective-permute-start.9
  72.7 0.3 shard_map.92
  73.0 2.5 %collective-permute-start.8 = (f32[256,256]{1,0:T(8,128)S(1)}, f32[256,256]{1,0:T(8,128)S(1)}, u32[]{:S(2)}, u32[]{:S(2)}) collective-permute-start(f32[256,256]{1,0:T(8,128)S(1)} %get-tuple-element.36), channel_id=1, source_target_pairs={{0,8},{1,9},{2,10},{3,11},{4,12},{5,13},{6,14},{7,15},{8,0},{9,1},... | collective-permute-start | bytes 786440 | tf_op jit(solution)/shard_map/ppermute | solution.py:279
  75.6 8.4 %collective-permute-done.10.refs_2_ = f32[128,512]{1,0:T(8,128)S(1)} collective-permute-done((f32[128,512]{1,0:T(8,128)S(1)}, f32[128,512]{1,0:T(8,128)S(1)}, u32[]{:S(2)}, u32[]{:S(2)}) %collective-permute-start.10) | collective-permute-done | bytes 262176 | tf_op jit(solution)/shard_map/ppermute | solution.py:279
  84.0 6.1 %collective-permute-done.11.refs_3_ = f32[128,512]{1,0:T(8,128)S(1)} collective-permute-done((f32[128,512]{1,0:T(8,128)S(1)}, f32[128,512]{1,0:T(8,128)S(1)}, u32[]{:S(2)}, u32[]{:S(2)}) %collective-permute-start.11) | collective-permute-done | bytes 262176 | tf_op jit(solution)/shard_map/ppermute | solution.py:279
  90.0 0.4 shard_map.93
  90.5 0.1 collective-permute-start.12
  90.6 2.6 %collective-permute-done.12.refs_4_ = f32[512,512]{1,0:T(8,128)S(1)} collective-permute-done((f32[512,512]{1,0:T(8,128)S(1)}, f32[512,512]{1,0:T(8,128)S(1)}, u32[]{:S(2)}, u32[]{:S(2)}) %collective-permute-start.12) | collective-permute-done | bytes 1048608 | tf_op jit(solution)/shard_map/ppermute | solution.py:279
  93.2 0.4 shard_map.94
  93.7 0.7 collective-permute-start.13
  94.4 3.1 %convolution_convert_fusion = bf16[128,4096]{1,0:T(8,128)(2,1)} fusion(bf16[128,768]{1,0:T(8,128)(2,1)S(1)} %get-tuple-element.33, bf16[4096,768]{1,0:T(8,128)(2,1)S(1)} %bitcast.3), kind=kOutput, calls=%fused_computation | convolution fusion | flops 805830656 | bytes 7536640 | tf_op jit(solution)/shard_map/dot_general | solution.py:353
  97.5 22.3 %collective-permute-done.13.refs_3_ = f32[256,512]{1,0:T(8,128)S(1)} collective-permute-done((f32[256,512]{1,0:T(8,128)S(1)}, f32[256,512]{1,0:T(8,128)S(1)}, u32[]{:S(2)}, u32[]{:S(2)}) %collective-permute-start.13) | collective-permute-done | bytes 524320 | tf_op jit(solution)/shard_map/ppermute | solution.py:279
  119.8 1.0 shard_map.95
  (21 shorter events, 0.0 us)
Async XLA Ops:
  0.6 1.2 %copy-start.1 = (bf16[128,4096]{1,0:T(8,128)(2,1)S(1)}, bf16[128,4096]{1,0:T(8,128)(2,1)}, u32[]{:S(2)}) copy-start(bf16[128,4096]{1,0:T(8,128)(2,1)} %x_ref.3) | copy-start | bytes 3145732
  1.9 32.6 %copy-start.3 = (f32[272,256]{1,0:T(8,128)S(1)}, f32[272,256]{1,0:T(8,128)}, u32[]{:S(2)}) copy-start(f32[272,256]{1,0:T(8,128)} %constant.5.clone.turn_ref) | copy-start | bytes 835588
  4.0 21.8 %collective-permute-start = (f32[3,2,128,256]{3,2,1,0:T(8,128)}, f32[3,2,128,256]{3,2,1,0:T(8,128)S(1)}, u32[]{:S(2)}, u32[]{:S(2)}) collective-permute-start(f32[3,2,128,256]{3,2,1,0:T(8,128)} %get-tuple-element.24), channel_id=1, source_target_pairs={{0,2},{1,3},{2,0},{3,1},{4,6},{5,7},{6,4},{7,5},{8,10},{9,11},{10,... | collective-permute-start | bytes 2359304 | tf_op jit(solution)/shard_map/ppermute | solution.py:279
  6.9 23.0 %collective-permute-start.1 = (f32[3,2,128,256]{3,2,1,0:T(8,128)}, f32[3,2,128,256]{3,2,1,0:T(8,128)S(1)}, u32[]{:S(2)}, u32[]{:S(2)}) collective-permute-start(f32[3,2,128,256]{3,2,1,0:T(8,128)} %get-tuple-element.25), channel_id=1, source_target_pairs={{0,4},{1,5},{2,6},{3,7},{4,0},{5,1},{6,2},{7,3},{8,12},{9,13},{10,... | collective-permute-start | bytes 2359304 | tf_op jit(solution)/shard_map/ppermute | solution.py:279
  8.5 2.8 %copy-start = (bf16[4096,768]{1,0:T(8,128)(2,1)S(1)}, bf16[4096,768]{1,0:T(8,128)(2,1)}, u32[]{:S(2)}) copy-start(bf16[4096,768]{1,0:T(8,128)(2,1)} %w_ref.1) | copy-start | bytes 18874372
  11.3 0.9 copy-start.6
  12.2 0.8 copy-start.7
  15.7 14.2 %copy-start.4 = (bf16[3,256,128]{2,1,0:T(8,128)(2,1)}, bf16[3,256,128]{2,1,0:T(8,128)(2,1)S(1)}, u32[]{:S(2)}) copy-start(bf16[3,256,128]{2,1,0:T(8,128)(2,1)S(1)} %get-tuple-element.28.gates_ref) | copy-start | bytes 589828
  15.7 18.7 %all-to-all-start = ((f32[16,3,16,128]{3,2,1,0:T(8,128)}), f32[16,3,16,128]{3,2,1,0:T(8,128)S(1)}, u32[]{:S(2)}, u32[]{:S(2)}) async-start(f32[16,3,16,128]{3,2,1,0:T(8,128)} %get-tuple-element.22), calls=%async_computation | async-start | bytes 786432 | tf_op jit(solution)/shard_map/all_to_all | solution.py:322
  30.2 0.7 copy-start.8
  30.9 0.7 copy-start.9
  34.5 1.5 %copy-start.2 = (bf16[3648,256]{1,0:T(8,128)(2,1)S(1)}, bf16[3648,256]{1,0:T(8,128)(2,1)}, u32[]{:S(2)}) copy-start(bf16[3648,256]{1,0:T(8,128)(2,1)} %constant.4.clone.table_ref) | copy-start | bytes 5603332
  36.0 58.4 %slice-start = ((s8[6291456]{0:T(1024)(128)(4,1)}), s8[2097152]{0:T(1024)(128)(4,1)S(1)}, s32[]{:S(2)}) async-start(s8[6291456]{0:T(1024)(128)(4,1)} %bitcast.2), calls=%async_computation.2 | async-start | bytes 4194304
  39.3 18.7 %all-to-all-start.1 = ((f32[16,3,16,128]{3,2,1,0:T(8,128)}), f32[16,3,16,128]{3,2,1,0:T(8,128)S(1)}, u32[]{:S(2)}, u32[]{:S(2)}) async-start(f32[16,3,16,128]{3,2,1,0:T(8,128)} %shard_map.88), calls=%async_computation.1 | async-start | bytes 786432 | tf_op jit(solution)/shard_map/all_to_all | solution.py:332
  42.9 15.0 %collective-permute-start.2 = (f32[1,2,128,256]{3,2,1,0:T(8,128)}, f32[1,2,128,256]{3,2,1,0:T(8,128)S(1)}, u32[]{:S(2)}, u32[]{:S(2)}) collective-permute-start(f32[1,2,128,256]{3,2,1,0:T(8,128)} %copy-done.9), channel_id=1, source_target_pairs={{0,4},{1,5},{2,6},{3,7},{4,0},{5,1},{6,2},{7,3},{8,12},{9,13},{10,... | collective-permute-start | bytes 786440 | tf_op jit(solution)/shard_map/ppermute | solution.py:279
  44.7 13.1 %collective-permute-start.3 = (f32[1,2,128,256]{3,2,1,0:T(8,128)}, f32[1,2,128,256]{3,2,1,0:T(8,128)S(1)}, u32[]{:S(2)}, u32[]{:S(2)}) collective-permute-start(f32[1,2,128,256]{3,2,1,0:T(8,128)} %copy-done.8), channel_id=1, source_target_pairs={{0,2},{1,3},{2,0},{3,1},{4,6},{5,7},{6,4},{7,5},{8,10},{9,11},{10,... | collective-permute-start | bytes 786440 | tf_op jit(solution)/shard_map/ppermute | solution.py:279
  58.0 0.9 copy-start.5
  59.7 34.6 %slice-start.1 = ((s8[6291456]{0:T(1024)(128)(4,1)}), s8[4194304]{0:T(1024)(128)(4,1)S(1)}, s32[]{:S(2)}) async-start(s8[6291456]{0:T(1024)(128)(4,1)} %bitcast.2), calls=%async_computation.3 | async-start | bytes 8388608
  59.7 5.5 %collective-permute-start.4 = (f32[128,256]{1,0:T(8,128)S(1)}, f32[128,256]{1,0:T(8,128)S(1)}, u32[]{:S(2)}, u32[]{:S(2)}) collective-permute-start(f32[128,256]{1,0:T(8,128)S(1)} %get-tuple-element.34.refs_0_), channel_id=1, source_target_pairs={{0,2},{1,3},{2,0},{3,1},{4,6},{5,7},{6,4},{7,5},{8,10},{9,11},{10,... | collective-permute-start | bytes 393224 | tf_op jit(solution)/shard_map/ppermute | solution.py:279
  61.2 6.2 %collective-permute-start.5 = (f32[128,256]{1,0:T(8,128)S(1)}, f32[128,256]{1,0:T(8,128)S(1)}, u32[]{:S(2)}, u32[]{:S(2)}) collective-permute-start(f32[128,256]{1,0:T(8,128)S(1)} %get-tuple-element.34.refs_0_), channel_id=1, source_target_pairs={{0,4},{1,5},{2,6},{3,7},{4,0},{5,1},{6,2},{7,3},{8,12},{9,13},{10,... | collective-permute-start | bytes 393224 | tf_op jit(solution)/shard_map/ppermute | solution.py:279
  61.8 7.0 %collective-permute-start.6 = (f32[128,256]{1,0:T(8,128)S(1)}, f32[128,256]{1,0:T(8,128)S(1)}, u32[]{:S(2)}, u32[]{:S(2)}) collective-permute-start(f32[128,256]{1,0:T(8,128)S(1)} %get-tuple-element.34.refs_0_), channel_id=1, source_target_pairs={{0,6},{1,7},{2,4},{3,5},{4,2},{5,3},{6,0},{7,1},{8,14},{9,15},{10,... | collective-permute-start | bytes 393224 | tf_op jit(solution)/shard_map/ppermute | solution.py:279
  69.1 3.6 %collective-permute-start.7 = (f32[512,256]{1,0:T(8,128)S(1)}, f32[512,256]{1,0:T(8,128)S(1)}, u32[]{:S(2)}, u32[]{:S(2)}) collective-permute-start(f32[512,256]{1,0:T(8,128)S(1)} %shard_map.91), channel_id=1, source_target_pairs={{0,1},{1,0},{2,3},{3,2},{4,5},{5,4},{6,7},{7,6},{8,9},{9,8},{10,11... | collective-permute-start | bytes 1572872 | tf_op jit(solution)/shard_map/ppermute | solution.py:279
  69.2 14.8 %collective-permute-start.10 = (f32[128,512]{1,0:T(8,128)S(1)}, f32[128,512]{1,0:T(8,128)S(1)}, u32[]{:S(2)}, u32[]{:S(2)}) collective-permute-start(f32[128,512]{1,0:T(8,128)S(1)} %get-tuple-element.37.refs_0_), channel_id=1, source_target_pairs={{0,4},{1,5},{2,6},{3,7},{4,0},{5,1},{6,2},{7,3},{8,12},{9,13},{10,... | collective-permute-start | bytes 786440 | tf_op jit(solution)/shard_map/ppermute | solution.py:279
  69.9 20.2 %collective-permute-start.11 = (f32[128,512]{1,0:T(8,128)S(1)}, f32[128,512]{1,0:T(8,128)S(1)}, u32[]{:S(2)}, u32[]{:S(2)}) collective-permute-start(f32[128,512]{1,0:T(8,128)S(1)} %get-tuple-element.37.refs_0_), channel_id=1, source_target_pairs={{0,6},{1,7},{2,4},{3,5},{4,2},{5,3},{6,0},{7,1},{8,14},{9,15},{10,... | collective-permute-start | bytes 786440 | tf_op jit(solution)/shard_map/ppermute | solution.py:279
  72.2 17.9 %collective-permute-start.9 = (f32[128,512]{1,0:T(8,128)S(1)}, f32[128,512]{1,0:T(8,128)S(1)}, u32[]{:S(2)}, u32[]{:S(2)}) collective-permute-start(f32[128,512]{1,0:T(8,128)S(1)} %get-tuple-element.37.refs_0_), channel_id=1, source_target_pairs={{0,2},{1,3},{2,0},{3,1},{4,6},{5,7},{6,4},{7,5},{8,10},{9,11},{10,... | collective-permute-start | bytes 786440 | tf_op jit(solution)/shard_map/ppermute | solution.py:279
  73.0 17.0 %collective-permute-start.8 = (f32[256,256]{1,0:T(8,128)S(1)}, f32[256,256]{1,0:T(8,128)S(1)}, u32[]{:S(2)}, u32[]{:S(2)}) collective-permute-start(f32[256,256]{1,0:T(8,128)S(1)} %get-tuple-element.36), channel_id=1, source_target_pairs={{0,8},{1,9},{2,10},{3,11},{4,12},{5,13},{6,14},{7,15},{8,0},{9,1},... | collective-permute-start | bytes 786440 | tf_op jit(solution)/shard_map/ppermute | solution.py:279
  90.5 2.7 %collective-permute-start.12 = (f32[512,512]{1,0:T(8,128)S(1)}, f32[512,512]{1,0:T(8,128)S(1)}, u32[]{:S(2)}, u32[]{:S(2)}) collective-permute-start(f32[512,512]{1,0:T(8,128)S(1)} %shard_map.93), channel_id=1, source_target_pairs={{0,1},{1,0},{2,3},{3,2},{4,5},{5,4},{6,7},{7,6},{8,9},{9,8},{10,11... | collective-permute-start | bytes 3145736 | tf_op jit(solution)/shard_map/ppermute | solution.py:279
  93.7 26.2 %collective-permute-start.13 = (f32[256,512]{1,0:T(8,128)S(1)}, f32[256,512]{1,0:T(8,128)S(1)}, u32[]{:S(2)}, u32[]{:S(2)}) collective-permute-start(f32[256,512]{1,0:T(8,128)S(1)} %get-tuple-element.39), channel_id=1, source_target_pairs={{0,8},{1,9},{2,10},{3,11},{4,12},{5,13},{6,14},{7,15},{8,0},{9,1},... | collective-permute-start | bytes 1572872 | tf_op jit(solution)/shard_map/ppermute | solution.py:279

commit v4 on v3

--- a/solution.py
+++ b/solution.py
@@ -209,7 +209,8 @@
             ].T.astype(jnp.bfloat16)
 
 
-def turn_kernel(own_ref, y_ref, z_ref, out_own_ref, out_other_ref, relay_z_ref, relay_y_ref):
+def turn_kernel(own_ref, y_ref, z_ref, *refs):
+    out_own_ref, out_other_ref, relay_z_ref, relay_y_ref = refs[-4:]
     relay_z_ref[0] = y_ref[1]
     relay_y_ref[0] = z_ref[1]
     turn_blocks(((own_ref, 0), (y_ref, 0), (z_ref, 2)), out_own_ref)
@@ -286,6 +287,9 @@
         compiler_params=params,
     )(inputs)
     from_y, from_z = exchange(to_y, 2), exchange(to_z, 4)
+    pairs, turn = transform_tables(blocks, width, rows)
+    table, places = packed(pairs)
+    table, turn = jnp.asarray(table), jnp.asarray(turn)
     *turned, relay_z, relay_y = pl.pallas_call(
         turn_kernel,
         out_shape=[shaped(far * part, (SIDE - 1) * rows, dtype=bf16)] * 2
@@ -294,7 +298,7 @@
         cost_estimate=pl.CostEstimate(
             flops=0, bytes_accessed=200 * SIDE * far * rows * part, transcendentals=0
         ),
-    )(own, from_y, from_z)
+    )(own, from_y, from_z, table, turn)
     corners = exchange(relay_z, 4), exchange(relay_y, 2)
     signals, gates = pl.pallas_call(
         functools.partial(project_kernel, scaling),
@@ -320,15 +324,13 @@
     )(inputs, in_weight, filter_taps, grad_out)
 
     signals = lax.all_to_all(signals, "seq", split_axis=0, concat_axis=0, tiled=True)
-    pairs, turn = transform_tables(blocks, width, rows)
-    table, places = packed(pairs)
     results = pl.pallas_call(
         functools.partial(conv_kernel, places),
         in_specs=[inside] * 3 + [anywhere] * 2,
         out_shape=shaped(blocks, 3, width, rows),
         scratch_shapes=[pltpu.VMEM((blocks * width, 3 * rows), f32)],
         compiler_params=params,
-    )(signals, jnp.asarray(table), jnp.asarray(turn), *turned)
+    )(signals, table, turn, *turned)
     results = lax.all_to_all(results, "seq", split_axis=0, concat_axis=0, tiled=True)
     turned_corners = pl.pallas_call(
         corner_kernel,

time: 121 us -> 125 us (1.033)
  local copies, waits for them, and re-layouts: 9.61 us -> 14.2 us
  waiting for transfers between devices: 69.7 us -> 66 us
  starting transfers between devices: 25.8 us -> 28.3 us
    unnamed x24 -> x36, local copies, waits for them, and re-layouts: 9.61 us -> 14.2 us
    all_to_all x1, waiting for transfers between devices: 2.85 us -> 0.01 us  [per_device(): lax.all_to_all(signals, 'seq', split_axis=0, concat_axis=0, tiled=True)]
    all_to_all x1, starting transfers between devices: 3.55 us -> 5.92 us  [per_device(): lax.all_to_all(results, 'seq', split_axis=0, concat_axis=0, tiled=True)]
  transfers between devices with their start and end apart: 16 -> 16, of which waited for: 11 -> 10; matrix products, arithmetic and copies ran while one was open for 3% -> 2% of each run, Pallas kernels for 3% -> 3%
where the time goes in v4:
time: 125 us
  waiting for transfers between devices  66 us (53%)
  starting transfers between devices  28.3 us (23%)
  local copies, waits for them, and re-layouts  14.2 us (11%)
  Pallas kernels  12.2 us (10%)
  matrix products  3.11 us (2%)
    ppermute x14, waiting for transfers between devices, exchange(): return lax.ppermute(value, 'seq', [(i, i ^ flip) for i in range(blocks)])  66 us
    ppermute x14, starting transfers between devices, exchange(): return lax.ppermute(value, 'seq', [(i, i ^ flip) for i in range(blocks)])  18.4 us
    unnamed x36, local copies, waits for them, and re-layouts  14.2 us
    all_to_all x1, starting transfers between devices, per_device(): lax.all_to_all(results, 'seq', split_axis=0, concat_axis=0, tiled=True)  5.92 us
    all_to_all x1, starting transfers between devices, per_device(): lax.all_to_all(signals, 'seq', split_axis=0, concat_axis=0, tiled=True)  3.97 us
    pallas_call x1, Pallas kernels, per_device(): pl.pallas_call(functools.partial(conv_kernel, places), in_specs=[inside]...  3.33 us
    dot_general x1, matrix products, per_device(): lax.dot_general(grad_proj, in_weight, (((1,), (1,)), ((), ())), preferred...  3.11 us
  transfers between devices with their start and end apart: 16, of which 10 were waited for; matrix products, arithmetic and copies ran while one was open for 2% of the time, Pallas kernels for 3%

profile of v4, /device:TPU:0, one launch (start us, length us, event | category | flops | bytes accessed | tf_op | source)
XLA Modules:
  0.0 124.6 jit_solution(10509638328477238325)
XLA Ops:
  0.6 1.2 copy-done.3
  1.9 2.1 %shard_map.86 = (f32[2,2,128,256]{3,2,1,0:T(8,128)S(1)}, f32[3,2,128,256]{3,2,1,0:T(8,128)}, f32[3,2,128,256]{3,2,1,0:T(8,128)}) custom-call(bf16[128,4096]{1,0:T(8,128)(2,1)S(1)} %copy-done.3), custom_call_target="tpu_custom_call" | custom-call | tf_op jit(solution)/shard_map/pallas_call | solution.py:284
  4.0 0.8 copy-done.7
  4.7 3.0 %collective-permute-start = (f32[3,2,128,256]{3,2,1,0:T(8,128)}, f32[3,2,128,256]{3,2,1,0:T(8,128)S(1)}, u32[]{:S(2)}, u32[]{:S(2)}) collective-permute-start(f32[3,2,128,256]{3,2,1,0:T(8,128)} %get-tuple-element.24), channel_id=1, source_target_pairs={{0,2},{1,3},{2,0},{3,1},{4,6},{5,7},{6,4},{7,5},{8,10},{9,11},{10,... | collective-permute-start | bytes 2359304 | tf_op jit(solution)/shard_map/ppermute | solution.py:280
  7.7 1.6 %collective-permute-start.1 = (f32[3,2,128,256]{3,2,1,0:T(8,128)}, f32[3,2,128,256]{3,2,1,0:T(8,128)}, u32[]{:S(2)}, u32[]{:S(2)}) collective-permute-start(f32[3,2,128,256]{3,2,1,0:T(8,128)} %get-tuple-element.25), channel_id=1, source_target_pairs={{0,4},{1,5},{2,6},{3,7},{4,0},{5,1},{6,2},{7,3},{8,12},{9,13},{10,... | collective-permute-start | bytes 2359304 | tf_op jit(solution)/shard_map/ppermute | solution.py:280
  9.3 2.8 %copy-done = bf16[4096,768]{1,0:T(8,128)(2,1)S(1)} copy-done((bf16[4096,768]{1,0:T(8,128)(2,1)S(1)}, bf16[4096,768]{1,0:T(8,128)(2,1)}, u32[]{:S(2)}) %copy-start) | copy-done | bytes 6291480
  12.1 0.9 copy-done.12
  13.0 0.8 copy-done.13
  13.8 1.9 %shard_map.85 = (f32[16,3,16,128]{3,2,1,0:T(8,128)S(1)}, bf16[3,256,128]{2,1,0:T(8,128)(2,1)S(1)}) custom-call(bf16[128,4096]{1,0:T(8,128)(2,1)S(1)} %copy-done.3, bf16[4096,768]{1,0:T(8,128)(2,1)S(1)} %copy-done, f32[128,256]{1,0:T(8,128)S(1)} %copy-done.12, bf16[128,256]{1,0:T(8,128)(2,1)S(1)} %copy-done.13), custom_call_target="tpu_custom_call" | custom-call | flops 805306368 | bytes 7340032 | tf_op jit(solution)/shard_map/pallas_call | solution.py:303
  15.8 0.8 copy-done.9
  16.5 4.0 %all-to-all-start = ((f32[16,3,16,128]{3,2,1,0:T(8,128)}), f32[16,3,16,128]{3,2,1,0:T(8,128)S(1)}, u32[]{:S(2)}, u32[]{:S(2)}) async-start(f32[16,3,16,128]{3,2,1,0:T(8,128)} %copy-done.9), calls=%async_computation | async-start | bytes 786432 | tf_op jit(solution)/shard_map/all_to_all | solution.py:326
  20.5 6.1 %collective-permute-done.y_ref = f32[3,2,128,256]{3,2,1,0:T(8,128)S(1)} collective-permute-done((f32[3,2,128,256]{3,2,1,0:T(8,128)}, f32[3,2,128,256]{3,2,1,0:T(8,128)S(1)}, u32[]{:S(2)}, u32[]{:S(2)}) %collective-permute-start) | collective-permute-done | bytes 786464 | tf_op jit(solution)/shard_map/ppermute | solution.py:280
  26.6 0.9 copy-done.5
  27.5 3.3 %collective-permute-done.1.z_ref = f32[3,2,128,256]{3,2,1,0:T(8,128)} collective-permute-done((f32[3,2,128,256]{3,2,1,0:T(8,128)}, f32[3,2,128,256]{3,2,1,0:T(8,128)}, u32[]{:S(2)}, u32[]{:S(2)}) %collective-permute-start.1) | collective-permute-done | bytes 786464 | tf_op jit(solution)/shard_map/ppermute | solution.py:280
  30.8 1.1 copy-done.6
  31.9 1.0 copy-done.8
  33.0 1.4 %shard_map.87 = (bf16[512,384]{1,0:T(8,128)(2,1)S(1)}, bf16[512,384]{1,0:T(8,128)(2,1)S(1)}, f32[1,2,128,256]{3,2,1,0:T(8,128)S(1)}, f32[1,2,128,256]{3,2,1,0:T(8,128)S(1)}) custom-call(f32[2,2,128,256]{3,2,1,0:T(8,128)S(1)} %copy-done.8, f32[3,2,128,256]{3,2,1,0:T(8,128)S(1)} %copy-done.6, f32[3,2,128,256]{3,2,1,0:T(8,128)} %collective-permute-done.1.z_ref, ...), custom_call_target="tpu_custom_call" | custom-call | bytes 52428800 | tf_op jit(solution)/shard_map/pallas_call | solution.py:293
  34.4 0.7 copy-done.14
  35.1 0.7 copy-done.15
  35.8 1.5 %copy-done.2 = bf16[3648,256]{1,0:T(8,128)(2,1)S(1)} copy-done((bf16[3648,256]{1,0:T(8,128)(2,1)S(1)}, bf16[3648,256]{1,0:T(8,128)(2,1)}, u32[]{:S(2)}) %copy-start.2) | copy-done | bytes 1867800
  37.3 3.3 %shard_map.88 = f32[16,3,16,128]{3,2,1,0:T(8,128)} custom-call(f32[16,3,16,128]{3,2,1,0:T(8,128)S(1)} %all-to-all-done.x_ref, bf16[3648,256]{1,0:T(8,128)(2,1)S(1)} %copy-done.2, f32[272,256]{1,0:T(8,128)S(1)} %copy-done.4, bf16[512,384]{1,0:T(8,128)(2,1)S(1)} %get-tuple-element.26.refs_0_.x_ref, bf16[512,384]{1,0:T(8,128)(2,1)S(1)} %get-tuple-element.27.refs_1_.x_ref), custom_call_target="tpu_custom_call" | custom-call | tf_op jit(solution)/shard_map/pallas_call | solution.py:327
  40.7 5.9 %all-to-all-start.1 = ((f32[16,3,16,128]{3,2,1,0:T(8,128)}), f32[16,3,16,128]{3,2,1,0:T(8,128)S(1)}, u32[]{:S(2)}, u32[]{:S(2)}) async-start(f32[16,3,16,128]{3,2,1,0:T(8,128)} %shard_map.88), calls=%async_computation.1 | async-start | bytes 786432 | tf_op jit(solution)/shard_map/all_to_all | solution.py:334
  46.6 1.9 %collective-permute-start.2 = (f32[1,2,128,256]{3,2,1,0:T(8,128)}, f32[1,2,128,256]{3,2,1,0:T(8,128)S(1)}, u32[]{:S(2)}, u32[]{:S(2)}) collective-permute-start(f32[1,2,128,256]{3,2,1,0:T(8,128)} %copy-done.15), channel_id=1, source_target_pairs={{0,4},{1,5},{2,6},{3,7},{4,0},{5,1},{6,2},{7,3},{8,12},{9,13},{10,... | collective-permute-start | bytes 786440 | tf_op jit(solution)/shard_map/ppermute | solution.py:280
  48.5 1.5 %collective-permute-start.3 = (f32[1,2,128,256]{3,2,1,0:T(8,128)}, f32[1,2,128,256]{3,2,1,0:T(8,128)S(1)}, u32[]{:S(2)}, u32[]{:S(2)}) collective-permute-start(f32[1,2,128,256]{3,2,1,0:T(8,128)} %copy-done.14), channel_id=1, source_target_pairs={{0,2},{1,3},{2,0},{3,1},{4,6},{5,7},{6,4},{7,5},{8,10},{9,11},{10,... | collective-permute-start | bytes 786440 | tf_op jit(solution)/shard_map/ppermute | solution.py:280
  50.0 11.7 %collective-permute-done.2.corner_own_ref = f32[1,2,128,256]{3,2,1,0:T(8,128)S(1)} collective-permute-done((f32[1,2,128,256]{3,2,1,0:T(8,128)}, f32[1,2,128,256]{3,2,1,0:T(8,128)S(1)}, u32[]{:S(2)}, u32[]{:S(2)}) %collective-permute-start.2) | collective-permute-done | bytes 262176 | tf_op jit(solution)/shard_map/ppermute | solution.py:280
  61.8 0.9 copy-done.11
  62.7 0.8 shard_map.90
  63.6 1.5 %collective-permute-start.4 = (f32[128,256]{1,0:T(8,128)S(1)}, f32[128,256]{1,0:T(8,128)S(1)}, u32[]{:S(2)}, u32[]{:S(2)}) collective-permute-start(f32[128,256]{1,0:T(8,128)S(1)} %get-tuple-element.34.refs_0_), channel_id=1, source_target_pairs={{0,2},{1,3},{2,0},{3,1},{4,6},{5,7},{6,4},{7,5},{8,10},{9,11},{10,... | collective-permute-start | bytes 393224 | tf_op jit(solution)/shard_map/ppermute | solution.py:280
  65.0 0.6 collective-permute-start.5
  65.6 1.5 %collective-permute-start.6 = (f32[128,256]{1,0:T(8,128)S(1)}, f32[128,256]{1,0:T(8,128)S(1)}, u32[]{:S(2)}, u32[]{:S(2)}) collective-permute-start(f32[128,256]{1,0:T(8,128)S(1)} %get-tuple-element.34.refs_0_), channel_id=1, source_target_pairs={{0,6},{1,7},{2,4},{3,5},{4,2},{5,3},{6,0},{7,1},{8,14},{9,15},{10,... | collective-permute-start | bytes 393224 | tf_op jit(solution)/shard_map/ppermute | solution.py:280
  67.1 2.0 %collective-permute-done.4.refs_1_ = f32[128,256]{1,0:T(8,128)S(1)} collective-permute-done((f32[128,256]{1,0:T(8,128)S(1)}, f32[128,256]{1,0:T(8,128)S(1)}, u32[]{:S(2)}, u32[]{:S(2)}) %collective-permute-start.4) | collective-permute-done | bytes 131104 | tf_op jit(solution)/shard_map/ppermute | solution.py:280
  69.1 2.1 %collective-permute-done.5.refs_2_ = f32[128,256]{1,0:T(8,128)S(1)} collective-permute-done((f32[128,256]{1,0:T(8,128)S(1)}, f32[128,256]{1,0:T(8,128)S(1)}, u32[]{:S(2)}, u32[]{:S(2)}) %collective-permute-start.5) | collective-permute-done | bytes 131104 | tf_op jit(solution)/shard_map/ppermute | solution.py:280
  71.2 1.4 %collective-permute-done.6.refs_3_ = f32[128,256]{1,0:T(8,128)S(1)} collective-permute-done((f32[128,256]{1,0:T(8,128)S(1)}, f32[128,256]{1,0:T(8,128)S(1)}, u32[]{:S(2)}, u32[]{:S(2)}) %collective-permute-start.6) | collective-permute-done | bytes 131104 | tf_op jit(solution)/shard_map/ppermute | solution.py:280
  72.6 0.3 shard_map.91
  73.0 0.8 collective-permute-start.10
  73.8 2.2 %collective-permute-start.11 = (f32[128,512]{1,0:T(8,128)S(1)}, f32[128,512]{1,0:T(8,128)S(1)}, u32[]{:S(2)}, u32[]{:S(2)}) collective-permute-start(f32[128,512]{1,0:T(8,128)S(1)} %get-tuple-element.37.refs_0_), channel_id=1, source_target_pairs={{0,6},{1,7},{2,4},{3,5},{4,2},{5,3},{6,0},{7,1},{8,14},{9,15},{10,... | collective-permute-start | bytes 786440 | tf_op jit(solution)/shard_map/ppermute | solution.py:280
  76.0 0.6 collective-permute-start.9
  76.6 0.3 shard_map.92
  76.9 2.5 %collective-permute-start.8 = (f32[256,256]{1,0:T(8,128)S(1)}, f32[256,256]{1,0:T(8,128)S(1)}, u32[]{:S(2)}, u32[]{:S(2)}) collective-permute-start(f32[256,256]{1,0:T(8,128)S(1)} %get-tuple-element.36), channel_id=1, source_target_pairs={{0,8},{1,9},{2,10},{3,11},{4,12},{5,13},{6,14},{7,15},{8,0},{9,1},... | collective-permute-start | bytes 786440 | tf_op jit(solution)/shard_map/ppermute | solution.py:280
  79.3 8.4 %collective-permute-done.10.refs_2_ = f32[128,512]{1,0:T(8,128)S(1)} collective-permute-done((f32[128,512]{1,0:T(8,128)S(1)}, f32[128,512]{1,0:T(8,128)S(1)}, u32[]{:S(2)}, u32[]{:S(2)}) %collective-permute-start.10) | collective-permute-done | bytes 262176 | tf_op jit(solution)/shard_map/ppermute | solution.py:280
  87.8 6.1 %collective-permute-done.11.refs_3_ = f32[128,512]{1,0:T(8,128)S(1)} collective-permute-done((f32[128,512]{1,0:T(8,128)S(1)}, f32[128,512]{1,0:T(8,128)S(1)}, u32[]{:S(2)}, u32[]{:S(2)}) %collective-permute-start.11) | collective-permute-done | bytes 262176 | tf_op jit(solution)/shard_map/ppermute | solution.py:280
  93.9 0.4 shard_map.93
  94.4 2.6 %collective-permute-done.12.refs_4_ = f32[512,512]{1,0:T(8,128)S(1)} collective-permute-done((f32[512,512]{1,0:T(8,128)S(1)}, f32[512,512]{1,0:T(8,128)S(1)}, u32[]{:S(2)}, u32[]{:S(2)}) %collective-permute-start.12) | collective-permute-done | bytes 1048608 | tf_op jit(solution)/shard_map/ppermute | solution.py:280
  97.0 0.4 shard_map.94
  97.5 0.8 collective-permute-start.13
  98.3 3.1 %convolution_convert_fusion = bf16[128,4096]{1,0:T(8,128)(2,1)} fusion(bf16[128,768]{1,0:T(8,128)(2,1)S(1)} %get-tuple-element.33, bf16[4096,768]{1,0:T(8,128)(2,1)S(1)} %bitcast.3), kind=kOutput, calls=%fused_computation | convolution fusion | flops 805830656 | bytes 7536640 | tf_op jit(solution)/shard_map/dot_general | solution.py:355
  101.4 22.2 %collective-permute-done.13.refs_3_ = f32[256,512]{1,0:T(8,128)S(1)} collective-permute-done((f32[256,512]{1,0:T(8,128)S(1)}, f32[256,512]{1,0:T(8,128)S(1)}, u32[]{:S(2)}, u32[]{:S(2)}) %collective-permute-start.13) | collective-permute-done | bytes 524320 | tf_op jit(solution)/shard_map/ppermute | solution.py:280
  123.6 1.0 shard_map.95
  (33 shorter events, 0.3 us)
Async XLA Ops:
  0.6 1.2 copy-start.3
  1.9 28.9 %copy-start.4 = (f32[272,256]{1,0:T(8,128)S(1)}, f32[272,256]{1,0:T(8,128)}, u32[]{:S(2)}) copy-start(f32[272,256]{1,0:T(8,128)} %constant.5.clone.refs_1_.turn_ref) | copy-start | bytes 835588
  4.0 0.8 copy-start.7
  4.7 21.9 %collective-permute-start = (f32[3,2,128,256]{3,2,1,0:T(8,128)}, f32[3,2,128,256]{3,2,1,0:T(8,128)S(1)}, u32[]{:S(2)}, u32[]{:S(2)}) collective-permute-start(f32[3,2,128,256]{3,2,1,0:T(8,128)} %get-tuple-element.24), channel_id=1, source_target_pairs={{0,2},{1,3},{2,0},{3,1},{4,6},{5,7},{6,4},{7,5},{8,10},{9,11},{10,... | collective-permute-start | bytes 2359304 | tf_op jit(solution)/shard_map/ppermute | solution.py:280
  7.7 23.1 %collective-permute-start.1 = (f32[3,2,128,256]{3,2,1,0:T(8,128)}, f32[3,2,128,256]{3,2,1,0:T(8,128)}, u32[]{:S(2)}, u32[]{:S(2)}) collective-permute-start(f32[3,2,128,256]{3,2,1,0:T(8,128)} %get-tuple-element.25), channel_id=1, source_target_pairs={{0,4},{1,5},{2,6},{3,7},{4,0},{5,1},{6,2},{7,3},{8,12},{9,13},{10,... | collective-permute-start | bytes 2359304 | tf_op jit(solution)/shard_map/ppermute | solution.py:280
  9.3 2.8 %copy-start = (bf16[4096,768]{1,0:T(8,128)(2,1)S(1)}, bf16[4096,768]{1,0:T(8,128)(2,1)}, u32[]{:S(2)}) copy-start(bf16[4096,768]{1,0:T(8,128)(2,1)} %w_ref.1) | copy-start | bytes 18874372
  12.1 0.9 copy-start.12
  13.0 0.8 copy-start.13
  13.8 17.0 %copy-start.1 = (bf16[3648,256]{1,0:T(8,128)(2,1)S(1)}, bf16[3648,256]{1,0:T(8,128)(2,1)}, u32[]{:S(2)}) copy-start(bf16[3648,256]{1,0:T(8,128)(2,1)} %constant.4.clone.refs_0_.table_ref) | copy-start | bytes 5603332
  15.8 0.8 copy-start.9
  16.5 14.3 %copy-start.10 = (bf16[3,256,128]{2,1,0:T(8,128)(2,1)}, bf16[3,256,128]{2,1,0:T(8,128)(2,1)S(1)}, u32[]{:S(2)}) copy-start(bf16[3,256,128]{2,1,0:T(8,128)(2,1)S(1)} %get-tuple-element.28.gates_ref) | copy-start | bytes 589828
  16.5 19.3 %all-to-all-start = ((f32[16,3,16,128]{3,2,1,0:T(8,128)}), f32[16,3,16,128]{3,2,1,0:T(8,128)S(1)}, u32[]{:S(2)}, u32[]{:S(2)}) async-start(f32[16,3,16,128]{3,2,1,0:T(8,128)} %copy-done.9), calls=%async_computation | async-start | bytes 786432 | tf_op jit(solution)/shard_map/all_to_all | solution.py:326
  26.6 0.9 copy-start.5
  30.8 1.1 copy-start.6
  31.9 1.0 copy-start.8
  34.4 0.7 copy-start.14
  35.1 0.7 copy-start.15
  35.8 1.5 %copy-start.2 = (bf16[3648,256]{1,0:T(8,128)(2,1)S(1)}, bf16[3648,256]{1,0:T(8,128)(2,1)}, u32[]{:S(2)}) copy-start(bf16[3648,256]{1,0:T(8,128)(2,1)} %constant.4.clone.refs_0_.table_ref) | copy-start | bytes 5603332
  37.3 61.0 %slice-start = ((s8[6291456]{0:T(1024)(128)(4,1)}), s8[2097152]{0:T(1024)(128)(4,1)S(1)}, s32[]{:S(2)}) async-start(s8[6291456]{0:T(1024)(128)(4,1)} %bitcast.2), calls=%async_computation.2 | async-start | bytes 4194304
  40.7 21.1 %all-to-all-start.1 = ((f32[16,3,16,128]{3,2,1,0:T(8,128)}), f32[16,3,16,128]{3,2,1,0:T(8,128)S(1)}, u32[]{:S(2)}, u32[]{:S(2)}) async-start(f32[16,3,16,128]{3,2,1,0:T(8,128)} %shard_map.88), calls=%async_computation.1 | async-start | bytes 786432 | tf_op jit(solution)/shard_map/all_to_all | solution.py:334
  46.6 15.1 %collective-permute-start.2 = (f32[1,2,128,256]{3,2,1,0:T(8,128)}, f32[1,2,128,256]{3,2,1,0:T(8,128)S(1)}, u32[]{:S(2)}, u32[]{:S(2)}) collective-permute-start(f32[1,2,128,256]{3,2,1,0:T(8,128)} %copy-done.15), channel_id=1, source_target_pairs={{0,4},{1,5},{2,6},{3,7},{4,0},{5,1},{6,2},{7,3},{8,12},{9,13},{10,... | collective-permute-start | bytes 786440 | tf_op jit(solution)/shard_map/ppermute | solution.py:280
  48.5 13.1 %collective-permute-start.3 = (f32[1,2,128,256]{3,2,1,0:T(8,128)}, f32[1,2,128,256]{3,2,1,0:T(8,128)S(1)}, u32[]{:S(2)}, u32[]{:S(2)}) collective-permute-start(f32[1,2,128,256]{3,2,1,0:T(8,128)} %copy-done.14), channel_id=1, source_target_pairs={{0,2},{1,3},{2,0},{3,1},{4,6},{5,7},{6,4},{7,5},{8,10},{9,11},{10,... | collective-permute-start | bytes 786440 | tf_op jit(solution)/shard_map/ppermute | solution.py:280
  61.8 0.9 copy-start.11
  63.6 34.7 %slice-start.1 = ((s8[6291456]{0:T(1024)(128)(4,1)}), s8[4194304]{0:T(1024)(128)(4,1)S(1)}, s32[]{:S(2)}) async-start(s8[6291456]{0:T(1024)(128)(4,1)} %bitcast.2), calls=%async_computation.3 | async-start | bytes 8388608
  63.6 5.5 %collective-permute-start.4 = (f32[128,256]{1,0:T(8,128)S(1)}, f32[128,256]{1,0:T(8,128)S(1)}, u32[]{:S(2)}, u32[]{:S(2)}) collective-permute-start(f32[128,256]{1,0:T(8,128)S(1)} %get-tuple-element.34.refs_0_), channel_id=1, source_target_pairs={{0,2},{1,3},{2,0},{3,1},{4,6},{5,7},{6,4},{7,5},{8,10},{9,11},{10,... | collective-permute-start | bytes 393224 | tf_op jit(solution)/shard_map/ppermute | solution.py:280
  65.0 6.2 %collective-permute-start.5 = (f32[128,256]{1,0:T(8,128)S(1)}, f32[128,256]{1,0:T(8,128)S(1)}, u32[]{:S(2)}, u32[]{:S(2)}) collective-permute-start(f32[128,256]{1,0:T(8,128)S(1)} %get-tuple-element.34.refs_0_), channel_id=1, source_target_pairs={{0,4},{1,5},{2,6},{3,7},{4,0},{5,1},{6,2},{7,3},{8,12},{9,13},{10,... | collective-permute-start | bytes 393224 | tf_op jit(solution)/shard_map/ppermute | solution.py:280
  65.6 7.0 %collective-permute-start.6 = (f32[128,256]{1,0:T(8,128)S(1)}, f32[128,256]{1,0:T(8,128)S(1)}, u32[]{:S(2)}, u32[]{:S(2)}) collective-permute-start(f32[128,256]{1,0:T(8,128)S(1)} %get-tuple-element.34.refs_0_), channel_id=1, source_target_pairs={{0,6},{1,7},{2,4},{3,5},{4,2},{5,3},{6,0},{7,1},{8,14},{9,15},{10,... | collective-permute-start | bytes 393224 | tf_op jit(solution)/shard_map/ppermute | solution.py:280
  72.9 3.6 %collective-permute-start.7 = (f32[512,256]{1,0:T(8,128)S(1)}, f32[512,256]{1,0:T(8,128)S(1)}, u32[]{:S(2)}, u32[]{:S(2)}) collective-permute-start(f32[512,256]{1,0:T(8,128)S(1)} %shard_map.91), channel_id=1, source_target_pairs={{0,1},{1,0},{2,3},{3,2},{4,5},{5,4},{6,7},{7,6},{8,9},{9,8},{10,11... | collective-permute-start | bytes 1572872 | tf_op jit(solution)/shard_map/ppermute | solution.py:280
  73.0 14.8 %collective-permute-start.10 = (f32[128,512]{1,0:T(8,128)S(1)}, f32[128,512]{1,0:T(8,128)S(1)}, u32[]{:S(2)}, u32[]{:S(2)}) collective-permute-start(f32[128,512]{1,0:T(8,128)S(1)} %get-tuple-element.37.refs_0_), channel_id=1, source_target_pairs={{0,4},{1,5},{2,6},{3,7},{4,0},{5,1},{6,2},{7,3},{8,12},{9,13},{10,... | collective-permute-start | bytes 786440 | tf_op jit(solution)/shard_map/ppermute | solution.py:280
  73.8 20.1 %collective-permute-start.11 = (f32[128,512]{1,0:T(8,128)S(1)}, f32[128,512]{1,0:T(8,128)S(1)}, u32[]{:S(2)}, u32[]{:S(2)}) collective-permute-start(f32[128,512]{1,0:T(8,128)S(1)} %get-tuple-element.37.refs_0_), channel_id=1, source_target_pairs={{0,6},{1,7},{2,4},{3,5},{4,2},{5,3},{6,0},{7,1},{8,14},{9,15},{10,... | collective-permute-start | bytes 786440 | tf_op jit(solution)/shard_map/ppermute | solution.py:280
  76.0 17.9 %collective-permute-start.9 = (f32[128,512]{1,0:T(8,128)S(1)}, f32[128,512]{1,0:T(8,128)S(1)}, u32[]{:S(2)}, u32[]{:S(2)}) collective-permute-start(f32[128,512]{1,0:T(8,128)S(1)} %get-tuple-element.37.refs_0_), channel_id=1, source_target_pairs={{0,2},{1,3},{2,0},{3,1},{4,6},{5,7},{6,4},{7,5},{8,10},{9,11},{10,... | collective-permute-start | bytes 786440 | tf_op jit(solution)/shard_map/ppermute | solution.py:280
  76.9 17.0 %collective-permute-start.8 = (f32[256,256]{1,0:T(8,128)S(1)}, f32[256,256]{1,0:T(8,128)S(1)}, u32[]{:S(2)}, u32[]{:S(2)}) collective-permute-start(f32[256,256]{1,0:T(8,128)S(1)} %get-tuple-element.36), channel_id=1, source_target_pairs={{0,8},{1,9},{2,10},{3,11},{4,12},{5,13},{6,14},{7,15},{8,0},{9,1},... | collective-permute-start | bytes 786440 | tf_op jit(solution)/shard_map/ppermute | solution.py:280
  94.3 2.7 %collective-permute-start.12 = (f32[512,512]{1,0:T(8,128)S(1)}, f32[512,512]{1,0:T(8,128)S(1)}, u32[]{:S(2)}, u32[]{:S(2)}) collective-permute-start(f32[512,512]{1,0:T(8,128)S(1)} %shard_map.93), channel_id=1, source_target_pairs={{0,1},{1,0},{2,3},{3,2},{4,5},{5,4},{6,7},{7,6},{8,9},{9,8},{10,11... | collective-permute-start | bytes 3145736 | tf_op jit(solution)/shard_map/ppermute | solution.py:280
  97.5 26.2 %collective-permute-start.13 = (f32[256,512]{1,0:T(8,128)S(1)}, f32[256,512]{1,0:T(8,128)S(1)}, u32[]{:S(2)}, u32[]{:S(2)}) collective-permute-start(f32[256,512]{1,0:T(8,128)S(1)} %get-tuple-element.39), channel_id=1, source_target_pairs={{0,8},{1,9},{2,10},{3,11},{4,12},{5,13},{6,14},{7,15},{8,0},{9,1},... | collective-permute-start | bytes 1572872 | tf_op jit(solution)/shard_map/ppermute | solution.py:280

commit v5 on v3

--- a/solution.py
+++ b/solution.py
@@ -10,6 +10,7 @@
 from jax.sharding import PartitionSpec as P
 
 VMEM_LIMIT = 12 * 1024 * 1024
+VMEM_STREAM = 52 * 1024 * 1024
 SIDE = 4
 
 
@@ -311,7 +312,7 @@
         + [pl.BlockSpec((3, channels, rows), lambda i: (0, 0, 0))],
         out_shape=[shaped(blocks, 3, width, rows), shaped(3, channels, rows, dtype=bf16)],
         scratch_shapes=[pltpu.VMEM((rows, columns), f32)],
-        compiler_params=params,
+        compiler_params=pltpu.CompilerParams(vmem_limit_bytes=VMEM_STREAM),
         cost_estimate=pl.CostEstimate(
             flops=2 * rows * depth * columns,
             bytes_accessed=2 * depth * (rows + columns),

time: 121 us -> 123 us (1.017)
  waiting for transfers between devices: 69.7 us -> 62.2 us
  Pallas kernels: 11.8 us -> 15.6 us
  matrix products: 3.11 us -> 5.89 us
  starting transfers between devices: 25.8 us -> 28.3 us
    ppermute x14, waiting for transfers between devices: 66.9 us -> 62.2 us  [exchange(): return lax.ppermute(value, 'seq', [(i, i ^ flip) for i in range(blocks)])]
    all_to_all x1, waiting for transfers between devices: 2.85 us -> 0.01 us  [per_device(): lax.all_to_all(signals, 'seq', split_axis=0, concat_axis=0, tiled=True)]
    dot_general x1, matrix products: 3.11 us -> 5.89 us  [per_device(): lax.dot_general(grad_proj, in_weight, (((1,), (1,)), ((), ())), preferred...]
    pallas_call x1, Pallas kernels: 2.7 us -> 5.35 us  [per_device(): pl.pallas_call(functools.partial(project_kernel, scaling), grid=(steps,),...]
    all_to_all x1, starting transfers between devices: 3.55 us -> 5.92 us  [per_device(): lax.all_to_all(results, 'seq', split_axis=0, concat_axis=0, tiled=True)]
  transfers between devices with their start and end apart: 16 -> 16, of which waited for: 11 -> 10; matrix products, arithmetic and copies ran while one was open for 3% -> 5% of each run, Pallas kernels for 3% -> 6%
where the time goes in v5:
time: 123 us; the launch traced here: 122 us
  waiting for transfers between devices  62.2 us (51%)
  starting transfers between devices  28.3 us (23%)
  Pallas kernels  15.6 us (13%)
  local copies, waits for them, and re-layouts  9.45 us (8%)
  matrix products  5.89 us (5%)
    ppermute x14, waiting for transfers between devices, exchange(): return lax.ppermute(value, 'seq', [(i, i ^ flip) for i in range(blocks)])  62.2 us
    ppermute x14, starting transfers between devices, exchange(): return lax.ppermute(value, 'seq', [(i, i ^ flip) for i in range(blocks)])  18.4 us
    unnamed x24, local copies, waits for them, and re-layouts  9.45 us
    all_to_all x1, starting transfers between devices, per_device(): lax.all_to_all(results, 'seq', split_axis=0, concat_axis=0, tiled=True)  5.92 us
    dot_general x1, matrix products, per_device(): lax.dot_general(grad_proj, in_weight, (((1,), (1,)), ((), ())), preferred...  5.89 us
    pallas_call x1, Pallas kernels, per_device(): pl.pallas_call(functools.partial(project_kernel, scaling), grid=(steps,),...  5.35 us
    all_to_all x1, starting transfers between devices, per_device(): lax.all_to_all(signals, 'seq', split_axis=0, concat_axis=0, tiled=True)  3.97 us
    pallas_call x1, Pallas kernels, per_device(): pl.pallas_call(functools.partial(conv_kernel, places), in_specs=[inside]...  3.34 us
  transfers between devices with their start and end apart: 16, of which 10 were waited for; matrix products, arithmetic and copies ran while one was open for 5% of the time, Pallas kernels for 6%

profile of v5, /device:TPU:0, one launch (start us, length us, event | category | flops | bytes accessed | tf_op | source)
XLA Modules:
  0.0 122.2 jit_solution(2896327643850649091)
XLA Ops:
  0.6 1.2 copy-done
  1.9 2.1 %shard_map.86 = (f32[2,2,128,256]{3,2,1,0:T(8,128)S(1)}, f32[3,2,128,256]{3,2,1,0:T(8,128)}, f32[3,2,128,256]{3,2,1,0:T(8,128)}) custom-call(bf16[128,4096]{1,0:T(8,128)(2,1)S(1)} %copy-done), custom_call_target="tpu_custom_call" | custom-call | tf_op jit(solution)/shard_map/pallas_call | solution.py:284
  4.0 0.8 copy-done.5
  4.8 3.0 %collective-permute-start = (f32[3,2,128,256]{3,2,1,0:T(8,128)}, f32[3,2,128,256]{3,2,1,0:T(8,128)S(1)}, u32[]{:S(2)}, u32[]{:S(2)}) collective-permute-start(f32[3,2,128,256]{3,2,1,0:T(8,128)} %get-tuple-element.24), channel_id=1, source_target_pairs={{0,2},{1,3},{2,0},{3,1},{4,6},{5,7},{6,4},{7,5},{8,10},{9,11},{10,... | collective-permute-start | bytes 2359304 | tf_op jit(solution)/shard_map/ppermute | solution.py:280
  7.7 1.6 %collective-permute-start.1 = (f32[3,2,128,256]{3,2,1,0:T(8,128)}, f32[3,2,128,256]{3,2,1,0:T(8,128)}, u32[]{:S(2)}, u32[]{:S(2)}) collective-permute-start(f32[3,2,128,256]{3,2,1,0:T(8,128)} %get-tuple-element.25), channel_id=1, source_target_pairs={{0,4},{1,5},{2,6},{3,7},{4,0},{5,1},{6,2},{7,3},{8,12},{9,13},{10,... | collective-permute-start | bytes 2359304 | tf_op jit(solution)/shard_map/ppermute | solution.py:280
  9.3 1.2 %copy-done.1 = bf16[128,4096]{1,0:T(8,128)(2,1)S(1)} copy-done((bf16[128,4096]{1,0:T(8,128)(2,1)S(1)}, bf16[128,4096]{1,0:T(8,128)(2,1)}, u32[]{:S(2)}) %copy-start.1) | copy-done | bytes 1048600
  10.5 0.9 copy-done.8
  11.4 0.8 copy-done.9
  12.3 5.3 %shard_map.85 = (f32[16,3,16,128]{3,2,1,0:T(8,128)}, bf16[3,256,128]{2,1,0:T(8,128)(2,1)S(1)}) custom-call(bf16[128,4096]{1,0:T(8,128)(2,1)S(1)} %copy-done.1, bf16[4096,768]{1,0:T(8,128)(2,1)} %w_ref.1, f32[128,256]{1,0:T(8,128)S(1)} %copy-done.8, bf16[128,256]{1,0:T(8,128)(2,1)S(1)} %copy-done.9), custom_call_target="tpu_custom_call" | custom-call | flops 805306368 | bytes 7340032 | tf_op jit(solution)/shard_map/pallas_call | solution.py:300
  17.6 4.0 %all-to-all-start = ((f32[16,3,16,128]{3,2,1,0:T(8,128)}), f32[16,3,16,128]{3,2,1,0:T(8,128)S(1)}, u32[]{:S(2)}, u32[]{:S(2)}) async-start(f32[16,3,16,128]{3,2,1,0:T(8,128)} %get-tuple-element.22), calls=%async_computation | async-start | bytes 786432 | tf_op jit(solution)/shard_map/all_to_all | solution.py:323
  21.6 4.7 %collective-permute-done.y_ref = f32[3,2,128,256]{3,2,1,0:T(8,128)S(1)} collective-permute-done((f32[3,2,128,256]{3,2,1,0:T(8,128)}, f32[3,2,128,256]{3,2,1,0:T(8,128)S(1)}, u32[]{:S(2)}, u32[]{:S(2)}) %collective-permute-start) | collective-permute-done | bytes 786464 | tf_op jit(solution)/shard_map/ppermute | solution.py:280
  26.3 0.9 copy-done.3
  27.1 3.7 %collective-permute-done.1.z_ref = f32[3,2,128,256]{3,2,1,0:T(8,128)} collective-permute-done((f32[3,2,128,256]{3,2,1,0:T(8,128)}, f32[3,2,128,256]{3,2,1,0:T(8,128)}, u32[]{:S(2)}, u32[]{:S(2)}) %collective-permute-start.1) | collective-permute-done | bytes 786464 | tf_op jit(solution)/shard_map/ppermute | solution.py:280
  30.8 1.1 copy-done.4
  32.0 1.0 copy-done.6
  33.0 1.4 %shard_map.87 = (bf16[512,384]{1,0:T(8,128)(2,1)S(1)}, bf16[512,384]{1,0:T(8,128)(2,1)S(1)}, f32[1,2,128,256]{3,2,1,0:T(8,128)S(1)}, f32[1,2,128,256]{3,2,1,0:T(8,128)S(1)}) custom-call(f32[2,2,128,256]{3,2,1,0:T(8,128)S(1)} %copy-done.6, f32[3,2,128,256]{3,2,1,0:T(8,128)S(1)} %copy-done.4, f32[3,2,128,256]{3,2,1,0:T(8,128)} %collective-permute-done.1.z_ref), custom_call_target="tpu_custom_call" | custom-call | bytes 52428800 | tf_op jit(solution)/shard_map/pallas_call | solution.py:290
  34.5 0.7 copy-done.10
  35.1 0.7 copy-done.11
  35.8 3.3 %shard_map.88 = f32[16,3,16,128]{3,2,1,0:T(8,128)} custom-call(f32[16,3,16,128]{3,2,1,0:T(8,128)S(1)} %all-to-all-done.x_ref, bf16[3648,256]{1,0:T(8,128)(2,1)S(1)} %copy-done.2, f32[272,256]{1,0:T(8,128)S(1)} %copy-done.7, bf16[512,384]{1,0:T(8,128)(2,1)S(1)} %get-tuple-element.26.refs_0_.x_ref, bf16[512,384]{1,0:T(8,128)(2,1)S(1)} %get-tuple-element.27.refs_1_.x_ref), custom_call_target="tpu_custom_call" | custom-call | tf_op jit(solution)/shard_map/pallas_call | solution.py:326
  39.2 5.9 %all-to-all-start.1 = ((f32[16,3,16,128]{3,2,1,0:T(8,128)}), f32[16,3,16,128]{3,2,1,0:T(8,128)S(1)}, u32[]{:S(2)}, u32[]{:S(2)}) async-start(f32[16,3,16,128]{3,2,1,0:T(8,128)} %shard_map.88), calls=%async_computation.1 | async-start | bytes 786432 | tf_op jit(solution)/shard_map/all_to_all | solution.py:333
  45.1 1.9 %collective-permute-start.2 = (f32[1,2,128,256]{3,2,1,0:T(8,128)}, f32[1,2,128,256]{3,2,1,0:T(8,128)S(1)}, u32[]{:S(2)}, u32[]{:S(2)}) collective-permute-start(f32[1,2,128,256]{3,2,1,0:T(8,128)} %copy-done.11), channel_id=1, source_target_pairs={{0,4},{1,5},{2,6},{3,7},{4,0},{5,1},{6,2},{7,3},{8,12},{9,13},{10,... | collective-permute-start | bytes 786440 | tf_op jit(solution)/shard_map/ppermute | solution.py:280
  47.0 1.5 %collective-permute-start.3 = (f32[1,2,128,256]{3,2,1,0:T(8,128)}, f32[1,2,128,256]{3,2,1,0:T(8,128)S(1)}, u32[]{:S(2)}, u32[]{:S(2)}) collective-permute-start(f32[1,2,128,256]{3,2,1,0:T(8,128)} %copy-done.10), channel_id=1, source_target_pairs={{0,2},{1,3},{2,0},{3,1},{4,6},{5,7},{6,4},{7,5},{8,10},{9,11},{10,... | collective-permute-start | bytes 786440 | tf_op jit(solution)/shard_map/ppermute | solution.py:280
  48.5 11.7 %collective-permute-done.2.corner_own_ref = f32[1,2,128,256]{3,2,1,0:T(8,128)S(1)} collective-permute-done((f32[1,2,128,256]{3,2,1,0:T(8,128)}, f32[1,2,128,256]{3,2,1,0:T(8,128)S(1)}, u32[]{:S(2)}, u32[]{:S(2)}) %collective-permute-start.2) | collective-permute-done | bytes 262176 | tf_op jit(solution)/shard_map/ppermute | solution.py:280
  60.2 0.1 shard_map.89
  60.3 0.8 shard_map.90
  61.2 1.5 %collective-permute-start.4 = (f32[128,256]{1,0:T(8,128)S(1)}, f32[128,256]{1,0:T(8,128)S(1)}, u32[]{:S(2)}, u32[]{:S(2)}) collective-permute-start(f32[128,256]{1,0:T(8,128)S(1)} %get-tuple-element.34.refs_0_), channel_id=1, source_target_pairs={{0,2},{1,3},{2,0},{3,1},{4,6},{5,7},{6,4},{7,5},{8,10},{9,11},{10,... | collective-permute-start | bytes 393224 | tf_op jit(solution)/shard_map/ppermute | solution.py:280
  62.6 0.6 collective-permute-start.5
  63.2 1.5 %collective-permute-start.6 = (f32[128,256]{1,0:T(8,128)S(1)}, f32[128,256]{1,0:T(8,128)S(1)}, u32[]{:S(2)}, u32[]{:S(2)}) collective-permute-start(f32[128,256]{1,0:T(8,128)S(1)} %get-tuple-element.34.refs_0_), channel_id=1, source_target_pairs={{0,6},{1,7},{2,4},{3,5},{4,2},{5,3},{6,0},{7,1},{8,14},{9,15},{10,... | collective-permute-start | bytes 393224 | tf_op jit(solution)/shard_map/ppermute | solution.py:280
  64.7 2.0 %collective-permute-done.4.refs_1_ = f32[128,256]{1,0:T(8,128)S(1)} collective-permute-done((f32[128,256]{1,0:T(8,128)S(1)}, f32[128,256]{1,0:T(8,128)S(1)}, u32[]{:S(2)}, u32[]{:S(2)}) %collective-permute-start.4) | collective-permute-done | bytes 131104 | tf_op jit(solution)/shard_map/ppermute | solution.py:280
  66.7 2.1 %collective-permute-done.5.refs_2_ = f32[128,256]{1,0:T(8,128)S(1)} collective-permute-done((f32[128,256]{1,0:T(8,128)S(1)}, f32[128,256]{1,0:T(8,128)S(1)}, u32[]{:S(2)}, u32[]{:S(2)}) %collective-permute-start.5) | collective-permute-done | bytes 131104 | tf_op jit(solution)/shard_map/ppermute | solution.py:280
  68.8 1.4 %collective-permute-done.6.refs_3_ = f32[128,256]{1,0:T(8,128)S(1)} collective-permute-done((f32[128,256]{1,0:T(8,128)S(1)}, f32[128,256]{1,0:T(8,128)S(1)}, u32[]{:S(2)}, u32[]{:S(2)}) %collective-permute-start.6) | collective-permute-done | bytes 131104 | tf_op jit(solution)/shard_map/ppermute | solution.py:280
  70.2 0.3 shard_map.91
  70.5 0.1 collective-permute-start.7
  70.6 0.8 collective-permute-start.10
  71.4 2.2 %collective-permute-start.11 = (f32[128,512]{1,0:T(8,128)S(1)}, f32[128,512]{1,0:T(8,128)S(1)}, u32[]{:S(2)}, u32[]{:S(2)}) collective-permute-start(f32[128,512]{1,0:T(8,128)S(1)} %get-tuple-element.37.refs_0_), channel_id=1, source_target_pairs={{0,6},{1,7},{2,4},{3,5},{4,2},{5,3},{6,0},{7,1},{8,14},{9,15},{10,... | collective-permute-start | bytes 786440 | tf_op jit(solution)/shard_map/ppermute | solution.py:280
  73.6 0.6 collective-permute-start.9
  74.1 0.3 shard_map.92
  74.4 2.5 %collective-permute-start.8 = (f32[256,256]{1,0:T(8,128)S(1)}, f32[256,256]{1,0:T(8,128)S(1)}, u32[]{:S(2)}, u32[]{:S(2)}) collective-permute-start(f32[256,256]{1,0:T(8,128)S(1)} %get-tuple-element.36), channel_id=1, source_target_pairs={{0,8},{1,9},{2,10},{3,11},{4,12},{5,13},{6,14},{7,15},{8,0},{9,1},... | collective-permute-start | bytes 786440 | tf_op jit(solution)/shard_map/ppermute | solution.py:280
  76.9 8.4 %collective-permute-done.10.refs_2_ = f32[128,512]{1,0:T(8,128)S(1)} collective-permute-done((f32[128,512]{1,0:T(8,128)S(1)}, f32[128,512]{1,0:T(8,128)S(1)}, u32[]{:S(2)}, u32[]{:S(2)}) %collective-permute-start.10) | collective-permute-done | bytes 262176 | tf_op jit(solution)/shard_map/ppermute | solution.py:280
  85.4 6.1 %collective-permute-done.11.refs_3_ = f32[128,512]{1,0:T(8,128)S(1)} collective-permute-done((f32[128,512]{1,0:T(8,128)S(1)}, f32[128,512]{1,0:T(8,128)S(1)}, u32[]{:S(2)}, u32[]{:S(2)}) %collective-permute-start.11) | collective-permute-done | bytes 262176 | tf_op jit(solution)/shard_map/ppermute | solution.py:280
  91.4 0.4 shard_map.93
  91.9 0.1 collective-permute-start.12
  92.0 2.6 %collective-permute-done.12.refs_4_ = f32[512,512]{1,0:T(8,128)S(1)} collective-permute-done((f32[512,512]{1,0:T(8,128)S(1)}, f32[512,512]{1,0:T(8,128)S(1)}, u32[]{:S(2)}, u32[]{:S(2)}) %collective-permute-start.12) | collective-permute-done | bytes 1048608 | tf_op jit(solution)/shard_map/ppermute | solution.py:280
  94.6 0.4 shard_map.94
  95.1 0.8 collective-permute-start.13
  95.9 5.9 %convolution_convert_fusion = bf16[128,4096]{1,0:T(8,128)(2,1)} fusion(bf16[128,768]{1,0:T(8,128)(2,1)S(1)} %get-tuple-element.33, bf16[4096,768]{1,0:T(8,128)(2,1)} %w_ref.1), kind=kOutput, calls=%fused_computation | convolution fusion | flops 805830656 | bytes 7536640 | tf_op jit(solution)/shard_map/dot_general | solution.py:354
  101.8 19.4 %collective-permute-done.13.refs_3_ = f32[256,512]{1,0:T(8,128)S(1)} collective-permute-done((f32[256,512]{1,0:T(8,128)S(1)}, f32[256,512]{1,0:T(8,128)S(1)}, u32[]{:S(2)}, u32[]{:S(2)}) %collective-permute-start.13) | collective-permute-done | bytes 524320 | tf_op jit(solution)/shard_map/ppermute | solution.py:280
  121.2 1.0 shard_map.95
  (20 shorter events, 0.0 us)
Async XLA Ops:
  0.6 1.2 %copy-start = (bf16[128,4096]{1,0:T(8,128)(2,1)S(1)}, bf16[128,4096]{1,0:T(8,128)(2,1)}, u32[]{:S(2)}) copy-start(bf16[128,4096]{1,0:T(8,128)(2,1)} %x_ref.3) | copy-start | bytes 3145732
  1.9 34.0 %copy-start.7 = (f32[272,256]{1,0:T(8,128)S(1)}, f32[272,256]{1,0:T(8,128)}, u32[]{:S(2)}) copy-start(f32[272,256]{1,0:T(8,128)} %constant.5.clone.turn_ref) | copy-start | bytes 835588
  4.0 0.8 copy-start.5
  4.8 21.5 %collective-permute-start = (f32[3,2,128,256]{3,2,1,0:T(8,128)}, f32[3,2,128,256]{3,2,1,0:T(8,128)S(1)}, u32[]{:S(2)}, u32[]{:S(2)}) collective-permute-start(f32[3,2,128,256]{3,2,1,0:T(8,128)} %get-tuple-element.24), channel_id=1, source_target_pairs={{0,2},{1,3},{2,0},{3,1},{4,6},{5,7},{6,4},{7,5},{8,10},{9,11},{10,... | collective-permute-start | bytes 2359304 | tf_op jit(solution)/shard_map/ppermute | solution.py:280
  7.7 23.1 %collective-permute-start.1 = (f32[3,2,128,256]{3,2,1,0:T(8,128)}, f32[3,2,128,256]{3,2,1,0:T(8,128)}, u32[]{:S(2)}, u32[]{:S(2)}) collective-permute-start(f32[3,2,128,256]{3,2,1,0:T(8,128)} %get-tuple-element.25), channel_id=1, source_target_pairs={{0,4},{1,5},{2,6},{3,7},{4,0},{5,1},{6,2},{7,3},{8,12},{9,13},{10,... | collective-permute-start | bytes 2359304 | tf_op jit(solution)/shard_map/ppermute | solution.py:280
  9.3 1.2 %copy-start.1 = (bf16[128,4096]{1,0:T(8,128)(2,1)S(1)}, bf16[128,4096]{1,0:T(8,128)(2,1)}, u32[]{:S(2)}) copy-start(bf16[128,4096]{1,0:T(8,128)(2,1)} %x_ref.3) | copy-start | bytes 3145732
  10.5 0.9 copy-start.8
  11.4 0.8 copy-start.9
  12.3 23.6 %copy-start.2 = (bf16[3648,256]{1,0:T(8,128)(2,1)S(1)}, bf16[3648,256]{1,0:T(8,128)(2,1)}, u32[]{:S(2)}) copy-start(bf16[3648,256]{1,0:T(8,128)(2,1)} %constant.4.clone.table_ref) | copy-start | bytes 5603332
  17.6 18.2 %all-to-all-start = ((f32[16,3,16,128]{3,2,1,0:T(8,128)}), f32[16,3,16,128]{3,2,1,0:T(8,128)S(1)}, u32[]{:S(2)}, u32[]{:S(2)}) async-start(f32[16,3,16,128]{3,2,1,0:T(8,128)} %get-tuple-element.22), calls=%async_computation | async-start | bytes 786432 | tf_op jit(solution)/shard_map/all_to_all | solution.py:323
  26.3 0.9 copy-start.3
  30.8 1.1 copy-start.4
  32.0 1.0 copy-start.6
  34.4 0.7 copy-start.10
  35.1 0.7 copy-start.11
  39.2 21.1 %all-to-all-start.1 = ((f32[16,3,16,128]{3,2,1,0:T(8,128)}), f32[16,3,16,128]{3,2,1,0:T(8,128)S(1)}, u32[]{:S(2)}, u32[]{:S(2)}) async-start(f32[16,3,16,128]{3,2,1,0:T(8,128)} %shard_map.88), calls=%async_computation.1 | async-start | bytes 786432 | tf_op jit(solution)/shard_map/all_to_all | solution.py:333
  45.1 15.1 %collective-permute-start.2 = (f32[1,2,128,256]{3,2,1,0:T(8,128)}, f32[1,2,128,256]{3,2,1,0:T(8,128)S(1)}, u32[]{:S(2)}, u32[]{:S(2)}) collective-permute-start(f32[1,2,128,256]{3,2,1,0:T(8,128)} %copy-done.11), channel_id=1, source_target_pairs={{0,4},{1,5},{2,6},{3,7},{4,0},{5,1},{6,2},{7,3},{8,12},{9,13},{10,... | collective-permute-start | bytes 786440 | tf_op jit(solution)/shard_map/ppermute | solution.py:280
  47.0 13.1 %collective-permute-start.3 = (f32[1,2,128,256]{3,2,1,0:T(8,128)}, f32[1,2,128,256]{3,2,1,0:T(8,128)S(1)}, u32[]{:S(2)}, u32[]{:S(2)}) collective-permute-start(f32[1,2,128,256]{3,2,1,0:T(8,128)} %copy-done.10), channel_id=1, source_target_pairs={{0,2},{1,3},{2,0},{3,1},{4,6},{5,7},{6,4},{7,5},{8,10},{9,11},{10,... | collective-permute-start | bytes 786440 | tf_op jit(solution)/shard_map/ppermute | solution.py:280
  61.2 5.5 %collective-permute-start.4 = (f32[128,256]{1,0:T(8,128)S(1)}, f32[128,256]{1,0:T(8,128)S(1)}, u32[]{:S(2)}, u32[]{:S(2)}) collective-permute-start(f32[128,256]{1,0:T(8,128)S(1)} %get-tuple-element.34.refs_0_), channel_id=1, source_target_pairs={{0,2},{1,3},{2,0},{3,1},{4,6},{5,7},{6,4},{7,5},{8,10},{9,11},{10,... | collective-permute-start | bytes 393224 | tf_op jit(solution)/shard_map/ppermute | solution.py:280
  62.6 6.2 %collective-permute-start.5 = (f32[128,256]{1,0:T(8,128)S(1)}, f32[128,256]{1,0:T(8,128)S(1)}, u32[]{:S(2)}, u32[]{:S(2)}) collective-permute-start(f32[128,256]{1,0:T(8,128)S(1)} %get-tuple-element.34.refs_0_), channel_id=1, source_target_pairs={{0,4},{1,5},{2,6},{3,7},{4,0},{5,1},{6,2},{7,3},{8,12},{9,13},{10,... | collective-permute-start | bytes 393224 | tf_op jit(solution)/shard_map/ppermute | solution.py:280
  63.2 7.0 %collective-permute-start.6 = (f32[128,256]{1,0:T(8,128)S(1)}, f32[128,256]{1,0:T(8,128)S(1)}, u32[]{:S(2)}, u32[]{:S(2)}) collective-permute-start(f32[128,256]{1,0:T(8,128)S(1)} %get-tuple-element.34.refs_0_), channel_id=1, source_target_pairs={{0,6},{1,7},{2,4},{3,5},{4,2},{5,3},{6,0},{7,1},{8,14},{9,15},{10,... | collective-permute-start | bytes 393224 | tf_op jit(solution)/shard_map/ppermute | solution.py:280
  70.5 3.6 %collective-permute-start.7 = (f32[512,256]{1,0:T(8,128)S(1)}, f32[512,256]{1,0:T(8,128)S(1)}, u32[]{:S(2)}, u32[]{:S(2)}) collective-permute-start(f32[512,256]{1,0:T(8,128)S(1)} %shard_map.91), channel_id=1, source_target_pairs={{0,1},{1,0},{2,3},{3,2},{4,5},{5,4},{6,7},{7,6},{8,9},{9,8},{10,11... | collective-permute-start | bytes 1572872 | tf_op jit(solution)/shard_map/ppermute | solution.py:280
  70.6 14.8 %collective-permute-start.10 = (f32[128,512]{1,0:T(8,128)S(1)}, f32[128,512]{1,0:T(8,128)S(1)}, u32[]{:S(2)}, u32[]{:S(2)}) collective-permute-start(f32[128,512]{1,0:T(8,128)S(1)} %get-tuple-element.37.refs_0_), channel_id=1, source_target_pairs={{0,4},{1,5},{2,6},{3,7},{4,0},{5,1},{6,2},{7,3},{8,12},{9,13},{10,... | collective-permute-start | bytes 786440 | tf_op jit(solution)/shard_map/ppermute | solution.py:280
  71.4 20.1 %collective-permute-start.11 = (f32[128,512]{1,0:T(8,128)S(1)}, f32[128,512]{1,0:T(8,128)S(1)}, u32[]{:S(2)}, u32[]{:S(2)}) collective-permute-start(f32[128,512]{1,0:T(8,128)S(1)} %get-tuple-element.37.refs_0_), channel_id=1, source_target_pairs={{0,6},{1,7},{2,4},{3,5},{4,2},{5,3},{6,0},{7,1},{8,14},{9,15},{10,... | collective-permute-start | bytes 786440 | tf_op jit(solution)/shard_map/ppermute | solution.py:280
  73.6 17.9 %collective-permute-start.9 = (f32[128,512]{1,0:T(8,128)S(1)}, f32[128,512]{1,0:T(8,128)S(1)}, u32[]{:S(2)}, u32[]{:S(2)}) collective-permute-start(f32[128,512]{1,0:T(8,128)S(1)} %get-tuple-element.37.refs_0_), channel_id=1, source_target_pairs={{0,2},{1,3},{2,0},{3,1},{4,6},{5,7},{6,4},{7,5},{8,10},{9,11},{10,... | collective-permute-start | bytes 786440 | tf_op jit(solution)/shard_map/ppermute | solution.py:280
  74.4 17.0 %collective-permute-start.8 = (f32[256,256]{1,0:T(8,128)S(1)}, f32[256,256]{1,0:T(8,128)S(1)}, u32[]{:S(2)}, u32[]{:S(2)}) collective-permute-start(f32[256,256]{1,0:T(8,128)S(1)} %get-tuple-element.36), channel_id=1, source_target_pairs={{0,8},{1,9},{2,10},{3,11},{4,12},{5,13},{6,14},{7,15},{8,0},{9,1},... | collective-permute-start | bytes 786440 | tf_op jit(solution)/shard_map/ppermute | solution.py:280
  91.9 2.7 %collective-permute-start.12 = (f32[512,512]{1,0:T(8,128)S(1)}, f32[512,512]{1,0:T(8,128)S(1)}, u32[]{:S(2)}, u32[]{:S(2)}) collective-permute-start(f32[512,512]{1,0:T(8,128)S(1)} %shard_map.93), channel_id=1, source_target_pairs={{0,1},{1,0},{2,3},{3,2},{4,5},{5,4},{6,7},{7,6},{8,9},{9,8},{10,11... | collective-permute-start | bytes 3145736 | tf_op jit(solution)/shard_map/ppermute | solution.py:280
  95.1 26.2 %collective-permute-start.13 = (f32[256,512]{1,0:T(8,128)S(1)}, f32[256,512]{1,0:T(8,128)S(1)}, u32[]{:S(2)}, u32[]{:S(2)}) collective-permute-start(f32[256,512]{1,0:T(8,128)S(1)} %get-tuple-element.39), channel_id=1, source_target_pairs={{0,8},{1,9},{2,10},{3,11},{4,12},{5,13},{6,14},{7,15},{8,0},{9,1},... | collective-permute-start | bytes 1572872 | tf_op jit(solution)/shard_map/ppermute | solution.py:280

commit v6 on v3

--- a/solution.py
+++ b/solution.py
@@ -324,11 +324,11 @@
     table, places = packed(pairs)
     results = pl.pallas_call(
         functools.partial(conv_kernel, places),
-        in_specs=[inside] * 3 + [anywhere] * 2,
+        in_specs=[inside] * 3 + [anywhere] * 3,
         out_shape=shaped(blocks, 3, width, rows),
         scratch_shapes=[pltpu.VMEM((blocks * width, 3 * rows), f32)],
         compiler_params=params,
-    )(signals, jnp.asarray(table), jnp.asarray(turn), *turned)
+    )(signals, jnp.asarray(table), jnp.asarray(turn), *turned, corners[0])
     results = lax.all_to_all(results, "seq", split_axis=0, concat_axis=0, tiled=True)
     turned_corners = pl.pallas_call(
         corner_kernel,

time: 121 us -> 127 us (1.050)
  local copies, waits for them, and re-layouts: 9.61 us -> 12.3 us
  waiting for transfers between devices: 69.7 us -> 71.2 us
  starting transfers between devices: 25.8 us -> 27.1 us
    unnamed x24 -> x28, local copies, waits for them, and re-layouts: 9.61 us -> 12.3 us
    ppermute x14, waiting for transfers between devices: 66.9 us -> 68.2 us  [exchange(): return lax.ppermute(value, 'seq', [(i, i ^ flip) for i in range(blocks)])]
  transfers between devices with their start and end apart: 16 -> 16, of which waited for: 11 -> 12; matrix products, arithmetic and copies ran while one was open for 3% -> 2% of each run, Pallas kernels for 3% -> 3%
where the time goes in v6:
time: 127 us; the launch traced here: 126 us
  waiting for transfers between devices  71.2 us (56%)
  starting transfers between devices  27.1 us (21%)
  local copies, waits for them, and re-layouts  12.3 us (10%)
  Pallas kernels  11.4 us (9%)
  matrix products  3.11 us (2%)
    ppermute x14, waiting for transfers between devices, exchange(): return lax.ppermute(value, 'seq', [(i, i ^ flip) for i in range(blocks)])  68.2 us
    ppermute x14, starting transfers between devices, exchange(): return lax.ppermute(value, 'seq', [(i, i ^ flip) for i in range(blocks)])  18.4 us
    unnamed x28, local copies, waits for them, and re-layouts  12.3 us
    all_to_all x1, starting transfers between devices, per_device(): lax.all_to_all(results, 'seq', split_axis=0, concat_axis=0, tiled=True)  4.71 us
    all_to_all x1, starting transfers between devices, per_device(): lax.all_to_all(signals, 'seq', split_axis=0, concat_axis=0, tiled=True)  3.97 us
    dot_general x1, matrix products, per_device(): lax.dot_general(grad_proj, in_weight, (((1,), (1,)), ((), ())), preferred...  3.11 us
    all_to_all x1, waiting for transfers between devices, per_device(): lax.all_to_all(signals, 'seq', split_axis=0, concat_axis=0, tiled=True)  3.01 us
    pallas_call x1, Pallas kernels, per_device(): pl.pallas_call(functools.partial(project_kernel, scaling), grid=(steps,),...  2.68 us
  transfers between devices with their start and end apart: 16, of which 12 were waited for; matrix products, arithmetic and copies ran while one was open for 2% of the time, Pallas kernels for 3%

profile of v6, /device:TPU:0, one launch (start us, length us, event | category | flops | bytes accessed | tf_op | source)
XLA Modules:
  0.0 125.9 jit_solution(15226553454436424518)
XLA Ops:
  0.6 1.2 copy-done.1
  1.9 1.8 %shard_map.86 = (f32[2,2,128,256]{3,2,1,0:T(8,128)S(1)}, f32[3,2,128,256]{3,2,1,0:T(8,128)}, f32[3,2,128,256]{3,2,1,0:T(8,128)S(1)}) custom-call(bf16[128,4096]{1,0:T(8,128)(2,1)S(1)} %copy-done.1), custom_call_target="tpu_custom_call" | custom-call | tf_op jit(solution)/shard_map/pallas_call | solution.py:283
  3.7 3.0 %collective-permute-start = (f32[3,2,128,256]{3,2,1,0:T(8,128)}, f32[3,2,128,256]{3,2,1,0:T(8,128)S(1)}, u32[]{:S(2)}, u32[]{:S(2)}) collective-permute-start(f32[3,2,128,256]{3,2,1,0:T(8,128)} %get-tuple-element.24), channel_id=1, source_target_pairs={{0,2},{1,3},{2,0},{3,1},{4,6},{5,7},{6,4},{7,5},{8,10},{9,11},{10,... | collective-permute-start | bytes 2359304 | tf_op jit(solution)/shard_map/ppermute | solution.py:279
  6.6 1.6 %collective-permute-start.1 = (f32[3,2,128,256]{3,2,1,0:T(8,128)S(1)}, f32[3,2,128,256]{3,2,1,0:T(8,128)S(1)}, u32[]{:S(2)}, u32[]{:S(2)}) collective-permute-start(f32[3,2,128,256]{3,2,1,0:T(8,128)S(1)} %get-tuple-element.25), channel_id=1, source_target_pairs={{0,4},{1,5},{2,6},{3,7},{4,0},{5,1},{6,2},{7,3},{8,12},{9,13},{10,... | collective-permute-start | bytes 2359304 | tf_op jit(solution)/shard_map/ppermute | solution.py:279
  8.2 2.8 %copy-done = bf16[4096,768]{1,0:T(8,128)(2,1)S(1)} copy-done((bf16[4096,768]{1,0:T(8,128)(2,1)S(1)}, bf16[4096,768]{1,0:T(8,128)(2,1)}, u32[]{:S(2)}) %copy-start) | copy-done | bytes 6291480
  11.0 0.9 copy-done.9
  11.9 0.8 copy-done.10
  12.7 2.7 %shard_map.85 = (f32[16,3,16,128]{3,2,1,0:T(8,128)}, bf16[3,256,128]{2,1,0:T(8,128)(2,1)S(1)}) custom-call(bf16[128,4096]{1,0:T(8,128)(2,1)S(1)} %copy-done.1, bf16[4096,768]{1,0:T(8,128)(2,1)S(1)} %copy-done, f32[128,256]{1,0:T(8,128)S(1)} %copy-done.9, bf16[128,256]{1,0:T(8,128)(2,1)S(1)} %copy-done.10), custom_call_target="tpu_custom_call" | custom-call | flops 805306368 | bytes 7340032 | tf_op jit(solution)/shard_map/pallas_call | solution.py:299
  15.4 0.7 copy-done.7
  16.1 4.0 %all-to-all-start = ((f32[16,3,16,128]{3,2,1,0:T(8,128)}), f32[16,3,16,128]{3,2,1,0:T(8,128)S(1)}, u32[]{:S(2)}, u32[]{:S(2)}) async-start(f32[16,3,16,128]{3,2,1,0:T(8,128)} %get-tuple-element.22), calls=%async_computation | async-start | bytes 786432 | tf_op jit(solution)/shard_map/all_to_all | solution.py:322
  20.1 5.3 %collective-permute-done.y_ref = f32[3,2,128,256]{3,2,1,0:T(8,128)S(1)} collective-permute-done((f32[3,2,128,256]{3,2,1,0:T(8,128)}, f32[3,2,128,256]{3,2,1,0:T(8,128)S(1)}, u32[]{:S(2)}, u32[]{:S(2)}) %collective-permute-start) | collective-permute-done | bytes 786464 | tf_op jit(solution)/shard_map/ppermute | solution.py:279
  25.4 5.4 %collective-permute-done.1.z_ref = f32[3,2,128,256]{3,2,1,0:T(8,128)S(1)} collective-permute-done((f32[3,2,128,256]{3,2,1,0:T(8,128)S(1)}, f32[3,2,128,256]{3,2,1,0:T(8,128)S(1)}, u32[]{:S(2)}, u32[]{:S(2)}) %collective-permute-start.1) | collective-permute-done | bytes 786464 | tf_op jit(solution)/shard_map/ppermute | solution.py:279
  30.8 0.9 shard_map.87
  31.7 0.7 copy-done.11
  32.5 3.0 %all-to-all-done.x_ref = f32[16,3,16,128]{3,2,1,0:T(8,128)S(1)} async-done(((f32[16,3,16,128]{3,2,1,0:T(8,128)}), f32[16,3,16,128]{3,2,1,0:T(8,128)S(1)}, u32[]{:S(2)}, u32[]{:S(2)}) %all-to-all-start) | async-done | bytes 393248 | tf_op jit(solution)/shard_map/all_to_all | solution.py:322
  35.5 3.6 %collective-permute-done.2.refs_2_.corner_own_ref = f32[1,2,128,256]{3,2,1,0:T(8,128)S(1)} collective-permute-done((f32[1,2,128,256]{3,2,1,0:T(8,128)}, f32[1,2,128,256]{3,2,1,0:T(8,128)S(1)}, u32[]{:S(2)}, u32[]{:S(2)}) %collective-permute-start.2) | collective-permute-done | bytes 262176 | tf_op jit(solution)/shard_map/ppermute | solution.py:279
  39.0 1.6 %copy-done.2 = bf16[3648,256]{1,0:T(8,128)(2,1)S(1)} copy-done((bf16[3648,256]{1,0:T(8,128)(2,1)S(1)}, bf16[3648,256]{1,0:T(8,128)(2,1)}, u32[]{:S(2)}) %copy-start.2) | copy-done | bytes 1867800
  40.6 1.0 copy-done.6
  41.6 2.6 %shard_map.88 = f32[16,3,16,128]{3,2,1,0:T(8,128)S(1)} custom-call(f32[16,3,16,128]{3,2,1,0:T(8,128)S(1)} %all-to-all-done.x_ref, bf16[3648,256]{1,0:T(8,128)(2,1)S(1)} %copy-done.2, f32[272,256]{1,0:T(8,128)S(1)} %copy-done.6, bf16[512,384]{1,0:T(8,128)(2,1)S(1)} %get-tuple-element.26.refs_0_.x_ref, bf16[512,384]{1,0:T(8,128)(2,1)S(1)} %get-tuple-element.27.refs_1_.x_ref, ...), custom_call_target="tpu_custom_call" | custom-call | tf_op jit(solution)/shard_map/pallas_call | solution.py:325
  44.2 0.7 copy-done.3
  44.9 4.7 %all-to-all-start.1 = ((f32[16,3,16,128]{3,2,1,0:T(8,128)}), f32[16,3,16,128]{3,2,1,0:T(8,128)S(1)}, u32[]{:S(2)}, u32[]{:S(2)}) async-start(f32[16,3,16,128]{3,2,1,0:T(8,128)} %copy-done.3), calls=%async_computation.1 | async-start | bytes 786432 | tf_op jit(solution)/shard_map/all_to_all | solution.py:332
  49.7 1.9 %collective-permute-start.3 = (f32[1,2,128,256]{3,2,1,0:T(8,128)}, f32[1,2,128,256]{3,2,1,0:T(8,128)S(1)}, u32[]{:S(2)}, u32[]{:S(2)}) collective-permute-start(f32[1,2,128,256]{3,2,1,0:T(8,128)} %copy-done.11), channel_id=1, source_target_pairs={{0,2},{1,3},{2,0},{3,1},{4,6},{5,7},{6,4},{7,5},{8,10},{9,11},{10,... | collective-permute-start | bytes 786440 | tf_op jit(solution)/shard_map/ppermute | solution.py:279
  51.6 11.0 %collective-permute-done.3.corner_other_ref = f32[1,2,128,256]{3,2,1,0:T(8,128)S(1)} collective-permute-done((f32[1,2,128,256]{3,2,1,0:T(8,128)}, f32[1,2,128,256]{3,2,1,0:T(8,128)S(1)}, u32[]{:S(2)}, u32[]{:S(2)}) %collective-permute-start.3) | collective-permute-done | bytes 262176 | tf_op jit(solution)/shard_map/ppermute | solution.py:279
  62.6 0.9 copy-done.5
  63.6 0.1 shard_map.89
  63.7 0.9 copy-done.8
  64.6 0.8 shard_map.90
  65.5 0.7 collective-permute-start.4
  66.1 1.4 %collective-permute-start.5 = (f32[128,256]{1,0:T(8,128)S(1)}, f32[128,256]{1,0:T(8,128)S(1)}, u32[]{:S(2)}, u32[]{:S(2)}) collective-permute-start(f32[128,256]{1,0:T(8,128)S(1)} %get-tuple-element.34.refs_0_), channel_id=1, source_target_pairs={{0,4},{1,5},{2,6},{3,7},{4,0},{5,1},{6,2},{7,3},{8,12},{9,13},{10,... | collective-permute-start | bytes 393224 | tf_op jit(solution)/shard_map/ppermute | solution.py:279
  67.5 1.5 %collective-permute-start.6 = (f32[128,256]{1,0:T(8,128)S(1)}, f32[128,256]{1,0:T(8,128)S(1)}, u32[]{:S(2)}, u32[]{:S(2)}) collective-permute-start(f32[128,256]{1,0:T(8,128)S(1)} %get-tuple-element.34.refs_0_), channel_id=1, source_target_pairs={{0,6},{1,7},{2,4},{3,5},{4,2},{5,3},{6,0},{7,1},{8,14},{9,15},{10,... | collective-permute-start | bytes 393224 | tf_op jit(solution)/shard_map/ppermute | solution.py:279
  69.0 2.0 %collective-permute-done.4.refs_1_ = f32[128,256]{1,0:T(8,128)S(1)} collective-permute-done((f32[128,256]{1,0:T(8,128)S(1)}, f32[128,256]{1,0:T(8,128)S(1)}, u32[]{:S(2)}, u32[]{:S(2)}) %collective-permute-start.4) | collective-permute-done | bytes 131104 | tf_op jit(solution)/shard_map/ppermute | solution.py:279
  71.0 1.2 collective-permute-done.5.refs_2_
  72.2 2.3 %collective-permute-done.6.refs_3_ = f32[128,256]{1,0:T(8,128)S(1)} collective-permute-done((f32[128,256]{1,0:T(8,128)S(1)}, f32[128,256]{1,0:T(8,128)S(1)}, u32[]{:S(2)}, u32[]{:S(2)}) %collective-permute-start.6) | collective-permute-done | bytes 131104 | tf_op jit(solution)/shard_map/ppermute | solution.py:279
  74.5 0.3 shard_map.91
  74.9 1.5 %collective-permute-start.10 = (f32[128,512]{1,0:T(8,128)S(1)}, f32[128,512]{1,0:T(8,128)S(1)}, u32[]{:S(2)}, u32[]{:S(2)}) collective-permute-start(f32[128,512]{1,0:T(8,128)S(1)} %get-tuple-element.37.refs_0_), channel_id=1, source_target_pairs={{0,4},{1,5},{2,6},{3,7},{4,0},{5,1},{6,2},{7,3},{8,12},{9,13},{10,... | collective-permute-start | bytes 786440 | tf_op jit(solution)/shard_map/ppermute | solution.py:279
  76.4 0.9 collective-permute-start.11
  77.3 1.1 collective-permute-start.9
  78.4 0.3 shard_map.92
  78.8 2.6 %collective-permute-start.8 = (f32[256,256]{1,0:T(8,128)S(1)}, f32[256,256]{1,0:T(8,128)S(1)}, u32[]{:S(2)}, u32[]{:S(2)}) collective-permute-start(f32[256,256]{1,0:T(8,128)S(1)} %get-tuple-element.36), channel_id=1, source_target_pairs={{0,8},{1,9},{2,10},{3,11},{4,12},{5,13},{6,14},{7,15},{8,0},{9,1},... | collective-permute-start | bytes 786440 | tf_op jit(solution)/shard_map/ppermute | solution.py:279
  81.3 8.3 %collective-permute-done.10.refs_2_ = f32[128,512]{1,0:T(8,128)S(1)} collective-permute-done((f32[128,512]{1,0:T(8,128)S(1)}, f32[128,512]{1,0:T(8,128)S(1)}, u32[]{:S(2)}, u32[]{:S(2)}) %collective-permute-start.10) | collective-permute-done | bytes 262176 | tf_op jit(solution)/shard_map/ppermute | solution.py:279
  89.7 5.5 %collective-permute-done.11.refs_3_ = f32[128,512]{1,0:T(8,128)S(1)} collective-permute-done((f32[128,512]{1,0:T(8,128)S(1)}, f32[128,512]{1,0:T(8,128)S(1)}, u32[]{:S(2)}, u32[]{:S(2)}) %collective-permute-start.11) | collective-permute-done | bytes 262176 | tf_op jit(solution)/shard_map/ppermute | solution.py:279
  95.2 0.4 shard_map.93
  95.7 2.6 %collective-permute-done.12.refs_4_ = f32[512,512]{1,0:T(8,128)S(1)} collective-permute-done((f32[512,512]{1,0:T(8,128)S(1)}, f32[512,512]{1,0:T(8,128)S(1)}, u32[]{:S(2)}, u32[]{:S(2)}) %collective-permute-start.12) | collective-permute-done | bytes 1048608 | tf_op jit(solution)/shard_map/ppermute | solution.py:279
  98.3 0.4 shard_map.94
  98.8 2.1 %collective-permute-start.13 = (f32[256,512]{1,0:T(8,128)S(1)}, f32[256,512]{1,0:T(8,128)S(1)}, u32[]{:S(2)}, u32[]{:S(2)}) collective-permute-start(f32[256,512]{1,0:T(8,128)S(1)} %get-tuple-element.39), channel_id=1, source_target_pairs={{0,8},{1,9},{2,10},{3,11},{4,12},{5,13},{6,14},{7,15},{8,0},{9,1},... | collective-permute-start | bytes 1572872 | tf_op jit(solution)/shard_map/ppermute | solution.py:279
  100.9 3.1 %convolution_convert_fusion = bf16[128,4096]{1,0:T(8,128)(2,1)} fusion(bf16[128,768]{1,0:T(8,128)(2,1)S(1)} %get-tuple-element.33, bf16[4096,768]{1,0:T(8,128)(2,1)S(1)} %bitcast.3), kind=kOutput, calls=%fused_computation | convolution fusion | flops 805830656 | bytes 7536640 | tf_op jit(solution)/shard_map/dot_general | solution.py:353
  104.1 20.9 %collective-permute-done.13.refs_3_ = f32[256,512]{1,0:T(8,128)S(1)} collective-permute-done((f32[256,512]{1,0:T(8,128)S(1)}, f32[256,512]{1,0:T(8,128)S(1)}, u32[]{:S(2)}, u32[]{:S(2)}) %collective-permute-start.13) | collective-permute-done | bytes 524320 | tf_op jit(solution)/shard_map/ppermute | solution.py:279
  125.0 1.0 shard_map.95
  (25 shorter events, 0.2 us)
Async XLA Ops:
  0.6 1.2 copy-start.1
  3.7 21.7 %collective-permute-start = (f32[3,2,128,256]{3,2,1,0:T(8,128)}, f32[3,2,128,256]{3,2,1,0:T(8,128)S(1)}, u32[]{:S(2)}, u32[]{:S(2)}) collective-permute-start(f32[3,2,128,256]{3,2,1,0:T(8,128)} %get-tuple-element.24), channel_id=1, source_target_pairs={{0,2},{1,3},{2,0},{3,1},{4,6},{5,7},{6,4},{7,5},{8,10},{9,11},{10,... | collective-permute-start | bytes 2359304 | tf_op jit(solution)/shard_map/ppermute | solution.py:279
  6.6 24.2 %collective-permute-start.1 = (f32[3,2,128,256]{3,2,1,0:T(8,128)S(1)}, f32[3,2,128,256]{3,2,1,0:T(8,128)S(1)}, u32[]{:S(2)}, u32[]{:S(2)}) collective-permute-start(f32[3,2,128,256]{3,2,1,0:T(8,128)S(1)} %get-tuple-element.25), channel_id=1, source_target_pairs={{0,4},{1,5},{2,6},{3,7},{4,0},{5,1},{6,2},{7,3},{8,12},{9,13},{10,... | collective-permute-start | bytes 2359304 | tf_op jit(solution)/shard_map/ppermute | solution.py:279
  8.2 2.8 %copy-start = (bf16[4096,768]{1,0:T(8,128)(2,1)S(1)}, bf16[4096,768]{1,0:T(8,128)(2,1)}, u32[]{:S(2)}) copy-start(bf16[4096,768]{1,0:T(8,128)(2,1)} %w_ref.1) | copy-start | bytes 18874372
  11.0 0.9 copy-start.9
  11.9 0.8 copy-start.10
  15.4 0.7 copy-start.7
  16.1 19.4 %all-to-all-start = ((f32[16,3,16,128]{3,2,1,0:T(8,128)}), f32[16,3,16,128]{3,2,1,0:T(8,128)S(1)}, u32[]{:S(2)}, u32[]{:S(2)}) async-start(f32[16,3,16,128]{3,2,1,0:T(8,128)} %get-tuple-element.22), calls=%async_computation | async-start | bytes 786432 | tf_op jit(solution)/shard_map/all_to_all | solution.py:322
  31.7 0.7 copy-start.11
  32.5 6.6 %collective-permute-start.2 = (f32[1,2,128,256]{3,2,1,0:T(8,128)}, f32[1,2,128,256]{3,2,1,0:T(8,128)S(1)}, u32[]{:S(2)}, u32[]{:S(2)}) collective-permute-start(f32[1,2,128,256]{3,2,1,0:T(8,128)} %get-tuple-element.28), channel_id=1, source_target_pairs={{0,4},{1,5},{2,6},{3,7},{4,0},{5,1},{6,2},{7,3},{8,12},{9,13},{10,... | collective-permute-start | bytes 786440 | tf_op jit(solution)/shard_map/ppermute | solution.py:279
  39.0 12.5 %copy-start.4 = (f32[1,2,128,256]{3,2,1,0:T(8,128)}, f32[1,2,128,256]{3,2,1,0:T(8,128)S(1)}, u32[]{:S(2)}) copy-start(f32[1,2,128,256]{3,2,1,0:T(8,128)S(1)} %collective-permute-done.2.refs_2_.corner_own_ref) | copy-start | bytes 786436
  39.0 1.6 %copy-start.2 = (bf16[3648,256]{1,0:T(8,128)(2,1)S(1)}, bf16[3648,256]{1,0:T(8,128)(2,1)}, u32[]{:S(2)}) copy-start(bf16[3648,256]{1,0:T(8,128)(2,1)} %constant.4.clone.table_ref) | copy-start | bytes 5603332
  40.6 1.0 copy-start.6
  41.6 59.3 %slice-start = ((s8[6291456]{0:T(1024)(128)(4,1)}), s8[2097152]{0:T(1024)(128)(4,1)S(1)}, s32[]{:S(2)}) async-start(s8[6291456]{0:T(1024)(128)(4,1)} %bitcast.2), calls=%async_computation.2 | async-start | bytes 4194304
  44.2 0.7 copy-start.3
  44.9 18.8 %all-to-all-start.1 = ((f32[16,3,16,128]{3,2,1,0:T(8,128)}), f32[16,3,16,128]{3,2,1,0:T(8,128)S(1)}, u32[]{:S(2)}, u32[]{:S(2)}) async-start(f32[16,3,16,128]{3,2,1,0:T(8,128)} %copy-done.3), calls=%async_computation.1 | async-start | bytes 786432 | tf_op jit(solution)/shard_map/all_to_all | solution.py:332
  49.7 13.0 %collective-permute-start.3 = (f32[1,2,128,256]{3,2,1,0:T(8,128)}, f32[1,2,128,256]{3,2,1,0:T(8,128)S(1)}, u32[]{:S(2)}, u32[]{:S(2)}) collective-permute-start(f32[1,2,128,256]{3,2,1,0:T(8,128)} %copy-done.11), channel_id=1, source_target_pairs={{0,2},{1,3},{2,0},{3,1},{4,6},{5,7},{6,4},{7,5},{8,10},{9,11},{10,... | collective-permute-start | bytes 786440 | tf_op jit(solution)/shard_map/ppermute | solution.py:279
  62.6 1.0 copy-start.5
  63.7 0.9 copy-start.8
  65.5 35.5 %slice-start.1 = ((s8[6291456]{0:T(1024)(128)(4,1)}), s8[4194304]{0:T(1024)(128)(4,1)S(1)}, s32[]{:S(2)}) async-start(s8[6291456]{0:T(1024)(128)(4,1)} %bitcast.2), calls=%async_computation.3 | async-start | bytes 8388608
  65.5 5.5 %collective-permute-start.4 = (f32[128,256]{1,0:T(8,128)S(1)}, f32[128,256]{1,0:T(8,128)S(1)}, u32[]{:S(2)}, u32[]{:S(2)}) collective-permute-start(f32[128,256]{1,0:T(8,128)S(1)} %get-tuple-element.34.refs_0_), channel_id=1, source_target_pairs={{0,2},{1,3},{2,0},{3,1},{4,6},{5,7},{6,4},{7,5},{8,10},{9,11},{10,... | collective-permute-start | bytes 393224 | tf_op jit(solution)/shard_map/ppermute | solution.py:279
  66.1 6.1 %collective-permute-start.5 = (f32[128,256]{1,0:T(8,128)S(1)}, f32[128,256]{1,0:T(8,128)S(1)}, u32[]{:S(2)}, u32[]{:S(2)}) collective-permute-start(f32[128,256]{1,0:T(8,128)S(1)} %get-tuple-element.34.refs_0_), channel_id=1, source_target_pairs={{0,4},{1,5},{2,6},{3,7},{4,0},{5,1},{6,2},{7,3},{8,12},{9,13},{10,... | collective-permute-start | bytes 393224 | tf_op jit(solution)/shard_map/ppermute | solution.py:279
  67.5 7.0 %collective-permute-start.6 = (f32[128,256]{1,0:T(8,128)S(1)}, f32[128,256]{1,0:T(8,128)S(1)}, u32[]{:S(2)}, u32[]{:S(2)}) collective-permute-start(f32[128,256]{1,0:T(8,128)S(1)} %get-tuple-element.34.refs_0_), channel_id=1, source_target_pairs={{0,6},{1,7},{2,4},{3,5},{4,2},{5,3},{6,0},{7,1},{8,14},{9,15},{10,... | collective-permute-start | bytes 393224 | tf_op jit(solution)/shard_map/ppermute | solution.py:279
  74.8 3.6 %collective-permute-start.7 = (f32[512,256]{1,0:T(8,128)S(1)}, f32[512,256]{1,0:T(8,128)S(1)}, u32[]{:S(2)}, u32[]{:S(2)}) collective-permute-start(f32[512,256]{1,0:T(8,128)S(1)} %shard_map.91), channel_id=1, source_target_pairs={{0,1},{1,0},{2,3},{3,2},{4,5},{5,4},{6,7},{7,6},{8,9},{9,8},{10,11... | collective-permute-start | bytes 1572872 | tf_op jit(solution)/shard_map/ppermute | solution.py:279
  74.9 14.8 %collective-permute-start.10 = (f32[128,512]{1,0:T(8,128)S(1)}, f32[128,512]{1,0:T(8,128)S(1)}, u32[]{:S(2)}, u32[]{:S(2)}) collective-permute-start(f32[128,512]{1,0:T(8,128)S(1)} %get-tuple-element.37.refs_0_), channel_id=1, source_target_pairs={{0,4},{1,5},{2,6},{3,7},{4,0},{5,1},{6,2},{7,3},{8,12},{9,13},{10,... | collective-permute-start | bytes 786440 | tf_op jit(solution)/shard_map/ppermute | solution.py:279
  76.4 18.7 %collective-permute-start.11 = (f32[128,512]{1,0:T(8,128)S(1)}, f32[128,512]{1,0:T(8,128)S(1)}, u32[]{:S(2)}, u32[]{:S(2)}) collective-permute-start(f32[128,512]{1,0:T(8,128)S(1)} %get-tuple-element.37.refs_0_), channel_id=1, source_target_pairs={{0,6},{1,7},{2,4},{3,5},{4,2},{5,3},{6,0},{7,1},{8,14},{9,15},{10,... | collective-permute-start | bytes 786440 | tf_op jit(solution)/shard_map/ppermute | solution.py:279
  77.3 17.9 %collective-permute-start.9 = (f32[128,512]{1,0:T(8,128)S(1)}, f32[128,512]{1,0:T(8,128)S(1)}, u32[]{:S(2)}, u32[]{:S(2)}) collective-permute-start(f32[128,512]{1,0:T(8,128)S(1)} %get-tuple-element.37.refs_0_), channel_id=1, source_target_pairs={{0,2},{1,3},{2,0},{3,1},{4,6},{5,7},{6,4},{7,5},{8,10},{9,11},{10,... | collective-permute-start | bytes 786440 | tf_op jit(solution)/shard_map/ppermute | solution.py:279
  78.8 16.4 %collective-permute-start.8 = (f32[256,256]{1,0:T(8,128)S(1)}, f32[256,256]{1,0:T(8,128)S(1)}, u32[]{:S(2)}, u32[]{:S(2)}) collective-permute-start(f32[256,256]{1,0:T(8,128)S(1)} %get-tuple-element.36), channel_id=1, source_target_pairs={{0,8},{1,9},{2,10},{3,11},{4,12},{5,13},{6,14},{7,15},{8,0},{9,1},... | collective-permute-start | bytes 786440 | tf_op jit(solution)/shard_map/ppermute | solution.py:279
  95.6 2.7 %collective-permute-start.12 = (f32[512,512]{1,0:T(8,128)S(1)}, f32[512,512]{1,0:T(8,128)S(1)}, u32[]{:S(2)}, u32[]{:S(2)}) collective-permute-start(f32[512,512]{1,0:T(8,128)S(1)} %shard_map.93), channel_id=1, source_target_pairs={{0,1},{1,0},{2,3},{3,2},{4,5},{5,4},{6,7},{7,6},{8,9},{9,8},{10,11... | collective-permute-start | bytes 3145736 | tf_op jit(solution)/shard_map/ppermute | solution.py:279
  98.8 26.2 %collective-permute-start.13 = (f32[256,512]{1,0:T(8,128)S(1)}, f32[256,512]{1,0:T(8,128)S(1)}, u32[]{:S(2)}, u32[]{:S(2)}) collective-permute-start(f32[256,512]{1,0:T(8,128)S(1)} %get-tuple-element.39), channel_id=1, source_target_pairs={{0,8},{1,9},{2,10},{3,11},{4,12},{5,13},{6,14},{7,15},{8,0},{9,1},... | collective-permute-start | bytes 1572872 | tf_op jit(solution)/shard_map/ppermute | solution.py:279
